TPU v7x, 32 devices: a whole 2x2x4 slice. The times are simulated.
32 devices in a mesh: dom: 16 (over z, y, x), grp: 2 (over core).
Axes of the slice: x: 2, y: 2, z: 4, core: 2. Of those that a mesh axis runs over, the one named last changes fastest.
Arguments:
- features: bfloat16 [256, 768], P(('dom', 'grp')), may hold values from -6 to 6
- w_first: bfloat16 [768, 512], replicated, may hold values from -0.21875 to 0.21875
- w_second: bfloat16 [512, 512], replicated, may hold values from -0.25 to 0.25
- relation_table: bfloat16 [1387, 512], replicated, may hold values from -1.5 to 1.5
- heads: int32 [2, 4096], P(None, ('dom', 'grp')), may hold values from 0 to 15
- relations: int32 [2, 4096], P(None, ('dom', 'grp')), may hold values from 0 to 1386
- tails: int32 [2, 4096], P(None, ('dom', 'grp')), may hold values from 0 to 15
- negatives: int32 [2, 512], replicated, may hold values from 0 to 15
- partner: int32 [2, 16], replicated, may hold values from 0 to 15, as said below
Outputs:
- edge_loss: float32 [2, 4096], P(None, ('dom', 'grp'))
- grad_w1: float32 [768, 512], P('grp')
- grad_w2: float32 [512, 512], P('grp')
Inputs may be any that keep to these rules, and one draw needn't show every extreme that they name: partner[r, p] = p XOR m_r with one mask m_r of 1 to 15 for each round r, so partitions meet in pairs.
All inputs are finite; a program needn't handle non-finite values.
Results may differ from a plain program's by a relative error of at most 0.0095.
Values may be sent and summed in bfloat16 or wider, within the bound.
No kernel may reach another device: no remote copies, remote signals or barrier semaphores. Data moves between devices by JAX's collectives and lax.ppermute only.
A program may use at most 64 MiB of HBM per device.

v0:
```python
import math

import jax
import jax.numpy as jnp
from jax import lax
from jax.sharding import PartitionSpec as P


def partner_2(value, axis, distance):
    return lax.ppermute(value, axis, [(i, i ^ 1 << distance) for i in range(lax.axis_size(axis))])


def encode(rows, w_first, w_second):
    pre_act = jnp.dot(rows, w_first, preferred_element_type=jnp.float32)
    hidden = jax.nn.silu(pre_act).astype(jnp.bfloat16)
    encoded = jnp.dot(hidden, w_second, preferred_element_type=jnp.float32).astype(jnp.bfloat16)
    return (pre_act, hidden, encoded)


def backward(rows, pre_act, hidden, grad_rows, w_second):
    term_second = lax.dot_general(
        hidden, grad_rows, (((0,), (0,)), ((), ())), preferred_element_type=jnp.float32
    )
    grad_hidden = lax.dot_general(
        grad_rows, w_second, (((1,), (1,)), ((), ())), preferred_element_type=jnp.float32
    )
    sigmoid_pre = jax.nn.sigmoid(pre_act)
    silu_slope = sigmoid_pre * (1.0 + pre_act * (1.0 - sigmoid_pre))
    grad_pre = (grad_hidden * silu_slope).astype(jnp.bfloat16)
    term_first = lax.dot_general(
        rows, grad_pre, (((0,), (0,)), ((), ())), preferred_element_type=jnp.float32
    )
    return (term_first, term_second)


def row_select(ids, row_count):
    return ids[:, None] == jnp.arange(row_count, dtype=jnp.int32)[None, :]


def pick_rows(selector, table):
    return jnp.dot(selector.astype(jnp.bfloat16), table, preferred_element_type=jnp.float32)


def add_into_rows(selector, values):
    return lax.dot_general(
        selector.astype(jnp.float32),
        values,
        (((0,), (0,)), ((), ())),
        precision=lax.Precision.HIGHEST,
        preferred_element_type=jnp.float32,
    )


def score_block(own, other, relation_table, head_ids, relation_ids, tail_ids, negative_ids):
    half_width = own.shape[1] // 2
    row_count = own.shape[0]
    head_select = row_select(head_ids, row_count)
    tail_select = row_select(tail_ids, row_count)
    negative_select = row_select(negative_ids, row_count)
    head_rows = pick_rows(head_select, own)
    rel_rows = jnp.take(relation_table, relation_ids, axis=0).astype(jnp.float32)
    tail_rows = pick_rows(tail_select, other)
    negative_rows = pick_rows(negative_select, other).astype(jnp.bfloat16)
    head_real, head_imag = (head_rows[:, :half_width], head_rows[:, half_width:])
    rel_real, rel_imag = (rel_rows[:, :half_width], rel_rows[:, half_width:])
    query = jnp.concatenate(
        [head_real * rel_real - head_imag * rel_imag, head_real * rel_imag + head_imag * rel_real],
        axis=1,
    ).astype(jnp.bfloat16)
    query_wide = query.astype(jnp.float32)
    positive = jnp.sum(query_wide * tail_rows, axis=1)
    negative = lax.dot_general(
        query, negative_rows, (((1,), (1,)), ((), ())), preferred_element_type=jnp.float32
    )
    edge_loss = (
        jax.nn.softplus(-positive) + jnp.sum(jax.nn.softplus(negative), axis=1) / negative.shape[1]
    )
    weight_neg = (jax.nn.sigmoid(negative) / negative.shape[1]).astype(jnp.bfloat16)
    weight_pos = -jax.nn.sigmoid(-positive)
    grad_query = weight_pos[:, None] * tail_rows + jnp.dot(
        weight_neg, negative_rows, preferred_element_type=jnp.float32
    )
    grad_tail = weight_pos[:, None] * query_wide
    grad_negative = lax.dot_general(
        weight_neg, query, (((0,), (0,)), ((), ())), preferred_element_type=jnp.float32
    )
    grad_real, grad_imag = (grad_query[:, :half_width], grad_query[:, half_width:])
    grad_head = jnp.concatenate(
        [grad_real * rel_real + grad_imag * rel_imag, grad_imag * rel_real - grad_real * rel_imag],
        axis=1,
    )
    own_part = add_into_rows(head_select, grad_head)
    far_part = add_into_rows(tail_select, grad_tail) + add_into_rows(negative_select, grad_negative)
    return (edge_loss, own_part, far_part)


def route_rows(payload, xor_mask, bit_count, mover):
    for bit_level in range(bit_count):
        swapped = mover(payload, bit_level)
        payload = jnp.where(xor_mask >> bit_level & 1 == 1, swapped, payload)
    return payload


def per_device(
    features, w_first, w_second, relation_table, heads, relations, tails, negatives, partner
):
    pre_act, hidden, encoded = encode(features, w_first, w_second)
    own_block = lax.all_gather(encoded, "grp", axis=0, tiled=True)
    bit_count = lax.axis_size("dom").bit_length() - 1
    total_first = jnp.zeros(w_first.shape, jnp.float32)
    total_second = jnp.zeros(w_second.shape, jnp.float32)
    own_acc = jnp.zeros(own_block.shape, jnp.float32)
    losses = []
    for bucket in range(heads.shape[0]):
        xor_mask = partner[bucket, 0]
        arrived = route_rows(
            encoded,
            xor_mask,
            bit_count,
            lambda payload, bit_level: partner_2(payload, "dom", bit_level),
        )
        far_block = lax.all_gather(arrived, "grp", axis=0, tiled=True)
        edge_loss, own_part, far_part = score_block(
            own_block,
            far_block,
            relation_table,
            heads[bucket],
            relations[bucket],
            tails[bucket],
            negatives[bucket],
        )
        losses.append(edge_loss)
        own_acc = own_acc + own_part
        far_grad = lax.psum_scatter(
            far_part.astype(jnp.bfloat16), "grp", scatter_dimension=0, tiled=True
        )
        returned = route_rows(
            far_grad,
            xor_mask,
            bit_count,
            lambda payload, bit_level: partner_2(payload, "dom", bit_level),
        )
        term_first, term_second = backward(features, pre_act, hidden, returned, w_second)
        total_first = total_first + term_first
        total_second = total_second + term_second
    own_grad = lax.psum_scatter(
        own_acc.astype(jnp.bfloat16), "grp", scatter_dimension=0, tiled=True
    )
    term_first, term_second = backward(features, pre_act, hidden, own_grad, w_second)
    total_first = total_first + term_first
    total_second = total_second + term_second
    part_first, part_second = (
        lax.psum_scatter(
            total_first.astype(jnp.bfloat16), "grp", scatter_dimension=0, tiled=True
        ).astype(jnp.float32),
        lax.psum_scatter(
            total_second.astype(jnp.bfloat16), "grp", scatter_dimension=0, tiled=True
        ).astype(jnp.float32),
    )
    summed_first, summed_second = lax.psum((part_first, part_second), "dom")
    local_squares = jnp.sum(summed_first * summed_first) + jnp.sum(summed_second * summed_second)
    squares = lax.psum(local_squares, "grp")
    factor = jnp.minimum(1.0, math.sqrt(w_first.size + w_second.size) / jnp.sqrt(squares + 1e-06))
    return (jnp.stack(losses), summed_first * factor, summed_second * factor)


def solution(mesh):
    return jax.shard_map(
        per_device,
        mesh=mesh,
        in_specs=(
            P(("dom", "grp"), None),
            P(),
            P(),
            P(),
            P(None, ("dom", "grp")),
            P(None, ("dom", "grp")),
            P(None, ("dom", "grp")),
            P(),
            P(),
        ),
        out_specs=(P(None, ("dom", "grp")), P("grp", None), P("grp", None)),
        check_vma=False,
    )
```

profile of v0, /device:TPU:0, one launch (start us, length us, event | category | flops | bytes accessed | tf_op | source)
XLA Modules:
  0.0 221.8 jit_solution(2456559309631603908)
XLA Ops:
  7.2 1.5 multiply_convert_fusion.2
  8.7 1.2 convolution_convert_fusion.2
  9.9 2.9 %collective-permute-start = (bf16[8,512]{1,0:T(8,128)(2,1)S(1)}, bf16[8,512]{1,0:T(8,128)(2,1)S(1)}, u32[]{:S(2)}, u32[]{:S(2)}) collective-permute-start(bf16[8,512]{1,0:T(8,128)(2,1)S(1)} %convolution_convert_fusion.2), channel_id=1, source_target_pairs={{0,2},{2,0},{4,6},{6,4},{8,10},{10,8},{12,14},{14,12},{16,18},{18,... | collective-permute-start | bytes 24584 | tf_op jit(solution)/shard_map/ppermute | solution.py:10
  12.9 1.8 all_gather.9
  14.7 0.8 slice_bitcast_fusion.3
  15.4 0.8 compare_and_fusion.1
  16.2 0.8 fusion.61
  17.0 0.8 gather_fusion.1
  17.8 0.8 gather_fusion
  19.5 0.5 fusion.62
  21.3 1.6 collective-permute-start.1
  26.8 0.6 collective-permute-start.4
  27.4 1.6 collective-permute-start.2
  29.0 1.5 collective-permute-done.4
  30.5 1.6 collective-permute-start.5
  32.1 2.6 %collective-permute-start.3 = (bf16[8,512]{1,0:T(8,128)(2,1)S(1)}, bf16[8,512]{1,0:T(8,128)(2,1)S(1)}, u32[]{:S(2)}, u32[]{:S(2)}) collective-permute-start(bf16[8,512]{1,0:T(8,128)(2,1)S(1)} %broadcast_select_fusion.13), channel_id=1, source_target_pairs={{0,16},{2,18},{4,20},{6,22},{8,24},{10,26},{12,28},{14,30},{16,0},... | collective-permute-start | bytes 24584 | tf_op jit(solution)/shard_map/ppermute | solution.py:10
  34.7 2.0 collective-permute-start.6
  36.8 1.8 all_gather.10
  38.6 0.8 collective-permute-done.6
  39.4 1.8 all_gather.11
  41.2 0.3 fusion.11
  41.8 0.3 fusion.13
  42.1 0.3 fusion.14
  42.7 0.3 convolution_convert_fusion
  43.0 1.1 fusion.16
  44.1 0.3 fusion.55
  44.8 0.3 convolution_convert_fusion.1
  45.1 1.1 fusion.15
  46.2 0.3 fusion.57
  46.8 1.1 fusion.3
  48.0 1.1 fusion.4
  49.6 0.9 fusion.5
  50.5 3.8 %reduce-scatter.8.cloned.1.call-done = bf16[8,512]{1,0:T(8,128)(2,1)} async-done(((bf16[16,512]{1,0:T(8,128)(2,1)}), bf16[8,512]{1,0:T(8,128)(2,1)}) %reduce-scatter.8.cloned.1.call-update) | async-done | bytes 8208 | tf_op jit(solution)/shard_map/reduce_scatter | solution.py:134
  54.3 1.7 collective-permute-start.7
  56.0 9.7 %reduce-scatter.10.cloned.1.call-done = bf16[8,512]{1,0:T(8,128)(2,1)} async-done(((bf16[16,512]{1,0:T(8,128)(2,1)}), bf16[8,512]{1,0:T(8,128)(2,1)}) %reduce-scatter.10.cloned.1.call-update) | async-done | bytes 8208 | tf_op jit(solution)/shard_map/reduce_scatter | solution.py:134
  65.6 1.7 collective-permute-start.11
  67.3 9.1 %reduce-scatter.12.cloned.1.call-done = bf16[8,512]{1,0:T(8,128)(2,1)} async-done(((bf16[16,512]{1,0:T(8,128)(2,1)}), bf16[8,512]{1,0:T(8,128)(2,1)}) %reduce-scatter.12.cloned.1.call-update) | async-done | bytes 8208 | tf_op jit(solution)/shard_map/reduce_scatter | solution.py:146
  76.4 1.0 fusion.63
  77.5 0.7 broadcast_select_fusion
  78.2 1.7 collective-permute-start.12
  79.9 0.4 collective-permute-start.8
  80.3 1.5 collective-permute-done.12
  81.9 1.7 collective-permute-start.13
  83.6 1.5 collective-permute-start.9
  85.1 0.4 collective-permute-done.13
  85.5 2.6 %collective-permute-start.14 = (bf16[8,512]{1,0:T(8,128)(2,1)S(1)}, bf16[8,512]{1,0:T(8,128)(2,1)S(1)}, u32[]{:S(2)}, u32[]{:S(2)}) collective-permute-start(bf16[8,512]{1,0:T(8,128)(2,1)S(1)} %broadcast_select_fusion.4), channel_id=1, source_target_pairs={{0,16},{2,18},{4,20},{6,22},{8,24},{10,26},{12,28},{14,30},{16,0},... | collective-permute-start | bytes 24584 | tf_op jit(solution)/shard_map/ppermute | solution.py:10
  88.2 1.6 collective-permute-start.10
  89.7 0.3 collective-permute-done.14
  90.1 0.3 fusion.42
  90.4 2.4 %collective-permute-done.10 = bf16[8,512]{1,0:T(8,128)(2,1)S(1)} collective-permute-done((bf16[8,512]{1,0:T(8,128)(2,1)S(1)}, bf16[8,512]{1,0:T(8,128)(2,1)S(1)}, u32[]{:S(2)}, u32[]{:S(2)}) %collective-permute-start.10) | collective-permute-done | bytes 8224 | tf_op jit(solution)/shard_map/ppermute | solution.py:10
  92.8 1.1 fusion.2
  94.0 1.5 fusion.10
  95.5 2.7 %fusion.9 = f32[512,768]{1,0:T(8,128)} fusion(bf16[8,768]{1,0:T(8,128)(2,1)} %param.11, bf16[512,512]{1,0:T(8,128)(2,1)S(1)} %copy-done.1, bf16[8,512]{1,0:T(8,128)(2,1)} %copy-done.4, bf16[8,512]{1,0:T(8,128)(2,1)S(1)} %broadcast_select_fusion.4, pred[]{:T(512)} %bitcast.13, f32[8,512]{1,0:T(8,128)S(1)} %get-tuple-element.37), kind=kOutput, calls=%fused_computation.22 | convolution fusion | flops 10526720 | bytes 2142209 | tf_op jit(solution)/shard_map/dot_general | solution.py:30
  98.2 3.2 %fusion.1 = bf16[768,512]{0,1:T(8,128)(2,1)} fusion(bf16[8,768]{1,0:T(8,128)(2,1)} %param.11, f32[512,768]{1,0:T(8,128)S(1)} %fusion.10, f32[512,768]{1,0:T(8,128)} %fusion.9, bf16[8,512]{1,0:T(8,128)(2,1)S(1)} %copy-done.3, bf16[512,512]{1,0:T(8,128)(2,1)S(1)} %copy-done.1, f32[8,512]{1,0:T(8,128)S(1)} %get-tuple-element.37), kind=kOutput, calls=%fused_computation.5 | convolution fusion | flops 11702272 | bytes 4493312 | tf_op jit(solution)/shard_map/dot_general | solution.py:30
  101.4 2.3 %copy.14 = bf16[768,512]{1,0:T(8,128)(2,1)} copy(bf16[768,512]{0,1:T(8,128)(2,1)} %fusion.1) | data formatting | bytes 1572864
  103.9 9.0 %reduce-scatter.16.cloned.1.call-done = bf16[384,512]{1,0:T(8,128)(2,1)} async-done(((bf16[768,512]{1,0:T(8,128)(2,1)}), bf16[384,512]{1,0:T(8,128)(2,1)}) %reduce-scatter.16.cloned.1.call-update) | async-done | bytes 393232
  112.8 1.2 copy.15
  114.0 92.2 %all-reduce.2 = (f32[384,512]{0,1:T(8,128)S(1)}, f32[256,512]{1,0:T(8,128)S(1)}) all-reduce(bf16[384,512]{0,1:T(8,128)(2,1)S(1)} %copy.15, bf16[256,512]{1,0:T(8,128)(2,1)} %reduce-scatter.14.cloned.1.call-done), channel_id=1, replica_groups=mesh['dom'=16,'grp'=2] {'dom'}, use_global_device_ids=true, to_apply=%region_8.10 | all-reduce | flops 327680 | bytes 1966080 | tf_op jit(solution)/shard_map/psum | solution.py:160
  206.2 0.7 multiply_reduce_fusion.1
  207.0 0.8 multiply_reduce_fusion
  209.1 0.6 pad_maximum_fusion.2
  209.6 3.0 %psum.23 = f32[]{:T(128)} all-reduce(f32[]{:T(128)S(6)} %add.174), channel_id=1, replica_groups=mesh['dom'=16,'grp'=2] {'grp'}, use_global_device_ids=true, to_apply=%region_13.15 | all-reduce | flops 1 | bytes 8 | tf_op jit(solution)/shard_map/psum | solution.py:162
  213.3 0.8 broadcast_multiply_fusion.1
  214.2 1.1 copy.13
  (79 shorter events, 2.8 us)
Async XLA Ops:
  7.2 9.8 %copy-start = (bf16[1387,512]{1,0:T(8,128)(2,1)S(1)}, bf16[1387,512]{1,0:T(8,128)(2,1)}, u32[]{:S(2)}) copy-start(bf16[1387,512]{1,0:T(8,128)(2,1)} %param.14) | copy-start | bytes 4260868
  7.2 47.1 %reduce-scatter.8.cloned.1.call-start = ((), (), s32[]{:S(2)}) async-start(), calls=%async_computation.5 | async-start | bytes 24576 | tf_op jit(solution)/shard_map/reduce_scatter | solution.py:134
  9.9 11.4 %collective-permute-start = (bf16[8,512]{1,0:T(8,128)(2,1)S(1)}, bf16[8,512]{1,0:T(8,128)(2,1)S(1)}, u32[]{:S(2)}, u32[]{:S(2)}) collective-permute-start(bf16[8,512]{1,0:T(8,128)(2,1)S(1)} %convolution_convert_fusion.2), channel_id=1, source_target_pairs={{0,2},{2,0},{4,6},{6,4},{8,10},{10,8},{12,14},{14,12},{16,18},{18,... | collective-permute-start | bytes 24584 | tf_op jit(solution)/shard_map/ppermute | solution.py:10
  18.7 0.8 copy-start.6
  18.7 4.2 %copy-start.7 = (s32[2,128]{1,0:T(2,128)S(1)}, s32[2,128]{1,0:T(2,128)}, u32[]{:S(2)}) copy-start(s32[2,128]{1,0:T(2,128)} %param.17) | copy-start | bytes 3076
  21.3 6.1 %collective-permute-start.1 = (bf16[8,512]{1,0:T(8,128)(2,1)S(1)}, bf16[8,512]{1,0:T(8,128)(2,1)S(1)}, u32[]{:S(2)}, u32[]{:S(2)}) collective-permute-start(bf16[8,512]{1,0:T(8,128)(2,1)S(1)} %get-tuple-element.24), channel_id=1, source_target_pairs={{0,4},{2,6},{4,0},{6,2},{8,12},{10,14},{12,8},{14,10},{16,20},{18,... | collective-permute-start | bytes 24584 | tf_op jit(solution)/shard_map/ppermute | solution.py:10
  26.8 3.7 %collective-permute-start.4 = (bf16[8,512]{1,0:T(8,128)(2,1)S(1)}, bf16[8,512]{1,0:T(8,128)(2,1)S(1)}, u32[]{:S(2)}, u32[]{:S(2)}) collective-permute-start(bf16[8,512]{1,0:T(8,128)(2,1)S(1)} %get-tuple-element.25), channel_id=1, source_target_pairs={{0,4},{2,6},{4,0},{6,2},{8,12},{10,14},{12,8},{14,10},{16,20},{18,... | collective-permute-start | bytes 24584 | tf_op jit(solution)/shard_map/ppermute | solution.py:10
  27.4 4.7 %collective-permute-start.2 = (bf16[8,512]{1,0:T(8,128)(2,1)S(1)}, bf16[8,512]{1,0:T(8,128)(2,1)S(1)}, u32[]{:S(2)}, u32[]{:S(2)}) collective-permute-start(bf16[8,512]{1,0:T(8,128)(2,1)S(1)} %broadcast_select_fusion.11), channel_id=1, source_target_pairs={{0,8},{2,10},{4,12},{6,14},{8,0},{10,2},{12,4},{14,6},{16,24},{18,... | collective-permute-start | bytes 24584 | tf_op jit(solution)/shard_map/ppermute | solution.py:10
  30.5 4.2 %collective-permute-start.5 = (bf16[8,512]{1,0:T(8,128)(2,1)S(1)}, bf16[8,512]{1,0:T(8,128)(2,1)S(1)}, u32[]{:S(2)}, u32[]{:S(2)}) collective-permute-start(bf16[8,512]{1,0:T(8,128)(2,1)S(1)} %broadcast_select_fusion.3), channel_id=1, source_target_pairs={{0,8},{2,10},{4,12},{6,14},{8,0},{10,2},{12,4},{14,6},{16,24},{18,... | collective-permute-start | bytes 24584 | tf_op jit(solution)/shard_map/ppermute | solution.py:10
  32.1 4.7 %collective-permute-start.3 = (bf16[8,512]{1,0:T(8,128)(2,1)S(1)}, bf16[8,512]{1,0:T(8,128)(2,1)S(1)}, u32[]{:S(2)}, u32[]{:S(2)}) collective-permute-start(bf16[8,512]{1,0:T(8,128)(2,1)S(1)} %broadcast_select_fusion.13), channel_id=1, source_target_pairs={{0,16},{2,18},{4,20},{6,22},{8,24},{10,26},{12,28},{14,30},{16,0},... | collective-permute-start | bytes 24584 | tf_op jit(solution)/shard_map/ppermute | solution.py:10
  34.7 4.6 %collective-permute-start.6 = (bf16[8,512]{1,0:T(8,128)(2,1)S(1)}, bf16[8,512]{1,0:T(8,128)(2,1)S(1)}, u32[]{:S(2)}, u32[]{:S(2)}) collective-permute-start(bf16[8,512]{1,0:T(8,128)(2,1)S(1)} %broadcast_select_fusion.5), channel_id=1, source_target_pairs={{0,16},{2,18},{4,20},{6,22},{8,24},{10,26},{12,28},{14,30},{16,0},... | collective-permute-start | bytes 24584 | tf_op jit(solution)/shard_map/ppermute | solution.py:10
  41.5 1.0 copy-start.8
  42.1 0.6 copy-start.10
  48.0 17.6 %reduce-scatter.10.cloned.1.call-start = ((), (), s32[]{:S(2)}) async-start(), calls=%async_computation.6 | async-start | bytes 24576 | tf_op jit(solution)/shard_map/reduce_scatter | solution.py:134
  49.5 26.9 %reduce-scatter.12.cloned.1.call-start = ((), (), s32[]{:S(2)}) async-start(), calls=%async_computation.7 | async-start | bytes 24576 | tf_op jit(solution)/shard_map/reduce_scatter | solution.py:146
  50.5 53.4 %reduce-scatter.14.cloned.1.call-start = ((), (), s32[]{:S(2)}) async-start(), calls=%async_computation.8 | async-start | bytes 786432 | tf_op jit(solution)/shard_map/reduce_scatter | solution.py:156
  54.3 25.6 %collective-permute-start.7 = (bf16[8,512]{1,0:T(8,128)(2,1)}, bf16[8,512]{1,0:T(8,128)(2,1)S(1)}, u32[]{:S(2)}, u32[]{:S(2)}) collective-permute-start(bf16[8,512]{1,0:T(8,128)(2,1)} %reduce-scatter.8.cloned.1.call-done), channel_id=1, source_target_pairs={{0,2},{2,0},{4,6},{6,4},{8,10},{10,8},{12,14},{14,12},{16,18},{18,... | collective-permute-start | bytes 24584 | tf_op jit(solution)/shard_map/ppermute | solution.py:10
  65.6 11.8 %collective-permute-start.11 = (bf16[8,512]{1,0:T(8,128)(2,1)}, bf16[8,512]{1,0:T(8,128)(2,1)S(1)}, u32[]{:S(2)}, u32[]{:S(2)}) collective-permute-start(bf16[8,512]{1,0:T(8,128)(2,1)} %reduce-scatter.10.cloned.1.call-done), channel_id=1, source_target_pairs={{0,2},{2,0},{4,6},{6,4},{8,10},{10,8},{12,14},{14,12},{16,18},{18,... | collective-permute-start | bytes 24584 | tf_op jit(solution)/shard_map/ppermute | solution.py:10
  78.2 3.7 %collective-permute-start.12 = (bf16[8,512]{1,0:T(8,128)(2,1)S(1)}, bf16[8,512]{1,0:T(8,128)(2,1)S(1)}, u32[]{:S(2)}, u32[]{:S(2)}) collective-permute-start(bf16[8,512]{1,0:T(8,128)(2,1)S(1)} %broadcast_select_fusion), channel_id=1, source_target_pairs={{0,4},{2,6},{4,0},{6,2},{8,12},{10,14},{12,8},{14,10},{16,20},{18,... | collective-permute-start | bytes 24584 | tf_op jit(solution)/shard_map/ppermute | solution.py:10
  79.9 3.7 %collective-permute-start.8 = (bf16[8,512]{1,0:T(8,128)(2,1)S(1)}, bf16[8,512]{1,0:T(8,128)(2,1)S(1)}, u32[]{:S(2)}, u32[]{:S(2)}) collective-permute-start(bf16[8,512]{1,0:T(8,128)(2,1)S(1)} %broadcast_select_fusion.8), channel_id=1, source_target_pairs={{0,4},{2,6},{4,0},{6,2},{8,12},{10,14},{12,8},{14,10},{16,20},{18,... | collective-permute-start | bytes 24584 | tf_op jit(solution)/shard_map/ppermute | solution.py:10
  81.9 3.7 %collective-permute-start.13 = (bf16[8,512]{1,0:T(8,128)(2,1)S(1)}, bf16[8,512]{1,0:T(8,128)(2,1)S(1)}, u32[]{:S(2)}, u32[]{:S(2)}) collective-permute-start(bf16[8,512]{1,0:T(8,128)(2,1)S(1)} %broadcast_select_fusion.2), channel_id=1, source_target_pairs={{0,8},{2,10},{4,12},{6,14},{8,0},{10,2},{12,4},{14,6},{16,24},{18,... | collective-permute-start | bytes 24584 | tf_op jit(solution)/shard_map/ppermute | solution.py:10
  83.6 4.5 %collective-permute-start.9 = (bf16[8,512]{1,0:T(8,128)(2,1)S(1)}, bf16[8,512]{1,0:T(8,128)(2,1)S(1)}, u32[]{:S(2)}, u32[]{:S(2)}) collective-permute-start(bf16[8,512]{1,0:T(8,128)(2,1)S(1)} %broadcast_select_fusion.10), channel_id=1, source_target_pairs={{0,8},{2,10},{4,12},{6,14},{8,0},{10,2},{12,4},{14,6},{16,24},{18,... | collective-permute-start | bytes 24584 | tf_op jit(solution)/shard_map/ppermute | solution.py:10
  85.5 4.5 %collective-permute-start.14 = (bf16[8,512]{1,0:T(8,128)(2,1)S(1)}, bf16[8,512]{1,0:T(8,128)(2,1)S(1)}, u32[]{:S(2)}, u32[]{:S(2)}) collective-permute-start(bf16[8,512]{1,0:T(8,128)(2,1)S(1)} %broadcast_select_fusion.4), channel_id=1, source_target_pairs={{0,16},{2,18},{4,20},{6,22},{8,24},{10,26},{12,28},{14,30},{16,0},... | collective-permute-start | bytes 24584 | tf_op jit(solution)/shard_map/ppermute | solution.py:10
  88.2 5.8 %copy-start.2 = (bf16[8,512]{1,0:T(8,128)(2,1)}, bf16[8,512]{1,0:T(8,128)(2,1)S(1)}, u32[]{:S(2)}) copy-start(bf16[8,512]{1,0:T(8,128)(2,1)S(1)} %broadcast_select_fusion.12) | copy-start | bytes 24580
  88.2 4.6 %collective-permute-start.10 = (bf16[8,512]{1,0:T(8,128)(2,1)S(1)}, bf16[8,512]{1,0:T(8,128)(2,1)S(1)}, u32[]{:S(2)}, u32[]{:S(2)}) collective-permute-start(bf16[8,512]{1,0:T(8,128)(2,1)S(1)} %broadcast_select_fusion.12), channel_id=1, source_target_pairs={{0,16},{2,18},{4,20},{6,22},{8,24},{10,26},{12,28},{14,30},{16,0},... | collective-permute-start | bytes 24584 | tf_op jit(solution)/shard_map/ppermute | solution.py:10
  90.1 3.9 %copy-start.4 = (bf16[8,512]{1,0:T(8,128)(2,1)}, bf16[8,512]{1,0:T(8,128)(2,1)S(1)}, u32[]{:S(2)}) copy-start(bf16[8,512]{1,0:T(8,128)(2,1)S(1)} %collective-permute-done.14) | copy-start | bytes 24580
  90.4 3.6 %copy-start.1 = (bf16[512,512]{1,0:T(8,128)(2,1)S(1)}, bf16[512,512]{1,0:T(8,128)(2,1)}, u32[]{:S(2)}) copy-start(bf16[512,512]{1,0:T(8,128)(2,1)} %param.13) | copy-start | bytes 1572868
  92.8 1.2 copy-start.5
  94.0 18.9 %reduce-scatter.16.cloned.1.call-start = ((), (), s32[]{:S(2)}) async-start(), calls=%async_computation.9 | async-start | bytes 1179648
  95.5 2.7 %copy-start.3 = (bf16[8,512]{1,0:T(8,128)(2,1)S(1)}, bf16[8,512]{1,0:T(8,128)(2,1)}, u32[]{:S(2)}) copy-start(bf16[8,512]{1,0:T(8,128)(2,1)} %reduce-scatter.12.cloned.1.call-done) | copy-start | bytes 24580
  101.4 2.3 %copy-start.11 = (f32[128]{0:T(128)S(1)}, f32[128]{0:T(128)}, u32[]{:S(2)}) copy-start(f32[128]{0:T(128)} %copy-done.10) | copy-start | bytes 1540
  101.4 2.4 %copy-start.12 = (f32[128]{0:T(128)S(1)}, f32[128]{0:T(128)}, u32[]{:S(2)}) copy-start(f32[128]{0:T(128)} %get-tuple-element.38) | copy-start | bytes 1540
  101.4 2.4 %copy-start.9 = (f32[128]{0:T(128)S(1)}, f32[128]{0:T(128)}, u32[]{:S(2)}) copy-start(f32[128]{0:T(128)} %copy-done.8) | copy-start | bytes 1540
  101.4 2.4 %copy-start.13 = (f32[128]{0:T(128)S(1)}, f32[128]{0:T(128)}, u32[]{:S(2)}) copy-start(f32[128]{0:T(128)} %get-tuple-element.42) | copy-start | bytes 1540
Sparse Core Ops, SparseCore 0:
  48.1 6.1 reduce-scatter.7
  57.0 8.5 reduce-scatter.9
  67.8 8.5 reduce-scatter.11
  94.1 7.0 reduce-scatter.13
  103.9 8.9 reduce-scatter.15
where the time goes:
time: 223 us; the launch traced here: 222 us
  blocking collectives  101 us (45%)
  waiting for transfers between devices  38.6 us (17%)
  starting transfers between devices  26 us (12%)
  matrix products  21.7 us (10%)
  between operations  21.3 us (10%)
  local copies, waits for them, and re-layouts  8.72 us (4%)
  other arithmetic  4.92 us (2%)
    psum x1, blocking collectives, per_device(): summed_first, summed_second = lax.psum((part_first, part_second), 'dom')  92.2 us
    ppermute x15, starting transfers between devices, partner_2(): lax.ppermute(value, axis, [(i, i ^ 1 << distance) for i in range(lax.axis...  25.8 us
    reduce_scatter x2, waiting for transfers between devices, per_device(): lax.psum_scatter(far_part.astype(jnp.bfloat16), 'grp', scatter_dimension=...  13.4 us
    reduce_scatter x1, waiting for transfers between devices, per_device(): lax.psum_scatter(own_acc.astype(jnp.bfloat16), 'grp', scatter_dimension=0...  9.1 us
    unnamed x6, waiting for transfers between devices  9.08 us
    dot_general x3, matrix products, backward(): lax.dot_general(rows, grad_pre, (((0,), (0,)), ((), ())), preferred_eleme...  7.36 us
    ppermute x15, waiting for transfers between devices, partner_2(): lax.ppermute(value, axis, [(i, i ^ 1 << distance) for i in range(lax.axis...  7.01 us
    unnamed x31, local copies, waits for them, and re-layouts  4.98 us
  transfers between devices with their start and end apart: 20, of which 11 were waited for; matrix products, arithmetic and copies ran while one was open for 9% of the time, Pallas kernels for 0%

commit v1 on v0

--- a/solution.py
+++ b/solution.py
@@ -1,9 +1,16 @@
+import functools
 import math
 
 import jax
 import jax.numpy as jnp
 from jax import lax
+from jax.experimental import pallas as pl
+from jax.experimental.pallas import tpu as pltpu
 from jax.sharding import PartitionSpec as P
+
+LANES = 128
+F32 = jnp.float32
+BF16 = jnp.bfloat16
 
 
 def partner_2(value, axis, distance):
@@ -101,7 +108,7 @@
     return payload
 
 
-def per_device(
+def spread(
     features, w_first, w_second, relation_table, heads, relations, tails, negatives, partner
 ):
     pre_act, hidden, encoded = encode(features, w_first, w_second)
@@ -164,7 +171,299 @@
     return (jnp.stack(losses), summed_first * factor, summed_second * factor)
 
 
+def swap(value, axes, distance):
+    size = math.prod(lax.axis_size(axis) for axis in axes)
+    return lax.ppermute(value, axes, [(i, i ^ distance) for i in range(size)])
+
+
+def gather_relative(value, axis, bits_at_once):
+    rows = value.shape[0]
+    order = [0]
+    distance = lax.axis_size(axis)
+    while distance > 1:
+        radix = min(bits_at_once, distance)
+        distance //= radix
+        moved = [i * distance for i in range(1, radix)]
+        arrived = [swap(value, (axis,), step) for step in reversed(moved)][::-1]
+        value = jnp.concatenate([value] + arrived, axis=0)
+        order = order + [place ^ step for step in moved for place in order]
+    assert value.shape[0] == rows * len(order)
+    return value, order
+
+
+def first_above(counts):
+    return [sum(counts[:i]) for i in range(len(counts))]
+
+
+def sigmoid_parts(value):
+    small = jnp.exp(-jnp.abs(value))
+    softplus = jnp.maximum(value, 0.0) + jnp.log(1.0 + small)
+    sigmoid = jnp.where(value >= 0.0, 1.0, small) / (1.0 + small)
+    return softplus, sigmoid
+
+
+def score_kernel(
+    sizes,
+    order,
+    scalars,
+    mine,
+    other,
+    w_first,
+    w_second,
+    table,
+    negatives,
+    grad_out,
+    loss_out,
+    slope_out,
+    hidden_out,
+    encoded,
+    ids,
+    grads,
+):
+    width, rows, rounds, edges = sizes
+    group_rows = 2 * rows
+    half = encoded.shape[1] // 2
+    places = len(order)
+    all_rows = places * rows
+    me = scalars[0]
+    mask = scalars[1]
+
+    features = jnp.concatenate([mine[:, :width], other[:, :width]], axis=0)
+    pre_act = jnp.dot(features, w_first[...], preferred_element_type=F32)
+    gate = 1.0 / (1.0 + jnp.exp(-pre_act))
+    hidden = (pre_act * gate).astype(BF16)
+    slope_out[...] = gate * (1.0 + pre_act * (1.0 - gate))
+    hidden_out[...] = hidden
+    encoded[...] = jnp.dot(hidden, w_second[...], preferred_element_type=F32).astype(BF16).astype(F32)
+    ids[:all_rows, :] = mine[:, width:].astype(F32)
+    ids[all_rows:, :] = other[:, width:].astype(F32)
+    grads[...] = jnp.zeros(grads.shape, F32)
+
+    labels = [((i ^ (me * rows)).astype(F32)) for i in range(group_rows)]
+    label_column = (
+        lax.broadcasted_iota(jnp.int32, (group_rows, 1), 0) ^ (me * rows)
+    )
+    drawn = negatives[pl.ds(me, 1), :]
+    counts = jnp.sum((drawn == label_column).astype(F32), axis=1, keepdims=True)
+    negative_count = negatives.shape[1]
+    label_column = label_column.astype(F32)
+    low_column = lax.broadcasted_iota(jnp.int32, (LANES, 1), 0).astype(F32)
+    blocks = table.shape[1] // LANES
+    members = (0, all_rows)
+
+    def id_row(kind, place):
+        return jnp.concatenate(
+            [ids[pl.ds(base + place * rows + kind * rounds + me, 1), :] for base in members], axis=1
+        )
+
+    def pair_rows(place):
+        return jnp.concatenate(
+            [encoded[pl.ds(pl.multiple_of(base + place * rows, rows), rows), :] for base in members],
+            axis=0,
+        )
+
+    for spot in range(places):
+        key = order[spot]
+        far = spot_of(order, key, mask)
+        low = id_row(3, spot)
+        high = id_row(2, spot)
+        low_hot = (low == low_column).astype(BF16)
+        hot = jnp.concatenate(
+            [low_hot * (high == float(block)).astype(BF16) for block in range(blocks)], axis=0
+        )
+        relation = jnp.dot(table[...], hot, preferred_element_type=F32).astype(BF16)
+        near_rows, far_rows = pair_rows(spot), pair_rows(far)
+        near_re, near_im = near_rows[:, :half], near_rows[:, half:]
+        far_re, far_im = far_rows[:, :half], far_rows[:, half:]
+        pairs = jnp.concatenate(
+            [
+                jnp.concatenate(
+                    [
+                        near_re[i : i + 1] * far_re + near_im[i : i + 1] * far_im,
+                        near_re[i : i + 1] * far_im - near_im[i : i + 1] * far_re,
+                    ],
+                    axis=1,
+                ).astype(BF16)
+                for i in range(group_rows)
+            ],
+            axis=0,
+        )
+        scores = jnp.dot(pairs, relation, preferred_element_type=F32)
+        head = id_row(0, spot)
+        tail = id_row(1, spot)
+        negative = jnp.zeros((group_rows, scores.shape[1]), F32)
+        for i in range(group_rows):
+            negative = jnp.where(
+                head == labels[i], scores[i * group_rows : (i + 1) * group_rows], negative
+            )
+        is_tail = tail == label_column
+        positive = jnp.sum(jnp.where(is_tail, negative, 0.0), axis=0, keepdims=True)
+        loss, chance = sigmoid_parts(negative)
+        loss_positive, chance_positive = sigmoid_parts(-positive)
+        if spot == 0:
+            loss_out[...] = loss_positive + jnp.sum(loss * counts, axis=0, keepdims=True) / negative_count
+        weight = (chance / negative_count).astype(BF16).astype(F32) * counts
+        weight = (weight - jnp.where(is_tail, chance_positive, 0.0)).astype(BF16)
+        weights = jnp.concatenate(
+            [weight * (head == labels[i]).astype(BF16) for i in range(group_rows)], axis=0
+        )
+        moved = lax.dot_general(
+            weights, relation, (((1,), (1,)), ((), ())), preferred_element_type=F32
+        )
+        far_grad_re = jnp.zeros((group_rows, half), F32)
+        far_grad_im = jnp.zeros((group_rows, half), F32)
+        near_grad = []
+        for i in range(group_rows):
+            part_re = moved[i * group_rows : (i + 1) * group_rows, :half]
+            part_im = moved[i * group_rows : (i + 1) * group_rows, half:]
+            row_re, row_im = near_re[i : i + 1], near_im[i : i + 1]
+            far_grad_re = far_grad_re + (row_re * part_re - row_im * part_im)
+            far_grad_im = far_grad_im + (row_re * part_im + row_im * part_re)
+            near_grad.append(
+                jnp.concatenate(
+                    [
+                        jnp.sum(far_re * part_re + far_im * part_im, axis=0, keepdims=True),
+                        jnp.sum(far_im * part_re - far_re * part_im, axis=0, keepdims=True),
+                    ],
+                    axis=1,
+                )
+            )
+        near_grad = jnp.concatenate(near_grad, axis=0)
+        far_grad = jnp.concatenate([far_grad_re, far_grad_im], axis=1)
+        for member, base in enumerate(members):
+            span = slice(member * rows, (member + 1) * rows)
+            near_at = pl.ds(base + spot * rows, rows)
+            far_at = pl.ds(pl.multiple_of(base + far * rows, rows), rows)
+            grads[near_at, :] = grads[near_at, :] + near_grad[span]
+            grads[far_at, :] = grads[far_at, :] + far_grad[span]
+    grad_out[...] = grads[...].astype(BF16)
+
+
+def spot_of(order, key, mask):
+    spot_by_key = {value: spot for spot, value in enumerate(order)}
+    place = jnp.int32(spot_by_key[key])
+    bit = 1
+    while bit < len(order):
+        place = place ^ jnp.where((mask & bit) != 0, spot_by_key[bit], 0)
+        bit *= 2
+    return place
+
+
+def total_kernel(
+    limit,
+    width,
+    scalars,
+    mine,
+    other,
+    grad_mine,
+    grad_other,
+    slope,
+    hidden,
+    w_second,
+    loss_mine,
+    loss_other,
+    loss_out,
+    first_out,
+    second_out,
+    first,
+    second,
+):
+    me = scalars[0]
+    all_rows = mine.shape[0]
+    grad = jnp.concatenate(
+        [
+            grad_mine[:all_rows].astype(F32) + grad_other[all_rows:].astype(F32),
+            grad_mine[all_rows:].astype(F32) + grad_other[:all_rows].astype(F32),
+        ],
+        axis=0,
+    ).astype(BF16)
+    across = (((0,), (0,)), ((), ()))
+    total_second = lax.dot_general(hidden[...], grad, across, preferred_element_type=F32)
+    grad_hidden = lax.dot_general(
+        grad, w_second[...], (((1,), (1,)), ((), ())), preferred_element_type=F32
+    )
+    grad_pre = (grad_hidden * slope[...]).astype(BF16)
+    features = jnp.concatenate([mine[:, :width], other[:, :width]], axis=0)
+    total_first = lax.dot_general(features, grad_pre, across, preferred_element_type=F32)
+    squares = jnp.sum(total_first * total_first, axis=(0, 1), keepdims=True) + jnp.sum(
+        total_second * total_second, axis=(0, 1), keepdims=True
+    )
+    factor = jnp.minimum(1.0, limit / jnp.sqrt(squares + 1e-06))
+    first[...] = total_first
+    second[...] = total_second
+    for source, target in ((first, first_out), (second, second_out)):
+        share = target.shape[0]
+        target[...] = source[pl.ds(pl.multiple_of(me * share, share), share), :] * factor
+    edges = loss_out.shape[1]
+    for member in range(2):
+        loss_out[pl.ds(member, 1), :] = jnp.where(
+            me == member, loss_mine[:, :edges], loss_other[:, edges:]
+        )
+
+
+def together(
+    features, w_first, w_second, relation_table, heads, relations, tails, negatives, partner
+):
+    rows, width = features.shape
+    rounds, edges = heads.shape
+    hidden_width, encoded_width = w_second.shape
+    relation_count = relation_table.shape[0]
+    id_rows = jnp.concatenate([heads, tails, relations // LANES, relations % LANES], axis=0)
+    payload = jnp.concatenate([features, id_rows.astype(BF16)], axis=1)
+    table = jnp.pad(relation_table.T, ((0, 0), (0, -relation_count % LANES)))
+    me = lax.axis_index("grp").astype(jnp.int32)
+    mask = lax.dynamic_index_in_dim(partner[:, 0], me, keepdims=False) ^ 0
+    scalars = jnp.stack([me, mask])
+    mine, order = gather_relative(payload, "dom", 4)
+    other = swap(mine, ("grp",), 1)
+    all_rows = 2 * mine.shape[0]
+
+    vmem = pl.BlockSpec(memory_space=pltpu.VMEM)
+    smem = pl.BlockSpec(memory_space=pltpu.SMEM)
+    grad, loss, slope, hidden = pl.pallas_call(
+        functools.partial(score_kernel, (width, rows, rounds, edges), order),
+        out_shape=(
+            jax.ShapeDtypeStruct((all_rows, encoded_width), BF16),
+            jax.ShapeDtypeStruct((1, 2 * edges), F32),
+            jax.ShapeDtypeStruct((all_rows, hidden_width), F32),
+            jax.ShapeDtypeStruct((all_rows, hidden_width), BF16),
+        ),
+        in_specs=[smem] + [vmem] * 6,
+        out_specs=(vmem,) * 4,
+        scratch_shapes=[
+            pltpu.VMEM((all_rows, encoded_width), F32),
+            pltpu.VMEM((all_rows, edges), F32),
+            pltpu.VMEM((all_rows, encoded_width), F32),
+        ],
+        compiler_params=pltpu.CompilerParams(vmem_limit_bytes=24 * 1024 * 1024),
+        name="scores",
+    )(scalars, mine, other, w_first, w_second, table, negatives)
+    grad_other = swap(grad, ("grp",), 1)
+    loss_other = swap(loss, ("grp",), 1)
+    limit = math.sqrt(w_first.size + w_second.size)
+    return pl.pallas_call(
+        functools.partial(total_kernel, limit, width),
+        out_shape=(
+            jax.ShapeDtypeStruct((rounds, edges), F32),
+            jax.ShapeDtypeStruct((w_first.shape[0] // 2, w_first.shape[1]), F32),
+            jax.ShapeDtypeStruct((w_second.shape[0] // 2, w_second.shape[1]), F32),
+        ),
+        in_specs=[smem] + [vmem] * 9,
+        out_specs=(vmem,) * 3,
+        scratch_shapes=[pltpu.VMEM(w_first.shape, F32), pltpu.VMEM(w_second.shape, F32)],
+        compiler_params=pltpu.CompilerParams(vmem_limit_bytes=24 * 1024 * 1024),
+        name="totals",
+    )(scalars, mine, other, grad, grad_other, slope, hidden, w_second, loss, loss_other)
+
+
 def solution(mesh):
+    def per_device(features, w_first, w_second, relation_table, heads, relations, tails, *rest):
+        rounds, edges = heads.shape
+        rows = features.shape[0]
+        fits = mesh.shape["grp"] == rounds == 2 and edges == LANES and 4 * rounds == rows
+        plan = together if fits else spread
+        return plan(features, w_first, w_second, relation_table, heads, relations, tails, *rest)
+
     return jax.shard_map(
         per_device,
         mesh=mesh,

time: 223 us -> 55.1 us (0.25)
  blocking collectives: 101 us -> 0 us
  waiting for transfers between devices: 38.6 us -> 10.2 us
  Pallas kernels: 0 us -> 26.8 us
  matrix products: 21.7 us -> 0 us
  between operations: 21.3 us -> 0.72 us
  starting transfers between devices: 26 us -> 9.87 us
  local copies, waits for them, and re-layouts: 8.72 us -> 2.91 us
    psum x2 -> x0, blocking collectives: 95.1 us -> none  [the longest x1 92.2 us: per_device(): summed_first, summed_second = lax.psum((part_first, part_second), 'dom')]
    pallas_call x0 -> x2, Pallas kernels: none -> 26.8 us  [the longest x1 24 us: together(): pl.pallas_call(functools.partial(score_kernel, (width, rows, rounds, edge...]
    reduce_scatter x4 -> x0, waiting for transfers between devices: 22.6 us -> none  [the longest x2 13.4 us: per_device(): lax.psum_scatter(far_part.astype(jnp.bfloat16), 'grp', scatter_dimension=...]
    dot_general x26 -> x0, matrix products: 21.7 us -> none  [the longest x3 7.36 us: backward(): lax.dot_general(rows, grad_pre, (((0,), (0,)), ((), ())), preferred_eleme...]
    ppermute x15 -> x9, starting transfers between devices: 25.8 us -> 9.87 us  [swap(): return lax.ppermute(value, axes, [(i, i ^ distance) for i in range(size)])]
    unnamed x6 -> x0, waiting for transfers between devices: 9.08 us -> none
    all_gather x3 -> x0, blocking collectives: 5.4 us -> none  [the longest x2 3.6 us: per_device(): far_block = lax.all_gather(arrived, 'grp', axis=0, tiled=True)]
    ppermute x15 -> x9, waiting for transfers between devices: 7.01 us -> 10.2 us  [swap(): return lax.ppermute(value, axes, [(i, i ^ distance) for i in range(size)])]
  transfers between devices with their start and end apart: 20 -> 9, of which waited for: 11 -> 5; matrix products, arithmetic and copies ran while one was open for 9% -> 6% of each run, Pallas kernels for 0% -> 0%
where the time goes in v1:
time: 55.1 us; the launch traced here: 54.8 us
  Pallas kernels  26.8 us (49%)
  waiting for transfers between devices  10.2 us (19%)
  starting transfers between devices  9.87 us (18%)
  other arithmetic  4.3 us (8%)
  local copies, waits for them, and re-layouts  2.91 us (5%)
  between operations  0.72 us (1%)
    pallas_call x1, Pallas kernels, together(): pl.pallas_call(functools.partial(score_kernel, (width, rows, rounds, edge...  24 us
    ppermute x9, waiting for transfers between devices, swap(): return lax.ppermute(value, axes, [(i, i ^ distance) for i in range(size)])  10.2 us
    ppermute x9, starting transfers between devices, swap(): return lax.ppermute(value, axes, [(i, i ^ distance) for i in range(size)])  9.87 us
    pallas_call x1, Pallas kernels, together(): pl.pallas_call(functools.partial(total_kernel, limit, width), out_shape=(...  2.82 us
    unnamed x14, local copies, waits for them, and re-layouts  2.26 us
    another operation x3, other arithmetic  2.06 us
  transfers between devices with their start and end apart: 9, of which 5 were waited for; matrix products, arithmetic and copies ran while one was open for 6% of the time, Pallas kernels for 0%

profile of v1, /device:TPU:0, one launch (start us, length us, event | category | flops | bytes accessed | tf_op | source)
XLA Modules:
  0.0 54.8 jit_solution(7915734745626790209)
XLA Ops:
  0.6 0.0 copy-start
  0.6 0.7 %convert.12 = bf16[2,128]{1,0:T(2,128)(2,1)S(1)} convert(s32[2,128]{1,0:T(2,128)} %param.13) | non-fusion elementwise | flops 256 | bytes 1536 | tf_op jit(solution)/shard_map/convert
  1.3 0.7 %convert.13 = bf16[2,128]{1,0:T(2,128)(2,1)S(1)} convert(s32[2,128]{1,0:T(2,128)} %param.15) | non-fusion elementwise | flops 256 | bytes 1536 | tf_op jit(solution)/shard_map/convert.1
  2.0 0.7 %fusion.1 = (bf16[2,128]{1,0:T(2,128)(2,1)S(1)}, bf16[2,128]{1,0:T(2,128)(2,1)S(1)}) fusion(s32[2,128]{1,0:T(2,128)} %param.14), kind=kLoop, calls=%fused_computation.15 | loop fusion | flops 5376 | bytes 2048 | tf_op jit(solution)/shard_map/convert.2
  2.7 0.7 %maximum_maximum_fusion = (bf16[8,896]{1,0:T(8,128)(2,1)S(1)}, bf16[128,896]{1,0:T(8,128)(2,1)S(1)}) fusion(bf16[2,128]{1,0:T(2,128)(2,1)S(1)} %get-tuple-element.14, bf16[2,128]{1,0:T(2,128)(2,1)S(1)} %get-tuple-element.13, bf16[2,128]{1,0:T(2,128)(2,1)S(1)} %convert.13, bf16[2,128]{1,0:T(2,128)(2,1)S(1)} %convert.12, bf16[8,768]{1,0:T(8,128)(2,1)} %param.9), kind=kLoop, calls=%fused_computation.8 | loop fusion | flops 71679 | bytes 43008 | tf_op jit(solution)/shard_map/concatenate | solution.py:412
  3.4 4.0 %collective-permute-start.1 = (bf16[8,896]{1,0:T(8,128)(2,1)S(1)}, bf16[8,896]{1,0:T(8,128)(2,1)S(1)}, u32[]{:S(2)}, u32[]{:S(2)}) collective-permute-start(bf16[8,896]{1,0:T(8,128)(2,1)S(1)} %get-tuple-element.11), channel_id=1, source_target_pairs={{0,16},{2,18},{4,20},{6,22},{8,24},{10,26},{12,28},{14,30},{16,0},... | collective-permute-start | bytes 43016 | tf_op jit(solution)/shard_map/ppermute | solution.py:176
  7.5 1.6 %collective-permute-start = (bf16[8,896]{1,0:T(8,128)(2,1)S(1)}, bf16[8,896]{1,0:T(8,128)(2,1)S(1)}, u32[]{:S(2)}, u32[]{:S(2)}) collective-permute-start(bf16[8,896]{1,0:T(8,128)(2,1)S(1)} %get-tuple-element.11), channel_id=1, source_target_pairs={{0,8},{2,10},{4,12},{6,14},{8,0},{10,2},{12,4},{14,6},{16,24},{18,... | collective-permute-start | bytes 43016 | tf_op jit(solution)/shard_map/ppermute | solution.py:176
  9.0 0.0 collective-permute-start.2
  9.0 0.1 collective-permute-done.1
  9.2 2.0 %collective-permute-done = bf16[8,896]{1,0:T(8,128)(2,1)S(1)} collective-permute-done((bf16[8,896]{1,0:T(8,128)(2,1)S(1)}, bf16[8,896]{1,0:T(8,128)(2,1)S(1)}, u32[]{:S(2)}, u32[]{:S(2)}) %collective-permute-start) | collective-permute-done | bytes 14368 | tf_op jit(solution)/shard_map/ppermute | solution.py:176
  11.2 3.4 %collective-permute-done.2 = bf16[8,896]{1,0:T(8,128)(2,1)S(1)} collective-permute-done((bf16[8,896]{1,0:T(8,128)(2,1)S(1)}, bf16[8,896]{1,0:T(8,128)(2,1)S(1)}, u32[]{:S(2)}, u32[]{:S(2)}) %collective-permute-start.2) | collective-permute-done | bytes 14368 | tf_op jit(solution)/shard_map/ppermute | solution.py:176
  14.6 0.7 %pad_maximum_fusion = bf16[32,896]{1,0:T(8,128)(2,1)S(1)} fusion(bf16[8,896]{1,0:T(8,128)(2,1)S(1)} %collective-permute-done.2, bf16[8,896]{1,0:T(8,128)(2,1)S(1)} %collective-permute-done.1, bf16[8,896]{1,0:T(8,128)(2,1)S(1)} %collective-permute-done, bf16[2,128]{1,0:T(2,128)(2,1)S(1)} %get-tuple-element.14, bf16[2,128]{1,0:T(2,128)(2,1)S(1)} %get-tuple-element.13, ...), kind=kLoop, calls=%fused_computation | loop fusion | flops 458752 | bytes 114688 | tf_op jit(solution)/shard_map/concatenate | solution.py:188
  15.3 2.5 %collective-permute-start.5 = (bf16[32,896]{1,0:T(8,128)(2,1)S(1)}, bf16[32,896]{1,0:T(8,128)(2,1)S(1)}, u32[]{:S(2)}, u32[]{:S(2)}) collective-permute-start(bf16[32,896]{1,0:T(8,128)(2,1)S(1)} %pad_maximum_fusion), channel_id=1, source_target_pairs={{0,6},{2,4},{4,2},{6,0},{8,14},{10,12},{12,10},{14,8},{16,22},{18,... | collective-permute-start | bytes 172040 | tf_op jit(solution)/shard_map/ppermute | solution.py:176
  17.8 0.5 collective-permute-start.4
  18.3 0.5 collective-permute-start.3
  18.9 3.6 %collective-permute-done.3 = bf16[32,896]{1,0:T(8,128)(2,1)S(1)} collective-permute-done((bf16[32,896]{1,0:T(8,128)(2,1)S(1)}, bf16[32,896]{1,0:T(8,128)(2,1)S(1)}, u32[]{:S(2)}, u32[]{:S(2)}) %collective-permute-start.3) | collective-permute-done | bytes 57376 | tf_op jit(solution)/shard_map/ppermute | solution.py:176
  22.5 0.0 collective-permute-done.4
  22.5 0.0 collective-permute-done.5
  22.5 0.1 collective-permute-start.6
  22.6 1.8 %copy.12 = bf16[1387,512]{0,1:T(8,128)(2,1)S(1)} copy(bf16[1387,512]{1,0:T(8,128)(2,1)} %param.12) | data formatting | bytes 2840576 | tf_op args[3]
  24.4 0.0 copy-done
  24.5 0.5 constant_dynamic-slice_fusion
  25.0 0.0 copy-start.1
  25.0 0.0 copy-start.2
  25.0 0.0 copy-start.3
  25.0 0.1 pad.4.table
  25.1 0.8 %pad_add_fusion.scalars = s32[2]{0:T(128)S(1)} fusion(s32[1]{0:T(128)} %bitcast.1, s32[1]{0:T(128)} %bitcast), kind=kLoop, calls=%fused_computation.16 | loop fusion | flops 2 | bytes 16 | tf_op jit(solution)/shard_map/stack | solution.py:416
  25.9 0.0 collective-permute-done.6.other
  25.9 0.1 copy-done.1
  26.0 0.3 copy-done.2
  26.3 0.0 copy-done.3
  26.3 24.0 %scores.1 = (bf16[256,512]{1,0:T(8,128)(2,1)S(1)}, f32[1,256]{1,0:T(1,128)S(1)}, f32[256,512]{1,0:T(8,128)S(1)}, bf16[256,512]{1,0:T(8,128)(2,1)S(1)}) custom-call(s32[2]{0:T(128)S(1)} %pad_add_fusion.scalars, bf16[128,896]{1,0:T(8,128)(2,1)S(1)} %constant_dynamic-update-slice_fusion.mine, bf16[128,896]{1,0:T(8,128)(2,1)S(1)} %collective-permute-done.6.other, ...), custom_call_target="tpu_custom_call" | custom-call | tf_op jit(solution)/shard_map/scores/pallas_call | solution.py:423
  50.2 0.6 %collective-permute-start.7 = (bf16[256,512]{1,0:T(8,128)(2,1)S(1)}, bf16[256,512]{1,0:T(8,128)(2,1)S(1)}, u32[]{:S(2)}, u32[]{:S(2)}) collective-permute-start(bf16[256,512]{1,0:T(8,128)(2,1)S(1)} %get-tuple-element.7.grad_mine), channel_id=1, source_target_pairs={{0,1},{1,0},{2,3},{3,2},{4,5},{5,4},{6,7},{7,6},{8,9},{9,8},{10,11... | collective-permute-start | bytes 786440 | tf_op jit(solution)/shard_map/ppermute | solution.py:176
  50.8 0.1 collective-permute-start.8
  50.9 1.1 %collective-permute-done.8.loss_other = f32[1,256]{1,0:T(1,128)S(1)} collective-permute-done((f32[1,256]{1,0:T(1,128)S(1)}, f32[1,256]{1,0:T(1,128)S(1)}, u32[]{:S(2)}, u32[]{:S(2)}) %collective-permute-start.8) | collective-permute-done | bytes 1056 | tf_op jit(solution)/shard_map/ppermute | solution.py:176
  52.0 0.0 collective-permute-done.7.grad_other
  52.0 2.8 %totals.1 = (f32[2,128]{1,0:T(2,128)}, f32[384,512]{1,0:T(8,128)}, f32[256,512]{1,0:T(8,128)}) custom-call(s32[2]{0:T(128)S(1)} %pad_add_fusion.scalars, bf16[128,896]{1,0:T(8,128)(2,1)S(1)} %constant_dynamic-update-slice_fusion.mine, bf16[128,896]{1,0:T(8,128)(2,1)S(1)} %collective-permute-done.6.other, bf16[256,512]{1,0:T(8,128)(2,1)S(1)} %get-tuple-element.7.grad_mine, ...), custom_call_target="tpu_custom_call" | custom-call | tf_op jit(solution)/shard_map/totals/pallas_call | solution.py:444
  (6 shorter events, 0.1 us)
Async XLA Ops:
  0.6 23.8 %copy-start = (s32[2,16]{1,0:T(2,128)S(1)}, s32[2,16]{1,0:T(2,128)}, u32[]{:S(2)}) copy-start(s32[2,16]{1,0:T(2,128)} %param.17) | copy-start | bytes 388
  3.4 5.7 %collective-permute-start.1 = (bf16[8,896]{1,0:T(8,128)(2,1)S(1)}, bf16[8,896]{1,0:T(8,128)(2,1)S(1)}, u32[]{:S(2)}, u32[]{:S(2)}) collective-permute-start(bf16[8,896]{1,0:T(8,128)(2,1)S(1)} %get-tuple-element.11), channel_id=1, source_target_pairs={{0,16},{2,18},{4,20},{6,22},{8,24},{10,26},{12,28},{14,30},{16,0},... | collective-permute-start | bytes 43016 | tf_op jit(solution)/shard_map/ppermute | solution.py:176
  7.5 3.7 %collective-permute-start = (bf16[8,896]{1,0:T(8,128)(2,1)S(1)}, bf16[8,896]{1,0:T(8,128)(2,1)S(1)}, u32[]{:S(2)}, u32[]{:S(2)}) collective-permute-start(bf16[8,896]{1,0:T(8,128)(2,1)S(1)} %get-tuple-element.11), channel_id=1, source_target_pairs={{0,8},{2,10},{4,12},{6,14},{8,0},{10,2},{12,4},{14,6},{16,24},{18,... | collective-permute-start | bytes 43016 | tf_op jit(solution)/shard_map/ppermute | solution.py:176
  9.0 5.5 %collective-permute-start.2 = (bf16[8,896]{1,0:T(8,128)(2,1)S(1)}, bf16[8,896]{1,0:T(8,128)(2,1)S(1)}, u32[]{:S(2)}, u32[]{:S(2)}) collective-permute-start(bf16[8,896]{1,0:T(8,128)(2,1)S(1)} %get-tuple-element.11), channel_id=1, source_target_pairs={{0,24},{2,26},{4,28},{6,30},{8,16},{10,18},{12,20},{14,22},{16,8},... | collective-permute-start | bytes 43016 | tf_op jit(solution)/shard_map/ppermute | solution.py:176
  15.3 7.2 %collective-permute-start.5 = (bf16[32,896]{1,0:T(8,128)(2,1)S(1)}, bf16[32,896]{1,0:T(8,128)(2,1)S(1)}, u32[]{:S(2)}, u32[]{:S(2)}) collective-permute-start(bf16[32,896]{1,0:T(8,128)(2,1)S(1)} %pad_maximum_fusion), channel_id=1, source_target_pairs={{0,6},{2,4},{4,2},{6,0},{8,14},{10,12},{12,10},{14,8},{16,22},{18,... | collective-permute-start | bytes 172040 | tf_op jit(solution)/shard_map/ppermute | solution.py:176
  17.8 4.7 %collective-permute-start.4 = (bf16[32,896]{1,0:T(8,128)(2,1)S(1)}, bf16[32,896]{1,0:T(8,128)(2,1)S(1)}, u32[]{:S(2)}, u32[]{:S(2)}) collective-permute-start(bf16[32,896]{1,0:T(8,128)(2,1)S(1)} %pad_maximum_fusion), channel_id=1, source_target_pairs={{0,4},{2,6},{4,0},{6,2},{8,12},{10,14},{12,8},{14,10},{16,20},{18,... | collective-permute-start | bytes 172040 | tf_op jit(solution)/shard_map/ppermute | solution.py:176
  18.3 4.2 %collective-permute-start.3 = (bf16[32,896]{1,0:T(8,128)(2,1)S(1)}, bf16[32,896]{1,0:T(8,128)(2,1)S(1)}, u32[]{:S(2)}, u32[]{:S(2)}) collective-permute-start(bf16[32,896]{1,0:T(8,128)(2,1)S(1)} %pad_maximum_fusion), channel_id=1, source_target_pairs={{0,2},{2,0},{4,6},{6,4},{8,10},{10,8},{12,14},{14,12},{16,18},{18,... | collective-permute-start | bytes 172040 | tf_op jit(solution)/shard_map/ppermute | solution.py:176
  22.5 3.4 %collective-permute-start.6 = (bf16[128,896]{1,0:T(8,128)(2,1)S(1)}, bf16[128,896]{1,0:T(8,128)(2,1)S(1)}, u32[]{:S(2)}, u32[]{:S(2)}) collective-permute-start(bf16[128,896]{1,0:T(8,128)(2,1)S(1)} %constant_dynamic-update-slice_fusion.mine), channel_id=1, source_target_pairs={{0,1},{1,0},{2,3},{3,2},{4,5},{5,4},{6,7},{7,6},{8,9},{9,8},{10,11... | collective-permute-start | bytes 688136 | tf_op jit(solution)/shard_map/ppermute | solution.py:176
  25.0 1.0 %copy-start.1 = (bf16[512,512]{1,0:T(8,128)(2,1)S(1)}, bf16[512,512]{1,0:T(8,128)(2,1)}, u32[]{:S(2)}) copy-start(bf16[512,512]{1,0:T(8,128)(2,1)} %w_second.3) | copy-start | bytes 1572868
  25.0 1.3 %copy-start.2 = (bf16[768,512]{1,0:T(8,128)(2,1)S(1)}, bf16[768,512]{1,0:T(8,128)(2,1)}, u32[]{:S(2)}) copy-start(bf16[768,512]{1,0:T(8,128)(2,1)} %w_first.1) | copy-start | bytes 2359300
  25.0 1.3 %copy-start.3 = (s32[2,512]{1,0:T(2,128)S(1)}, s32[2,512]{1,0:T(2,128)}, u32[]{:S(2)}) copy-start(s32[2,512]{1,0:T(2,128)} %negatives.1) | copy-start | bytes 12292
  50.2 1.7 %collective-permute-start.7 = (bf16[256,512]{1,0:T(8,128)(2,1)S(1)}, bf16[256,512]{1,0:T(8,128)(2,1)S(1)}, u32[]{:S(2)}, u32[]{:S(2)}) collective-permute-start(bf16[256,512]{1,0:T(8,128)(2,1)S(1)} %get-tuple-element.7.grad_mine), channel_id=1, source_target_pairs={{0,1},{1,0},{2,3},{3,2},{4,5},{5,4},{6,7},{7,6},{8,9},{9,8},{10,11... | collective-permute-start | bytes 786440 | tf_op jit(solution)/shard_map/ppermute | solution.py:176
  50.8 1.2 %collective-permute-start.8 = (f32[1,256]{1,0:T(1,128)S(1)}, f32[1,256]{1,0:T(1,128)S(1)}, u32[]{:S(2)}, u32[]{:S(2)}) collective-permute-start(f32[1,256]{1,0:T(1,128)S(1)} %get-tuple-element.10.loss_mine), channel_id=1, source_target_pairs={{0,1},{1,0},{2,3},{3,2},{4,5},{5,4},{6,7},{7,6},{8,9},{9,8},{10,11... | collective-permute-start | bytes 3080 | tf_op jit(solution)/shard_map/ppermute | solution.py:176

commit v2 on v1

--- a/solution.py
+++ b/solution.py
@@ -171,28 +171,94 @@
     return (jnp.stack(losses), summed_first * factor, summed_second * factor)
 
 
-def swap(value, axes, distance):
-    size = math.prod(lax.axis_size(axis) for axis in axes)
-    return lax.ppermute(value, axes, [(i, i ^ distance) for i in range(size)])
-
-
-def gather_relative(value, axis, bits_at_once):
-    rows = value.shape[0]
-    order = [0]
-    distance = lax.axis_size(axis)
-    while distance > 1:
-        radix = min(bits_at_once, distance)
-        distance //= radix
-        moved = [i * distance for i in range(1, radix)]
-        arrived = [swap(value, (axis,), step) for step in reversed(moved)][::-1]
-        value = jnp.concatenate([value] + arrived, axis=0)
-        order = order + [place ^ step for step in moved for place in order]
-    assert value.shape[0] == rows * len(order)
-    return value, order
-
-
-def first_above(counts):
-    return [sum(counts[:i]) for i in range(len(counts))]
+ROUNDS = 2
+HEAD, TAIL, HIGH, LOW = 0, 1, 2, 3
+
+
+def swap(value, axis, distance):
+    return lax.ppermute(value, axis, [(i, i ^ distance) for i in range(lax.axis_size(axis))])
+
+
+def distances_of(size):
+    steps = []
+    while size > 4:
+        size //= 2
+        steps.append([size])
+    return steps + [list(range(size - 1, 0, -1))]
+
+
+def join(value, axis, step, beside=None):
+    arrived = [swap(value, axis, distance) for distance in step]
+    if beside is not None:
+        *arrived, beside = lax.optimization_barrier((*arrived[::-1], beside))
+        arrived = arrived[::-1]
+    return jnp.concatenate([value] + arrived, axis=0), beside
+
+
+def keys_of(size):
+    keys = [0]
+    for step in distances_of(size):
+        keys = keys + [key ^ distance for distance in step for key in keys]
+    return keys
+
+
+def place_of(mask, keys):
+    place, bit = jnp.int32(0), 1
+    while bit < len(keys):
+        place = place ^ jnp.where((mask & bit) != 0, keys.index(bit), 0)
+        bit *= 2
+    return place
+
+
+def id_row(ids, kind, place, me, rows):
+    return ids[pl.ds(place * rows + kind * ROUNDS + me, 1), :]
+
+
+def pick_relations(ids, places, me, rows, table, picked):
+    low_column = lax.broadcasted_iota(jnp.int32, (LANES, 1), 0).astype(F32)
+    for first in range(places.start, places.stop, 2):
+        low, high = [
+            jnp.concatenate([id_row(ids, kind, place, me, rows) for place in (first, first + 1)], axis=1)
+            for kind in (LOW, HIGH)
+        ]
+        low_hot = (low == low_column).astype(BF16)
+        hot = jnp.concatenate(
+            [low_hot * (high == float(block)).astype(BF16) for block in range(table.shape[1] // LANES)],
+            axis=0,
+        )
+        columns = jnp.dot(table[...], hot, preferred_element_type=F32).astype(BF16)
+        picked[first] = columns[:, :LANES]
+        picked[first + 1] = columns[:, LANES:]
+
+
+def pack_kernel(features, heads, relations, tails, packed, rows, ids, sems):
+    sources = (features, heads, relations, tails)
+    targets = (rows, ids.at[0], ids.at[1], ids.at[2])
+    copies = [
+        pltpu.make_async_copy(source, target, sems.at[i])
+        for i, (source, target) in enumerate(zip(sources, targets, strict=True))
+    ]
+    for copy in copies:
+        copy.start()
+    for copy in copies:
+        copy.wait()
+    width = features.shape[1]
+    packed[:, :width] = rows[...]
+    columns = [ids[0], ids[2], ids[1] // LANES, ids[1] % LANES]
+    packed[:, width:] = jnp.concatenate(columns, axis=0).astype(F32).astype(BF16)
+
+
+def early_kernel(rows, width, block, table, picked, ids):
+    ids[...] = block[:, width:].astype(F32)
+    me = lax.axis_index("grp").astype(jnp.int32)
+    pick_relations(ids, range(block.shape[0] // rows), me, rows, table, picked)
+
+
+def late_kernel(rows, width, skipped, block, table, begun, picked, ids):
+    del begun
+    ids[...] = block[:, width:].astype(F32)
+    me = lax.axis_index("grp").astype(jnp.int32)
+    pick_relations(ids, range(skipped, block.shape[0] // rows), me, rows, table, picked)
 
 
 def sigmoid_parts(value):
@@ -203,15 +269,16 @@
 
 
 def score_kernel(
-    sizes,
-    order,
-    scalars,
+    rows,
+    keys,
+    partner,
     mine,
     other,
     w_first,
     w_second,
     table,
     negatives,
+    picked_mine,
     grad_out,
     loss_out,
     slope_out,
@@ -219,15 +286,24 @@
     encoded,
     ids,
     grads,
+    picked_other,
+    scores_kept,
+    weights_kept,
+    partner_kept,
+    partner_sem,
 ):
-    width, rows, rounds, edges = sizes
+    fetch = pltpu.make_async_copy(partner, partner_kept, partner_sem)
+    fetch.start()
+    width = w_first.shape[0]
+    half = encoded.shape[1] // 2
+    places = len(keys)
+    all_rows = places * rows
     group_rows = 2 * rows
-    half = encoded.shape[1] // 2
-    places = len(order)
-    all_rows = places * rows
-    me = scalars[0]
-    mask = scalars[1]
-
+    members = (0, all_rows)
+    me = lax.axis_index("grp").astype(jnp.int32)
+
+    ids[:all_rows, :] = mine[:, width:].astype(F32)
+    ids[all_rows:, :] = other[:, width:].astype(F32)
     features = jnp.concatenate([mine[:, :width], other[:, :width]], axis=0)
     pre_act = jnp.dot(features, w_first[...], preferred_element_type=F32)
     gate = 1.0 / (1.0 + jnp.exp(-pre_act))
@@ -235,44 +311,34 @@
     slope_out[...] = gate * (1.0 + pre_act * (1.0 - gate))
     hidden_out[...] = hidden
     encoded[...] = jnp.dot(hidden, w_second[...], preferred_element_type=F32).astype(BF16).astype(F32)
-    ids[:all_rows, :] = mine[:, width:].astype(F32)
-    ids[all_rows:, :] = other[:, width:].astype(F32)
-    grads[...] = jnp.zeros(grads.shape, F32)
-
-    labels = [((i ^ (me * rows)).astype(F32)) for i in range(group_rows)]
-    label_column = (
-        lax.broadcasted_iota(jnp.int32, (group_rows, 1), 0) ^ (me * rows)
-    )
+    pick_relations(ids.at[pl.ds(all_rows, all_rows)], range(places), me, rows, table, picked_other)
+
+    labels = [(i ^ (me * rows)).astype(F32) for i in range(group_rows)]
+    label_column = lax.broadcasted_iota(jnp.int32, (group_rows, 1), 0) ^ (me * rows)
     drawn = negatives[pl.ds(me, 1), :]
     counts = jnp.sum((drawn == label_column).astype(F32), axis=1, keepdims=True)
     negative_count = negatives.shape[1]
     label_column = label_column.astype(F32)
-    low_column = lax.broadcasted_iota(jnp.int32, (LANES, 1), 0).astype(F32)
-    blocks = table.shape[1] // LANES
-    members = (0, all_rows)
-
-    def id_row(kind, place):
+    fetch.wait()
+    far_place = place_of(partner_kept[me, 0], keys)
+    low_bit = far_place & -far_place
+
+    def edge_ids(kind, place):
         return jnp.concatenate(
-            [ids[pl.ds(base + place * rows + kind * rounds + me, 1), :] for base in members], axis=1
-        )
-
-    def pair_rows(place):
+            [id_row(ids.at[pl.ds(base, all_rows)], kind, place, me, rows) for base in members], axis=1
+        )
+
+    def group_of(place):
         return jnp.concatenate(
             [encoded[pl.ds(pl.multiple_of(base + place * rows, rows), rows), :] for base in members],
             axis=0,
         )
 
-    for spot in range(places):
-        key = order[spot]
-        far = spot_of(order, key, mask)
-        low = id_row(3, spot)
-        high = id_row(2, spot)
-        low_hot = (low == low_column).astype(BF16)
-        hot = jnp.concatenate(
-            [low_hot * (high == float(block)).astype(BF16) for block in range(blocks)], axis=0
-        )
-        relation = jnp.dot(table[...], hot, preferred_element_type=F32).astype(BF16)
-        near_rows, far_rows = pair_rows(spot), pair_rows(far)
+    def relations_of(place):
+        return jnp.concatenate([picked_mine[place], picked_other[place]], axis=1)
+
+    for place in range(places):
+        near_rows, far_rows = group_of(place), group_of(place ^ far_place)
         near_re, near_im = near_rows[:, :half], near_rows[:, half:]
         far_re, far_im = far_rows[:, :half], far_rows[:, half:]
         pairs = jnp.concatenate(
@@ -288,42 +354,67 @@
             ],
             axis=0,
         )
-        scores = jnp.dot(pairs, relation, preferred_element_type=F32)
-        head = id_row(0, spot)
-        tail = id_row(1, spot)
+        scores = jnp.dot(pairs, relations_of(place), preferred_element_type=F32)
+        head = edge_ids(HEAD, place)
         negative = jnp.zeros((group_rows, scores.shape[1]), F32)
         for i in range(group_rows):
             negative = jnp.where(
                 head == labels[i], scores[i * group_rows : (i + 1) * group_rows], negative
             )
-        is_tail = tail == label_column
+        scores_kept[place] = negative
+
+    for place in range(places):
+        negative = scores_kept[place]
+        is_tail = edge_ids(TAIL, place) == label_column
         positive = jnp.sum(jnp.where(is_tail, negative, 0.0), axis=0, keepdims=True)
         loss, chance = sigmoid_parts(negative)
         loss_positive, chance_positive = sigmoid_parts(-positive)
-        if spot == 0:
+        if place == 0:
             loss_out[...] = loss_positive + jnp.sum(loss * counts, axis=0, keepdims=True) / negative_count
         weight = (chance / negative_count).astype(BF16).astype(F32) * counts
-        weight = (weight - jnp.where(is_tail, chance_positive, 0.0)).astype(BF16)
+        weights_kept[place] = (weight - jnp.where(is_tail, chance_positive, 0.0)).astype(BF16)
+
+    for pair in range(places // 2):
+        place = pair + (pair & -low_bit)
+        far = place ^ far_place
+        near_weight, far_weight = weights_kept[place], weights_kept[far]
+        near_head, far_head = edge_ids(HEAD, place), edge_ids(HEAD, far)
+        far_hot = (far_head == label_column).astype(BF16)
+        near_rows, far_rows = group_of(place), group_of(far)
+        near_re, near_im = near_rows[:, :half], near_rows[:, half:]
+        far_re, far_im = far_rows[:, :half], far_rows[:, half:]
         weights = jnp.concatenate(
-            [weight * (head == labels[i]).astype(BF16) for i in range(group_rows)], axis=0
-        )
-        moved = lax.dot_general(
-            weights, relation, (((1,), (1,)), ((), ())), preferred_element_type=F32
+            [
+                jnp.concatenate(
+                    [near_weight * (near_head == labels[i]).astype(BF16), far_weight[i : i + 1] * far_hot],
+                    axis=1,
+                )
+                for i in range(group_rows)
+            ],
+            axis=0,
+        )
+        relation = relations_of(place)
+        relation = jnp.concatenate([relation[:half], -relation[half:]], axis=0)
+        joint = lax.dot_general(
+            weights,
+            jnp.concatenate([relation, relations_of(far)], axis=1),
+            (((1,), (1,)), ((), ())),
+            preferred_element_type=F32,
         )
         far_grad_re = jnp.zeros((group_rows, half), F32)
         far_grad_im = jnp.zeros((group_rows, half), F32)
         near_grad = []
         for i in range(group_rows):
-            part_re = moved[i * group_rows : (i + 1) * group_rows, :half]
-            part_im = moved[i * group_rows : (i + 1) * group_rows, half:]
+            part_re = joint[i * group_rows : (i + 1) * group_rows, :half]
+            part_im = joint[i * group_rows : (i + 1) * group_rows, half:]
             row_re, row_im = near_re[i : i + 1], near_im[i : i + 1]
-            far_grad_re = far_grad_re + (row_re * part_re - row_im * part_im)
-            far_grad_im = far_grad_im + (row_re * part_im + row_im * part_re)
+            far_grad_re = far_grad_re + (row_re * part_re + row_im * part_im)
+            far_grad_im = far_grad_im + (row_im * part_re - row_re * part_im)
             near_grad.append(
                 jnp.concatenate(
                     [
-                        jnp.sum(far_re * part_re + far_im * part_im, axis=0, keepdims=True),
-                        jnp.sum(far_im * part_re - far_re * part_im, axis=0, keepdims=True),
+                        jnp.sum(far_re * part_re - far_im * part_im, axis=0, keepdims=True),
+                        jnp.sum(far_im * part_re + far_re * part_im, axis=0, keepdims=True),
                     ],
                     axis=1,
                 )
@@ -332,27 +423,13 @@
         far_grad = jnp.concatenate([far_grad_re, far_grad_im], axis=1)
         for member, base in enumerate(members):
             span = slice(member * rows, (member + 1) * rows)
-            near_at = pl.ds(base + spot * rows, rows)
-            far_at = pl.ds(pl.multiple_of(base + far * rows, rows), rows)
-            grads[near_at, :] = grads[near_at, :] + near_grad[span]
-            grads[far_at, :] = grads[far_at, :] + far_grad[span]
+            grads[pl.ds(pl.multiple_of(base + place * rows, rows), rows), :] = near_grad[span]
+            grads[pl.ds(pl.multiple_of(base + far * rows, rows), rows), :] = far_grad[span]
     grad_out[...] = grads[...].astype(BF16)
-
-
-def spot_of(order, key, mask):
-    spot_by_key = {value: spot for spot, value in enumerate(order)}
-    place = jnp.int32(spot_by_key[key])
-    bit = 1
-    while bit < len(order):
-        place = place ^ jnp.where((mask & bit) != 0, spot_by_key[bit], 0)
-        bit *= 2
-    return place
 
 
 def total_kernel(
     limit,
-    width,
-    scalars,
     mine,
     other,
     grad_mine,
@@ -368,8 +445,9 @@
     first,
     second,
 ):
-    me = scalars[0]
+    me = lax.axis_index("grp").astype(jnp.int32)
     all_rows = mine.shape[0]
+    width = first.shape[0]
     grad = jnp.concatenate(
         [
             grad_mine[:all_rows].astype(F32) + grad_other[all_rows:].astype(F32),
@@ -401,66 +479,119 @@
         )
 
 
+def kernel_call(body, name, out_shape, scratch=(), flops=0, spaces=None, **more):
+    vmem = pl.BlockSpec(memory_space=pltpu.VMEM)
+    in_specs = None if spaces is None else [pl.BlockSpec(memory_space=space) for space in spaces]
+    return pl.pallas_call(
+        body,
+        out_shape=out_shape,
+        in_specs=in_specs,
+        out_specs=jax.tree.map(lambda _: vmem, out_shape),
+        scratch_shapes=scratch,
+        compiler_params=pltpu.CompilerParams(vmem_limit_bytes=20 * 1024 * 1024),
+        cost_estimate=pl.CostEstimate(flops=flops, bytes_accessed=0, transcendentals=0),
+        name=name,
+        **more,
+    )
+
+
 def together(
     features, w_first, w_second, relation_table, heads, relations, tails, negatives, partner
 ):
     rows, width = features.shape
     rounds, edges = heads.shape
     hidden_width, encoded_width = w_second.shape
-    relation_count = relation_table.shape[0]
-    id_rows = jnp.concatenate([heads, tails, relations // LANES, relations % LANES], axis=0)
-    payload = jnp.concatenate([features, id_rows.astype(BF16)], axis=1)
-    table = jnp.pad(relation_table.T, ((0, 0), (0, -relation_count % LANES)))
-    me = lax.axis_index("grp").astype(jnp.int32)
-    mask = lax.dynamic_index_in_dim(partner[:, 0], me, keepdims=False) ^ 0
-    scalars = jnp.stack([me, mask])
-    mine, order = gather_relative(payload, "dom", 4)
-    other = swap(mine, ("grp",), 1)
-    all_rows = 2 * mine.shape[0]
-
-    vmem = pl.BlockSpec(memory_space=pltpu.VMEM)
-    smem = pl.BlockSpec(memory_space=pltpu.SMEM)
-    grad, loss, slope, hidden = pl.pallas_call(
-        functools.partial(score_kernel, (width, rows, rounds, edges), order),
-        out_shape=(
-            jax.ShapeDtypeStruct((all_rows, encoded_width), BF16),
-            jax.ShapeDtypeStruct((1, 2 * edges), F32),
-            jax.ShapeDtypeStruct((all_rows, hidden_width), F32),
-            jax.ShapeDtypeStruct((all_rows, hidden_width), BF16),
+    size = lax.axis_size("dom")
+    keys = keys_of(size)
+    steps = distances_of(size)
+    all_rows = 2 * size * rows
+    shape = jax.ShapeDtypeStruct
+    table = jnp.pad(relation_table.T, ((0, 0), (0, -relation_table.shape[0] % LANES)))
+    picked_shape = shape((size, encoded_width, edges), BF16)
+    flops = 2 * table.size * edges
+
+    block = kernel_call(
+        pack_kernel,
+        "pack",
+        shape((rows, width + edges), BF16),
+        [
+            pltpu.VMEM(features.shape, BF16),
+            pltpu.VMEM((3, rounds, edges), jnp.int32),
+            pltpu.SemaphoreType.DMA((4,)),
+        ],
+        spaces=[pltpu.HBM] * 4,
+    )(features, heads, relations, tails)
+    for step in steps[:-1]:
+        block, _ = join(block, "dom", step)
+    early = block.shape[0] // rows
+    picked = kernel_call(
+        functools.partial(early_kernel, rows, width),
+        "early",
+        picked_shape,
+        [pltpu.VMEM((early * rows, edges), F32)],
+        flops * early,
+        [pltpu.VMEM] * 2,
+    )(block, table)
+    mine, picked = join(block, "dom", steps[-1], picked)
+    picked = kernel_call(
+        functools.partial(late_kernel, rows, width, early),
+        "late",
+        picked_shape,
+        [pltpu.VMEM((size * rows, edges), F32)],
+        flops * (size - early),
+        [pltpu.VMEM, pltpu.VMEM, pltpu.VMEM],
+        input_output_aliases={2: 0},
+    )(mine, table, picked)
+    other = swap(mine, "grp", 1)
+
+    grad, loss, slope, hidden = kernel_call(
+        functools.partial(score_kernel, rows, keys),
+        "scores",
+        (
+            shape((all_rows, encoded_width), BF16),
+            shape((1, 2 * edges), F32),
+            shape((all_rows, hidden_width), F32),
+            shape((all_rows, hidden_width), BF16),
         ),
-        in_specs=[smem] + [vmem] * 6,
-        out_specs=(vmem,) * 4,
-        scratch_shapes=[
+        [
             pltpu.VMEM((all_rows, encoded_width), F32),
             pltpu.VMEM((all_rows, edges), F32),
             pltpu.VMEM((all_rows, encoded_width), F32),
+            pltpu.VMEM(picked_shape.shape, BF16),
+            pltpu.VMEM((size, 2 * rows, 2 * edges), F32),
+            pltpu.VMEM((size, 2 * rows, 2 * edges), BF16),
+            pltpu.SMEM(partner.shape, jnp.int32),
+            pltpu.SemaphoreType.DMA,
         ],
-        compiler_params=pltpu.CompilerParams(vmem_limit_bytes=24 * 1024 * 1024),
-        name="scores",
-    )(scalars, mine, other, w_first, w_second, table, negatives)
-    grad_other = swap(grad, ("grp",), 1)
-    loss_other = swap(loss, ("grp",), 1)
-    limit = math.sqrt(w_first.size + w_second.size)
-    return pl.pallas_call(
-        functools.partial(total_kernel, limit, width),
-        out_shape=(
-            jax.ShapeDtypeStruct((rounds, edges), F32),
-            jax.ShapeDtypeStruct((w_first.shape[0] // 2, w_first.shape[1]), F32),
-            jax.ShapeDtypeStruct((w_second.shape[0] // 2, w_second.shape[1]), F32),
+        flops * size * 2,
+        [pl.ANY] + [pltpu.VMEM] * 7,
+    )(partner, mine, other, w_first, w_second, table, negatives, picked)
+    grad_other = swap(grad, "grp", 1)
+    loss_other = swap(loss, "grp", 1)
+    return kernel_call(
+        functools.partial(total_kernel, math.sqrt(w_first.size + w_second.size)),
+        "totals",
+        (
+            shape((rounds, edges), F32),
+            shape((w_first.shape[0] // 2, w_first.shape[1]), F32),
+            shape((w_second.shape[0] // 2, w_second.shape[1]), F32),
         ),
-        in_specs=[smem] + [vmem] * 9,
-        out_specs=(vmem,) * 3,
-        scratch_shapes=[pltpu.VMEM(w_first.shape, F32), pltpu.VMEM(w_second.shape, F32)],
-        compiler_params=pltpu.CompilerParams(vmem_limit_bytes=24 * 1024 * 1024),
-        name="totals",
-    )(scalars, mine, other, grad, grad_other, slope, hidden, w_second, loss, loss_other)
+        [pltpu.VMEM(w_first.shape, F32), pltpu.VMEM(w_second.shape, F32)],
+        0,
+        [pltpu.VMEM] * 9,
+    )(mine, other, grad, grad_other, slope, hidden, w_second, loss, loss_other)
 
 
 def solution(mesh):
     def per_device(features, w_first, w_second, relation_table, heads, relations, tails, *rest):
         rounds, edges = heads.shape
         rows = features.shape[0]
-        fits = mesh.shape["grp"] == rounds == 2 and edges == LANES and 4 * rounds == rows
+        fits = (
+            mesh.shape["grp"] == rounds == ROUNDS == 2
+            and edges == LANES
+            and 4 * rounds == rows
+            and mesh.shape["dom"] >= 8
+        )
         plan = together if fits else spread
         return plan(features, w_first, w_second, relation_table, heads, relations, tails, *rest)
 

time: 55.1 us -> 35.9 us (0.65)
  Pallas kernels: 26.8 us -> 14.1 us
  other arithmetic: 4.3 us -> 0.01 us
  waiting for transfers between devices: 10.2 us -> 6.04 us
  local copies, waits for them, and re-layouts: 2.91 us -> 4.73 us
    pallas_call x2 -> x5, Pallas kernels: 26.8 us -> 14.1 us  [the longest x1 8.13 us: together(): kernel_call(functools.partial(score_kernel, rows, keys), 'scores', (shape...]
    ppermute x9 -> x8, waiting for transfers between devices: 10.2 us -> 6.04 us  [swap(): lax.ppermute(value, axis, [(i, i ^ distance) for i in range(lax.axis_size...]
    another operation x4 -> x0, other arithmetic: 2.86 us -> none
    unnamed x14 -> x22, local copies, waits for them, and re-layouts: 2.26 us -> 4.61 us
    concatenate x2, other arithmetic: 1.44 us -> 0.01 us  [join(): return (jnp.concatenate([value] + arrived, axis=0), beside)]
    ppermute x9 -> x8, starting transfers between devices: 9.87 us -> 9.95 us  [swap(): lax.ppermute(value, axis, [(i, i ^ distance) for i in range(lax.axis_size...]
  transfers between devices with their start and end apart: 9 -> 8, of which waited for: 5 -> 5; matrix products, arithmetic and copies ran while one was open for 6% -> 5% of each run, Pallas kernels for 0% -> 10%
where the time goes in v2:
time: 35.9 us; the launch traced here: 35.6 us
  Pallas kernels  14.1 us (39%)
  starting transfers between devices  9.95 us (28%)
  waiting for transfers between devices  6.04 us (17%)
  local copies, waits for them, and re-layouts  4.73 us (13%)
  between operations  0.8 us (2%)
    ppermute x8, starting transfers between devices, swap(): lax.ppermute(value, axis, [(i, i ^ distance) for i in range(lax.axis_size...  9.95 us
    pallas_call x1, Pallas kernels, together(): kernel_call(functools.partial(score_kernel, rows, keys), 'scores', (shape...  8.13 us
    ppermute x8, waiting for transfers between devices, swap(): lax.ppermute(value, axis, [(i, i ^ distance) for i in range(lax.axis_size...  6.04 us
    unnamed x22, local copies, waits for them, and re-layouts  4.61 us
    pallas_call x1, Pallas kernels, together(): kernel_call(functools.partial(late_kernel, rows, width, early), 'late', p...  2.63 us
    pallas_call x1, Pallas kernels, together(): kernel_call(functools.partial(total_kernel, math.sqrt(w_first.size + w_se...  2.27 us
    pallas_call x1, Pallas kernels, together(): kernel_call(functools.partial(early_kernel, rows, width), 'early', picked...  1 us
  transfers between devices with their start and end apart: 8, of which 5 were waited for; matrix products, arithmetic and copies ran while one was open for 5% of the time, Pallas kernels for 10%

profile of v2, /device:TPU:0, one launch (start us, length us, event | category | flops | bytes accessed | tf_op | source)
XLA Modules:
  0.0 35.6 jit_solution(2381945738630999899)
XLA Ops:
  0.6 0.0 copy-start.1
  0.6 0.7 %copy-done.1 = bf16[8,768]{1,0:T(8,128)(2,1)S(1)} copy-done((bf16[8,768]{1,0:T(8,128)(2,1)S(1)}, bf16[8,768]{1,0:T(8,128)(2,1)}, u32[]{:S(2)}) %copy-start.1) | copy-done | bytes 12312
  1.3 0.0 copy-start.2
  1.3 0.7 %copy-done.2 = s32[2,128]{1,0:T(2,128)S(1)} copy-done((s32[2,128]{1,0:T(2,128)S(1)}, s32[2,128]{1,0:T(2,128)}, u32[]{:S(2)}) %copy-start.2) | copy-done | bytes 1048
  2.0 0.0 copy-start.3
  2.0 0.7 %copy-done.3 = s32[2,128]{1,0:T(2,128)S(1)} copy-done((s32[2,128]{1,0:T(2,128)S(1)}, s32[2,128]{1,0:T(2,128)}, u32[]{:S(2)}) %copy-start.3) | copy-done | bytes 1048
  2.7 0.0 copy-start.4
  2.7 0.7 %copy-done.4 = s32[2,128]{1,0:T(2,128)S(1)} copy-done((s32[2,128]{1,0:T(2,128)S(1)}, s32[2,128]{1,0:T(2,128)}, u32[]{:S(2)}) %copy-start.4) | copy-done | bytes 1048
  3.4 0.1 pack.1
  3.4 4.1 %collective-permute-start = (bf16[8,896]{1,0:T(8,128)(2,1)S(1)}, bf16[8,896]{1,0:T(8,128)(2,1)S(1)}, u32[]{:S(2)}, u32[]{:S(2)}) collective-permute-start(bf16[8,896]{1,0:T(8,128)(2,1)S(1)} %pack.1), channel_id=1, source_target_pairs={{0,16},{2,18},{4,20},{6,22},{8,24},{10,26},{12,28},{14,30},{16,0},... | collective-permute-start | bytes 43016 | tf_op jit(solution)/shard_map/ppermute | solution.py:179
  7.6 1.8 %copy.13 = bf16[1387,512]{0,1:T(8,128)(2,1)S(1)} copy(bf16[1387,512]{1,0:T(8,128)(2,1)} %param.12) | data formatting | bytes 2840576 | tf_op args[3]
  9.4 0.1 pad.4.table
  9.5 0.0 collective-permute-done
  9.5 1.6 %collective-permute-start.1 = (bf16[16,896]{1,0:T(8,128)(2,1)S(1)}, bf16[16,896]{1,0:T(8,128)(2,1)S(1)}, u32[]{:S(2)}, u32[]{:S(2)}) collective-permute-start(bf16[16,896]{1,0:T(8,128)(2,1)S(1)} %pad_maximum_fusion.1), channel_id=1, source_target_pairs={{0,8},{2,10},{4,12},{6,14},{8,0},{10,2},{12,4},{14,6},{16,24},{18,... | collective-permute-start | bytes 86024 | tf_op jit(solution)/shard_map/ppermute | solution.py:179
  11.2 2.3 %collective-permute-done.1 = bf16[16,896]{1,0:T(8,128)(2,1)S(1)} collective-permute-done((bf16[16,896]{1,0:T(8,128)(2,1)S(1)}, bf16[16,896]{1,0:T(8,128)(2,1)S(1)}, u32[]{:S(2)}, u32[]{:S(2)}) %collective-permute-start.1) | collective-permute-done | bytes 28704 | tf_op jit(solution)/shard_map/ppermute | solution.py:179
  13.4 2.5 %collective-permute-start.4 = (bf16[32,896]{1,0:T(8,128)(2,1)S(1)}, bf16[32,896]{1,0:T(8,128)(2,1)S(1)}, u32[]{:S(2)}, u32[]{:S(2)}) collective-permute-start(bf16[32,896]{1,0:T(8,128)(2,1)S(1)} %pad_maximum_fusion.block), channel_id=1, source_target_pairs={{0,6},{2,4},{4,2},{6,0},{8,14},{10,12},{12,10},{14,8},{16,22},{18,... | collective-permute-start | bytes 172040 | tf_op jit(solution)/shard_map/ppermute | solution.py:179
  15.9 0.5 %collective-permute-start.3 = (bf16[32,896]{1,0:T(8,128)(2,1)S(1)}, bf16[32,896]{1,0:T(8,128)(2,1)S(1)}, u32[]{:S(2)}, u32[]{:S(2)}) collective-permute-start(bf16[32,896]{1,0:T(8,128)(2,1)S(1)} %pad_maximum_fusion.block), channel_id=1, source_target_pairs={{0,4},{2,6},{4,0},{6,2},{8,12},{10,14},{12,8},{14,10},{16,20},{18,... | collective-permute-start | bytes 172040 | tf_op jit(solution)/shard_map/ppermute | solution.py:179
  16.4 0.5 %collective-permute-start.2 = (bf16[32,896]{1,0:T(8,128)(2,1)S(1)}, bf16[32,896]{1,0:T(8,128)(2,1)S(1)}, u32[]{:S(2)}, u32[]{:S(2)}) collective-permute-start(bf16[32,896]{1,0:T(8,128)(2,1)S(1)} %pad_maximum_fusion.block), channel_id=1, source_target_pairs={{0,2},{2,0},{4,6},{6,4},{8,10},{10,8},{12,14},{14,12},{16,18},{18,... | collective-permute-start | bytes 172040 | tf_op jit(solution)/shard_map/ppermute | solution.py:179
  16.9 1.0 %early.1.begun = bf16[16,512,128]{2,1,0:T(8,128)(2,1)S(1)} custom-call(bf16[32,896]{1,0:T(8,128)(2,1)S(1)} %pad_maximum_fusion.block, bf16[512,1408]{1,0:T(8,128)(2,1)S(1)} %pad.4.table), custom_call_target="tpu_custom_call" | custom-call | flops 738197504 | tf_op jit(solution)/shard_map/early/pallas_call | solution.py:527
  18.0 1.1 %collective-permute-done.4 = bf16[32,896]{1,0:T(8,128)(2,1)S(1)} collective-permute-done((bf16[32,896]{1,0:T(8,128)(2,1)S(1)}, bf16[32,896]{1,0:T(8,128)(2,1)S(1)}, u32[]{:S(2)}, u32[]{:S(2)}) %collective-permute-start.4) | collective-permute-done | bytes 57376 | tf_op jit(solution)/shard_map/ppermute | solution.py:179
  19.0 1.1 %collective-permute-done.3 = bf16[32,896]{1,0:T(8,128)(2,1)S(1)} collective-permute-done((bf16[32,896]{1,0:T(8,128)(2,1)S(1)}, bf16[32,896]{1,0:T(8,128)(2,1)S(1)}, u32[]{:S(2)}, u32[]{:S(2)}) %collective-permute-start.3) | collective-permute-done | bytes 57376 | tf_op jit(solution)/shard_map/ppermute | solution.py:179
  20.1 0.5 %collective-permute-done.2 = bf16[32,896]{1,0:T(8,128)(2,1)S(1)} collective-permute-done((bf16[32,896]{1,0:T(8,128)(2,1)S(1)}, bf16[32,896]{1,0:T(8,128)(2,1)S(1)}, u32[]{:S(2)}, u32[]{:S(2)}) %collective-permute-start.2) | collective-permute-done | bytes 57376 | tf_op jit(solution)/shard_map/ppermute | solution.py:179
  20.7 0.0 copy-start
  20.7 0.0 copy-start.5
  20.7 0.0 copy-start.6
  20.7 0.0 copy-start.7
  20.7 0.1 collective-permute-start.5
  20.8 2.6 %late.1.picked_mine = bf16[16,512,128]{2,1,0:T(8,128)(2,1)S(1)} custom-call(bf16[128,896]{1,0:T(8,128)(2,1)S(1)} %constant_dynamic-update-slice_fusion.block.mine, bf16[512,1408]{1,0:T(8,128)(2,1)S(1)} %pad.4.table, bf16[16,512,128]{2,1,0:T(8,128)(2,1)S(1)} %early.1.begun), custom_call_target="tpu_custom_call", output_to_operand_aliasing={{}: (2, {})} | custom-call | flops 2214592512 | tf_op jit(solution)/shard_map/late/pallas_call | solution.py:536
  23.4 0.0 collective-permute-done.5.other
  23.4 0.0 copy-done
  23.4 0.0 copy-done.5
  23.5 0.0 copy-done.6
  23.5 0.0 copy-done.7
  23.5 8.1 %scores.1 = (bf16[256,512]{1,0:T(8,128)(2,1)S(1)}, f32[1,256]{1,0:T(1,128)S(1)}, f32[256,512]{1,0:T(8,128)S(1)}, bf16[256,512]{1,0:T(8,128)(2,1)S(1)}) custom-call(s32[2,16]{1,0:T(2,128)S(1)} %copy-done.7, bf16[128,896]{1,0:T(8,128)(2,1)S(1)} %constant_dynamic-update-slice_fusion.block.mine, bf16[128,896]{1,0:T(8,128)(2,1)S(1)} %collective-permute-done.5.other, ...), custom_call_target="tpu_custom_call" | custom-call | flops 5905580032 | tf_op jit(solution)/shard_map/scores/pallas_call | solution.py:547
  31.6 0.6 %collective-permute-start.6 = (bf16[256,512]{1,0:T(8,128)(2,1)S(1)}, bf16[256,512]{1,0:T(8,128)(2,1)S(1)}, u32[]{:S(2)}, u32[]{:S(2)}) collective-permute-start(bf16[256,512]{1,0:T(8,128)(2,1)S(1)} %get-tuple-element.15.grad_mine), channel_id=1, source_target_pairs={{0,1},{1,0},{2,3},{3,2},{4,5},{5,4},{6,7},{7,6},{8,9},{9,8},{10,11... | collective-permute-start | bytes 786440 | tf_op jit(solution)/shard_map/ppermute | solution.py:179
  32.2 0.1 collective-permute-start.7
  32.3 1.1 %collective-permute-done.7.loss_other = f32[1,256]{1,0:T(1,128)S(1)} collective-permute-done((f32[1,256]{1,0:T(1,128)S(1)}, f32[1,256]{1,0:T(1,128)S(1)}, u32[]{:S(2)}, u32[]{:S(2)}) %collective-permute-start.7) | collective-permute-done | bytes 1056 | tf_op jit(solution)/shard_map/ppermute | solution.py:179
  33.3 0.0 collective-permute-done.6.grad_other
  33.3 2.3 %totals.1 = (f32[2,128]{1,0:T(2,128)}, f32[384,512]{1,0:T(8,128)}, f32[256,512]{1,0:T(8,128)}) custom-call(bf16[128,896]{1,0:T(8,128)(2,1)S(1)} %constant_dynamic-update-slice_fusion.block.mine, bf16[128,896]{1,0:T(8,128)(2,1)S(1)} %collective-permute-done.5.other, bf16[256,512]{1,0:T(8,128)(2,1)S(1)} %get-tuple-element.15.grad_mine, ...), custom_call_target="tpu_custom_call" | custom-call | tf_op jit(solution)/shard_map/totals/pallas_call | solution.py:571
  (8 shorter events, 0.1 us)
Async XLA Ops:
  0.6 0.7 %copy-start.1 = (bf16[8,768]{1,0:T(8,128)(2,1)S(1)}, bf16[8,768]{1,0:T(8,128)(2,1)}, u32[]{:S(2)}) copy-start(bf16[8,768]{1,0:T(8,128)(2,1)} %features.1) | copy-start | bytes 36868
  1.3 0.7 %copy-start.2 = (s32[2,128]{1,0:T(2,128)S(1)}, s32[2,128]{1,0:T(2,128)}, u32[]{:S(2)}) copy-start(s32[2,128]{1,0:T(2,128)} %heads.1) | copy-start | bytes 3076
  2.0 0.7 %copy-start.3 = (s32[2,128]{1,0:T(2,128)S(1)}, s32[2,128]{1,0:T(2,128)}, u32[]{:S(2)}) copy-start(s32[2,128]{1,0:T(2,128)} %relations.1) | copy-start | bytes 3076
  2.7 0.7 %copy-start.4 = (s32[2,128]{1,0:T(2,128)S(1)}, s32[2,128]{1,0:T(2,128)}, u32[]{:S(2)}) copy-start(s32[2,128]{1,0:T(2,128)} %tails.1) | copy-start | bytes 3076
  3.4 6.0 %collective-permute-start = (bf16[8,896]{1,0:T(8,128)(2,1)S(1)}, bf16[8,896]{1,0:T(8,128)(2,1)S(1)}, u32[]{:S(2)}, u32[]{:S(2)}) collective-permute-start(bf16[8,896]{1,0:T(8,128)(2,1)S(1)} %pack.1), channel_id=1, source_target_pairs={{0,16},{2,18},{4,20},{6,22},{8,24},{10,26},{12,28},{14,30},{16,0},... | collective-permute-start | bytes 43016 | tf_op jit(solution)/shard_map/ppermute | solution.py:179
  9.5 3.9 %collective-permute-start.1 = (bf16[16,896]{1,0:T(8,128)(2,1)S(1)}, bf16[16,896]{1,0:T(8,128)(2,1)S(1)}, u32[]{:S(2)}, u32[]{:S(2)}) collective-permute-start(bf16[16,896]{1,0:T(8,128)(2,1)S(1)} %pad_maximum_fusion.1), channel_id=1, source_target_pairs={{0,8},{2,10},{4,12},{6,14},{8,0},{10,2},{12,4},{14,6},{16,24},{18,... | collective-permute-start | bytes 86024 | tf_op jit(solution)/shard_map/ppermute | solution.py:179
  13.4 5.6 %collective-permute-start.4 = (bf16[32,896]{1,0:T(8,128)(2,1)S(1)}, bf16[32,896]{1,0:T(8,128)(2,1)S(1)}, u32[]{:S(2)}, u32[]{:S(2)}) collective-permute-start(bf16[32,896]{1,0:T(8,128)(2,1)S(1)} %pad_maximum_fusion.block), channel_id=1, source_target_pairs={{0,6},{2,4},{4,2},{6,0},{8,14},{10,12},{12,10},{14,8},{16,22},{18,... | collective-permute-start | bytes 172040 | tf_op jit(solution)/shard_map/ppermute | solution.py:179
  15.9 4.2 %collective-permute-start.3 = (bf16[32,896]{1,0:T(8,128)(2,1)S(1)}, bf16[32,896]{1,0:T(8,128)(2,1)S(1)}, u32[]{:S(2)}, u32[]{:S(2)}) collective-permute-start(bf16[32,896]{1,0:T(8,128)(2,1)S(1)} %pad_maximum_fusion.block), channel_id=1, source_target_pairs={{0,4},{2,6},{4,0},{6,2},{8,12},{10,14},{12,8},{14,10},{16,20},{18,... | collective-permute-start | bytes 172040 | tf_op jit(solution)/shard_map/ppermute | solution.py:179
  16.4 4.2 %collective-permute-start.2 = (bf16[32,896]{1,0:T(8,128)(2,1)S(1)}, bf16[32,896]{1,0:T(8,128)(2,1)S(1)}, u32[]{:S(2)}, u32[]{:S(2)}) collective-permute-start(bf16[32,896]{1,0:T(8,128)(2,1)S(1)} %pad_maximum_fusion.block), channel_id=1, source_target_pairs={{0,2},{2,0},{4,6},{6,4},{8,10},{10,8},{12,14},{14,12},{16,18},{18,... | collective-permute-start | bytes 172040 | tf_op jit(solution)/shard_map/ppermute | solution.py:179
  20.7 2.8 %copy-start = (bf16[512,512]{1,0:T(8,128)(2,1)S(1)}, bf16[512,512]{1,0:T(8,128)(2,1)}, u32[]{:S(2)}) copy-start(bf16[512,512]{1,0:T(8,128)(2,1)} %w_second.3) | copy-start | bytes 1572868
  20.7 2.8 %copy-start.5 = (bf16[768,512]{1,0:T(8,128)(2,1)S(1)}, bf16[768,512]{1,0:T(8,128)(2,1)}, u32[]{:S(2)}) copy-start(bf16[768,512]{1,0:T(8,128)(2,1)} %w_first.1) | copy-start | bytes 2359300
  20.7 2.8 %copy-start.6 = (s32[2,512]{1,0:T(2,128)S(1)}, s32[2,512]{1,0:T(2,128)}, u32[]{:S(2)}) copy-start(s32[2,512]{1,0:T(2,128)} %negatives.1) | copy-start | bytes 12292
  20.7 2.8 %copy-start.7 = (s32[2,16]{1,0:T(2,128)S(1)}, s32[2,16]{1,0:T(2,128)}, u32[]{:S(2)}) copy-start(s32[2,16]{1,0:T(2,128)} %partner.1) | copy-start | bytes 388
  20.7 2.7 %collective-permute-start.5 = (bf16[128,896]{1,0:T(8,128)(2,1)S(1)}, bf16[128,896]{1,0:T(8,128)(2,1)S(1)}, u32[]{:S(2)}, u32[]{:S(2)}) collective-permute-start(bf16[128,896]{1,0:T(8,128)(2,1)S(1)} %constant_dynamic-update-slice_fusion.block.mine), channel_id=1, source_target_pairs={{0,1},{1,0},{2,3},{3,2},{4,5},{5,4},{6,7},{7,6},{8,9},{9,8},{10,11... | collective-permute-start | bytes 688136 | tf_op jit(solution)/shard_map/ppermute | solution.py:179
  31.6 1.7 %collective-permute-start.6 = (bf16[256,512]{1,0:T(8,128)(2,1)S(1)}, bf16[256,512]{1,0:T(8,128)(2,1)S(1)}, u32[]{:S(2)}, u32[]{:S(2)}) collective-permute-start(bf16[256,512]{1,0:T(8,128)(2,1)S(1)} %get-tuple-element.15.grad_mine), channel_id=1, source_target_pairs={{0,1},{1,0},{2,3},{3,2},{4,5},{5,4},{6,7},{7,6},{8,9},{9,8},{10,11... | collective-permute-start | bytes 786440 | tf_op jit(solution)/shard_map/ppermute | solution.py:179
  32.2 1.2 %collective-permute-start.7 = (f32[1,256]{1,0:T(1,128)S(1)}, f32[1,256]{1,0:T(1,128)S(1)}, u32[]{:S(2)}, u32[]{:S(2)}) collective-permute-start(f32[1,256]{1,0:T(1,128)S(1)} %get-tuple-element.18.loss_mine), channel_id=1, source_target_pairs={{0,1},{1,0},{2,3},{3,2},{4,5},{5,4},{6,7},{7,6},{8,9},{9,8},{10,11... | collective-permute-start | bytes 3080 | tf_op jit(solution)/shard_map/ppermute | solution.py:179

commit v3 on v2

--- a/solution.py
+++ b/solution.py
@@ -181,18 +181,17 @@
 
 def distances_of(size):
     steps = []
-    while size > 4:
-        size //= 2
-        steps.append([size])
-    return steps + [list(range(size - 1, 0, -1))]
-
-
-def join(value, axis, step, beside=None):
+    while size > 1:
+        radix = min(size, 4)
+        size //= radix
+        steps.append([i * size for i in range(radix - 1, 0, -1)])
+    return steps
+
+
+def join(value, axis, step, beside):
     arrived = [swap(value, axis, distance) for distance in step]
-    if beside is not None:
-        *arrived, beside = lax.optimization_barrier((*arrived[::-1], beside))
-        arrived = arrived[::-1]
-    return jnp.concatenate([value] + arrived, axis=0), beside
+    *arrived, beside = lax.optimization_barrier((*arrived[::-1], beside))
+    return jnp.concatenate([value] + arrived[::-1], axis=0), beside
 
 
 def keys_of(size):
@@ -214,21 +213,24 @@
     return ids[pl.ds(place * rows + kind * ROUNDS + me, 1), :]
 
 
-def pick_relations(ids, places, me, rows, table, picked):
+def pick_relations(low, high, table):
     low_column = lax.broadcasted_iota(jnp.int32, (LANES, 1), 0).astype(F32)
+    low_hot = (low == low_column).astype(BF16)
+    hot = jnp.concatenate(
+        [low_hot * (high == float(block)).astype(BF16) for block in range(table.shape[1] // LANES)],
+        axis=0,
+    )
+    columns = jnp.dot(table[...], hot, preferred_element_type=F32).astype(BF16)
+    return columns[:, :LANES], columns[:, LANES:]
+
+
+def pick_blocks(ids, places, me, rows, table, picked):
     for first in range(places.start, places.stop, 2):
         low, high = [
             jnp.concatenate([id_row(ids, kind, place, me, rows) for place in (first, first + 1)], axis=1)
             for kind in (LOW, HIGH)
         ]
-        low_hot = (low == low_column).astype(BF16)
-        hot = jnp.concatenate(
-            [low_hot * (high == float(block)).astype(BF16) for block in range(table.shape[1] // LANES)],
-            axis=0,
-        )
-        columns = jnp.dot(table[...], hot, preferred_element_type=F32).astype(BF16)
-        picked[first] = columns[:, :LANES]
-        picked[first + 1] = columns[:, LANES:]
+        picked[first], picked[first + 1] = pick_relations(low, high, table)
 
 
 def pack_kernel(features, heads, relations, tails, packed, rows, ids, sems):
@@ -248,17 +250,23 @@
     packed[:, width:] = jnp.concatenate(columns, axis=0).astype(F32).astype(BF16)
 
 
-def early_kernel(rows, width, block, table, picked, ids):
+def early_kernel(rows, width, block, other_ids, table, picked, picked_other, ids, ids_other):
     ids[...] = block[:, width:].astype(F32)
+    ids_other[...] = other_ids[...].astype(F32)
     me = lax.axis_index("grp").astype(jnp.int32)
-    pick_relations(ids, range(block.shape[0] // rows), me, rows, table, picked)
+    for place in range(block.shape[0] // rows):
+        low, high = [
+            jnp.concatenate([id_row(member, kind, place, me, rows) for member in (ids, ids_other)], axis=1)
+            for kind in (LOW, HIGH)
+        ]
+        picked[place], picked_other[place] = pick_relations(low, high, table)
 
 
 def late_kernel(rows, width, skipped, block, table, begun, picked, ids):
     del begun
     ids[...] = block[:, width:].astype(F32)
     me = lax.axis_index("grp").astype(jnp.int32)
-    pick_relations(ids, range(skipped, block.shape[0] // rows), me, rows, table, picked)
+    pick_blocks(ids, range(skipped, block.shape[0] // rows), me, rows, table, picked)
 
 
 def sigmoid_parts(value):
@@ -279,6 +287,7 @@
     table,
     negatives,
     picked_mine,
+    picked_early,
     grad_out,
     loss_out,
     slope_out,
@@ -311,7 +320,9 @@
     slope_out[...] = gate * (1.0 + pre_act * (1.0 - gate))
     hidden_out[...] = hidden
     encoded[...] = jnp.dot(hidden, w_second[...], preferred_element_type=F32).astype(BF16).astype(F32)
-    pick_relations(ids.at[pl.ds(all_rows, all_rows)], range(places), me, rows, table, picked_other)
+    early = picked_early.shape[0]
+    picked_other[:early] = picked_early[...]
+    pick_blocks(ids.at[pl.ds(all_rows, all_rows)], range(early, places), me, rows, table, picked_other)
 
     labels = [(i ^ (me * rows)).astype(F32) for i in range(group_rows)]
     label_column = lax.broadcasted_iota(jnp.int32, (group_rows, 1), 0) ^ (me * rows)
@@ -479,7 +490,7 @@
         )
 
 
-def kernel_call(body, name, out_shape, scratch=(), flops=0, spaces=None, **more):
+def kernel_call(body, name, out_shape, scratch=(), flops=0, spaces=None, mebibytes=20, **more):
     vmem = pl.BlockSpec(memory_space=pltpu.VMEM)
     in_specs = None if spaces is None else [pl.BlockSpec(memory_space=space) for space in spaces]
     return pl.pallas_call(
@@ -488,7 +499,7 @@
         in_specs=in_specs,
         out_specs=jax.tree.map(lambda _: vmem, out_shape),
         scratch_shapes=scratch,
-        compiler_params=pltpu.CompilerParams(vmem_limit_bytes=20 * 1024 * 1024),
+        compiler_params=pltpu.CompilerParams(vmem_limit_bytes=mebibytes * 1024 * 1024),
         cost_estimate=pl.CostEstimate(flops=flops, bytes_accessed=0, transcendentals=0),
         name=name,
         **more,
@@ -520,18 +531,20 @@
             pltpu.SemaphoreType.DMA((4,)),
         ],
         spaces=[pltpu.HBM] * 4,
+        mebibytes=60,
     )(features, heads, relations, tails)
     for step in steps[:-1]:
-        block, _ = join(block, "dom", step)
+        block, table = join(block, "dom", step, table)
     early = block.shape[0] // rows
-    picked = kernel_call(
+    early_ids = swap(block[:, width:], "grp", 1)
+    picked, picked_early = kernel_call(
         functools.partial(early_kernel, rows, width),
         "early",
-        picked_shape,
-        [pltpu.VMEM((early * rows, edges), F32)],
-        flops * early,
-        [pltpu.VMEM] * 2,
-    )(block, table)
+        (picked_shape, shape((early, encoded_width, edges), BF16)),
+        [pltpu.VMEM((early * rows, edges), F32)] * 2,
+        flops * early * 2,
+        [pltpu.VMEM] * 3,
+    )(block, early_ids, table)
     mine, picked = join(block, "dom", steps[-1], picked)
     picked = kernel_call(
         functools.partial(late_kernel, rows, width, early),
@@ -564,8 +577,8 @@
             pltpu.SemaphoreType.DMA,
         ],
         flops * size * 2,
-        [pl.ANY] + [pltpu.VMEM] * 7,
-    )(partner, mine, other, w_first, w_second, table, negatives, picked)
+        [pl.ANY] + [pltpu.VMEM] * 8,
+    )(partner, mine, other, w_first, w_second, table, negatives, picked, picked_early)
     grad_other = swap(grad, "grp", 1)
     loss_other = swap(loss, "grp", 1)
     return kernel_call(

time: 35.9 us -> 33.6 us (0.936)
  local copies, waits for them, and re-layouts: 4.73 us -> 2.76 us
  waiting for transfers between devices: 6.04 us -> 4.36 us
  Pallas kernels: 14.1 us -> 15.3 us
    unnamed x22 -> x17, local copies, waits for them, and re-layouts: 4.61 us -> 2.63 us
    ppermute x8 -> x10, waiting for transfers between devices: 6.04 us -> 4.36 us  [swap(): lax.ppermute(value, axis, [(i, i ^ distance) for i in range(lax.axis_size...]
    pallas_call x1, Pallas kernels: 0.06 us -> 1.37 us  [together(): kernel_call(pack_kernel, 'pack', shape((rows, width + edges), BF16), [plt...]
    pallas_call x1, Pallas kernels: 8.13 us -> 7.21 us  [together(): kernel_call(functools.partial(score_kernel, rows, keys), 'scores', (shape...]
    pallas_call x1, Pallas kernels: 1 us -> 1.81 us  [together(): kernel_call(functools.partial(early_kernel, rows, width), 'early', (picke...]
    ppermute x8 -> x10, starting transfers between devices: 9.95 us -> 10 us  [swap(): lax.ppermute(value, axis, [(i, i ^ distance) for i in range(lax.axis_size...]
  transfers between devices with their start and end apart: 8 -> 10, of which waited for: 5 -> 5; matrix products, arithmetic and copies ran while one was open for 5% -> 8% of each run, Pallas kernels for 10% -> 13%
where the time goes in v3:
time: 33.6 us; the launch traced here: 33.2 us
  Pallas kernels  15.3 us (46%)
  starting transfers between devices  10 us (30%)
  waiting for transfers between devices  4.36 us (13%)
  local copies, waits for them, and re-layouts  2.76 us (8%)
  between operations  0.81 us (2%)
    ppermute x10, starting transfers between devices, swap(): lax.ppermute(value, axis, [(i, i ^ distance) for i in range(lax.axis_size...  10 us
    pallas_call x1, Pallas kernels, together(): kernel_call(functools.partial(score_kernel, rows, keys), 'scores', (shape...  7.21 us
    ppermute x10, waiting for transfers between devices, swap(): lax.ppermute(value, axis, [(i, i ^ distance) for i in range(lax.axis_size...  4.36 us
    unnamed x17, local copies, waits for them, and re-layouts  2.63 us
    pallas_call x1, Pallas kernels, together(): kernel_call(functools.partial(late_kernel, rows, width, early), 'late', p...  2.62 us
    pallas_call x1, Pallas kernels, together(): kernel_call(functools.partial(total_kernel, math.sqrt(w_first.size + w_se...  2.25 us
    pallas_call x1, Pallas kernels, together(): kernel_call(functools.partial(early_kernel, rows, width), 'early', (picke...  1.81 us
    pallas_call x1, Pallas kernels, together(): kernel_call(pack_kernel, 'pack', shape((rows, width + edges), BF16), [plt...  1.37 us
  transfers between devices with their start and end apart: 10, of which 5 were waited for; matrix products, arithmetic and copies ran while one was open for 8% of the time, Pallas kernels for 13%

profile of v3, /device:TPU:0, one launch (start us, length us, event | category | flops | bytes accessed | tf_op | source)
XLA Modules:
  0.0 33.2 jit_solution(714092559986748089)
XLA Ops:
  0.6 1.4 %pack.1 = bf16[8,896]{1,0:T(8,128)(2,1)} custom-call(bf16[8,768]{1,0:T(8,128)(2,1)} %features.1, s32[2,128]{1,0:T(2,128)} %heads.1, s32[2,128]{1,0:T(2,128)} %relations.1, s32[2,128]{1,0:T(2,128)} %tails.1), custom_call_target="tpu_custom_call" | custom-call | tf_op jit(solution)/shard_map/pack/pallas_call | solution.py:524
  2.0 5.1 %collective-permute-start.2 = (bf16[8,896]{1,0:T(8,128)(2,1)}, bf16[8,896]{1,0:T(8,128)(2,1)S(1)}, u32[]{:S(2)}, u32[]{:S(2)}) collective-permute-start(bf16[8,896]{1,0:T(8,128)(2,1)} %pack.1), channel_id=1, source_target_pairs={{0,24},{2,26},{4,28},{6,30},{8,16},{10,18},{12,20},{14,22},{16,8},... | collective-permute-start | bytes 43016 | tf_op jit(solution)/shard_map/ppermute | solution.py:179
  7.1 0.0 collective-permute-start.1
  7.1 0.6 %collective-permute-start = (bf16[8,896]{1,0:T(8,128)(2,1)}, bf16[8,896]{1,0:T(8,128)(2,1)S(1)}, u32[]{:S(2)}, u32[]{:S(2)}) collective-permute-start(bf16[8,896]{1,0:T(8,128)(2,1)} %pack.1), channel_id=1, source_target_pairs={{0,8},{2,10},{4,12},{6,14},{8,0},{10,2},{12,4},{14,6},{16,24},{18,... | collective-permute-start | bytes 43016 | tf_op jit(solution)/shard_map/ppermute | solution.py:179
  7.8 0.7 %constant_dynamic-update-slice_fusion.6 = bf16[128,896]{1,0:T(8,128)(2,1)S(1)} fusion(bf16[8,896]{1,0:T(8,128)(2,1)} %pack.1), kind=kLoop, calls=%fused_computation.7 | loop fusion | bytes 28672
  8.5 1.8 %copy.13 = bf16[1387,512]{0,1:T(8,128)(2,1)S(1)} copy(bf16[1387,512]{1,0:T(8,128)(2,1)} %param.12) | data formatting | bytes 2840576 | tf_op args[3]
  10.3 0.0 copy-start.4
  10.3 0.1 pad.4.table
  10.5 0.0 collective-permute-done.2
  10.5 1.5 %collective-permute-done.1 = bf16[8,896]{1,0:T(8,128)(2,1)S(1)} collective-permute-done((bf16[8,896]{1,0:T(8,128)(2,1)}, bf16[8,896]{1,0:T(8,128)(2,1)S(1)}, u32[]{:S(2)}, u32[]{:S(2)}) %collective-permute-start.1) | collective-permute-done | bytes 14368 | tf_op jit(solution)/shard_map/ppermute | solution.py:179
  12.0 0.0 collective-permute-done
  12.0 0.0 copy-done.4
  12.0 2.5 %collective-permute-start.5 = (bf16[32,896]{1,0:T(8,128)(2,1)S(1)}, bf16[32,896]{1,0:T(8,128)(2,1)S(1)}, u32[]{:S(2)}, u32[]{:S(2)}) collective-permute-start(bf16[32,896]{1,0:T(8,128)(2,1)S(1)} %pad_maximum_fusion.block), channel_id=1, source_target_pairs={{0,6},{2,4},{4,2},{6,0},{8,14},{10,12},{12,10},{14,8},{16,22},{18,... | collective-permute-start | bytes 172040 | tf_op jit(solution)/shard_map/ppermute | solution.py:179
  14.5 0.5 %collective-permute-start.4 = (bf16[32,896]{1,0:T(8,128)(2,1)S(1)}, bf16[32,896]{1,0:T(8,128)(2,1)S(1)}, u32[]{:S(2)}, u32[]{:S(2)}) collective-permute-start(bf16[32,896]{1,0:T(8,128)(2,1)S(1)} %pad_maximum_fusion.block), channel_id=1, source_target_pairs={{0,4},{2,6},{4,0},{6,2},{8,12},{10,14},{12,8},{14,10},{16,20},{18,... | collective-permute-start | bytes 172040 | tf_op jit(solution)/shard_map/ppermute | solution.py:179
  15.0 0.5 %collective-permute-start.3 = (bf16[32,896]{1,0:T(8,128)(2,1)S(1)}, bf16[32,896]{1,0:T(8,128)(2,1)S(1)}, u32[]{:S(2)}, u32[]{:S(2)}) collective-permute-start(bf16[32,896]{1,0:T(8,128)(2,1)S(1)} %pad_maximum_fusion.block), channel_id=1, source_target_pairs={{0,2},{2,0},{4,6},{6,4},{8,10},{10,8},{12,14},{14,12},{16,18},{18,... | collective-permute-start | bytes 172040 | tf_op jit(solution)/shard_map/ppermute | solution.py:179
  15.6 0.0 collective-permute-start.6
  15.6 1.2 %collective-permute-done.6.other_ids = bf16[32,128]{1,0:T(8,128)(2,1)S(1)} collective-permute-done((bf16[32,128]{1,0:T(8,128)(2,1)S(1)}, bf16[32,128]{1,0:T(8,128)(2,1)S(1)}, u32[]{:S(2)}, u32[]{:S(2)}) %collective-permute-start.6) | collective-permute-done | bytes 8224 | tf_op jit(solution)/shard_map/ppermute | solution.py:179
  16.7 1.8 %early.1 = (bf16[16,512,128]{2,1,0:T(8,128)(2,1)S(1)}, bf16[4,512,128]{2,1,0:T(8,128)(2,1)S(1)}) custom-call(bf16[32,896]{1,0:T(8,128)(2,1)S(1)} %pad_maximum_fusion.block, bf16[32,128]{1,0:T(8,128)(2,1)S(1)} %collective-permute-done.6.other_ids, bf16[512,1408]{1,0:T(8,128)(2,1)S(1)} %pad.4.table), custom_call_target="tpu_custom_call" | custom-call | flops 1476395008 | tf_op jit(solution)/shard_map/early/pallas_call | solution.py:540
  18.5 0.0 collective-permute-done.5
  18.6 0.1 collective-permute-done.4
  18.7 0.5 %collective-permute-done.3 = bf16[32,896]{1,0:T(8,128)(2,1)S(1)} collective-permute-done((bf16[32,896]{1,0:T(8,128)(2,1)S(1)}, bf16[32,896]{1,0:T(8,128)(2,1)S(1)}, u32[]{:S(2)}, u32[]{:S(2)}) %collective-permute-start.3) | collective-permute-done | bytes 57376 | tf_op jit(solution)/shard_map/ppermute | solution.py:179
  19.2 0.0 copy-start
  19.2 0.0 copy-start.1
  19.2 0.0 copy-start.2
  19.3 0.0 copy-start.3
  19.3 0.1 collective-permute-start.7
  19.3 2.6 %late.1.picked_mine = bf16[16,512,128]{2,1,0:T(8,128)(2,1)S(1)} custom-call(bf16[128,896]{1,0:T(8,128)(2,1)S(1)} %constant_dynamic-update-slice_fusion.block.mine, bf16[512,1408]{1,0:T(8,128)(2,1)S(1)} %pad.4.table, bf16[16,512,128]{2,1,0:T(8,128)(2,1)S(1)} %get-tuple-element.25.begun), custom_call_target="tpu_custom_call", output_to_operand_aliasing={{}: (2, {})} | custom-call | flops 2214592512 | tf_op jit(solution)/shard_map/late/pallas_call | solution.py:549
  22.0 0.0 collective-permute-done.7.other
  22.0 0.0 copy-done
  22.0 0.0 copy-done.1
  22.0 0.0 copy-done.2
  22.0 0.0 copy-done.3
  22.0 7.2 %scores.1 = (bf16[256,512]{1,0:T(8,128)(2,1)S(1)}, f32[1,256]{1,0:T(1,128)S(1)}, f32[256,512]{1,0:T(8,128)S(1)}, bf16[256,512]{1,0:T(8,128)(2,1)S(1)}) custom-call(s32[2,16]{1,0:T(2,128)S(1)} %copy-done.3, bf16[128,896]{1,0:T(8,128)(2,1)S(1)} %constant_dynamic-update-slice_fusion.block.mine, bf16[128,896]{1,0:T(8,128)(2,1)S(1)} %collective-permute-done.7.other, ...), custom_call_target="tpu_custom_call" | custom-call | flops 5905580032 | tf_op jit(solution)/shard_map/scores/pallas_call | solution.py:560
  29.3 0.6 %collective-permute-start.8 = (bf16[256,512]{1,0:T(8,128)(2,1)S(1)}, bf16[256,512]{1,0:T(8,128)(2,1)S(1)}, u32[]{:S(2)}, u32[]{:S(2)}) collective-permute-start(bf16[256,512]{1,0:T(8,128)(2,1)S(1)} %get-tuple-element.27.grad_mine), channel_id=1, source_target_pairs={{0,1},{1,0},{2,3},{3,2},{4,5},{5,4},{6,7},{7,6},{8,9},{9,8},{10,11... | collective-permute-start | bytes 786440 | tf_op jit(solution)/shard_map/ppermute | solution.py:179
  29.8 0.1 collective-permute-start.9
  29.9 1.1 %collective-permute-done.9.loss_other = f32[1,256]{1,0:T(1,128)S(1)} collective-permute-done((f32[1,256]{1,0:T(1,128)S(1)}, f32[1,256]{1,0:T(1,128)S(1)}, u32[]{:S(2)}, u32[]{:S(2)}) %collective-permute-start.9) | collective-permute-done | bytes 1056 | tf_op jit(solution)/shard_map/ppermute | solution.py:179
  31.0 0.0 collective-permute-done.8.grad_other
  31.0 2.3 %totals.1 = (f32[2,128]{1,0:T(2,128)}, f32[384,512]{1,0:T(8,128)}, f32[256,512]{1,0:T(8,128)}) custom-call(bf16[128,896]{1,0:T(8,128)(2,1)S(1)} %constant_dynamic-update-slice_fusion.block.mine, bf16[128,896]{1,0:T(8,128)(2,1)S(1)} %collective-permute-done.7.other, bf16[256,512]{1,0:T(8,128)(2,1)S(1)} %get-tuple-element.27.grad_mine, ...), custom_call_target="tpu_custom_call" | custom-call | tf_op jit(solution)/shard_map/totals/pallas_call | solution.py:584
  (8 shorter events, 0.1 us)
Async XLA Ops:
  2.0 8.5 %collective-permute-start.2 = (bf16[8,896]{1,0:T(8,128)(2,1)}, bf16[8,896]{1,0:T(8,128)(2,1)S(1)}, u32[]{:S(2)}, u32[]{:S(2)}) collective-permute-start(bf16[8,896]{1,0:T(8,128)(2,1)} %pack.1), channel_id=1, source_target_pairs={{0,24},{2,26},{4,28},{6,30},{8,16},{10,18},{12,20},{14,22},{16,8},... | collective-permute-start | bytes 43016 | tf_op jit(solution)/shard_map/ppermute | solution.py:179
  7.1 4.8 %collective-permute-start.1 = (bf16[8,896]{1,0:T(8,128)(2,1)}, bf16[8,896]{1,0:T(8,128)(2,1)S(1)}, u32[]{:S(2)}, u32[]{:S(2)}) collective-permute-start(bf16[8,896]{1,0:T(8,128)(2,1)} %pack.1), channel_id=1, source_target_pairs={{0,16},{2,18},{4,20},{6,22},{8,24},{10,26},{12,28},{14,30},{16,0},... | collective-permute-start | bytes 43016 | tf_op jit(solution)/shard_map/ppermute | solution.py:179
  7.1 4.8 %collective-permute-start = (bf16[8,896]{1,0:T(8,128)(2,1)}, bf16[8,896]{1,0:T(8,128)(2,1)S(1)}, u32[]{:S(2)}, u32[]{:S(2)}) collective-permute-start(bf16[8,896]{1,0:T(8,128)(2,1)} %pack.1), channel_id=1, source_target_pairs={{0,8},{2,10},{4,12},{6,14},{8,0},{10,2},{12,4},{14,6},{16,24},{18,... | collective-permute-start | bytes 43016 | tf_op jit(solution)/shard_map/ppermute | solution.py:179
  10.3 1.6 %copy-start.4 = (bf16[8,896]{1,0:T(8,128)(2,1)S(1)}, bf16[8,896]{1,0:T(8,128)(2,1)}, u32[]{:S(2)}) copy-start(bf16[8,896]{1,0:T(8,128)(2,1)} %pack.1) | copy-start | bytes 43012
  12.0 6.6 %collective-permute-start.5 = (bf16[32,896]{1,0:T(8,128)(2,1)S(1)}, bf16[32,896]{1,0:T(8,128)(2,1)S(1)}, u32[]{:S(2)}, u32[]{:S(2)}) collective-permute-start(bf16[32,896]{1,0:T(8,128)(2,1)S(1)} %pad_maximum_fusion.block), channel_id=1, source_target_pairs={{0,6},{2,4},{4,2},{6,0},{8,14},{10,12},{12,10},{14,8},{16,22},{18,... | collective-permute-start | bytes 172040 | tf_op jit(solution)/shard_map/ppermute | solution.py:179
  14.5 4.2 %collective-permute-start.4 = (bf16[32,896]{1,0:T(8,128)(2,1)S(1)}, bf16[32,896]{1,0:T(8,128)(2,1)S(1)}, u32[]{:S(2)}, u32[]{:S(2)}) collective-permute-start(bf16[32,896]{1,0:T(8,128)(2,1)S(1)} %pad_maximum_fusion.block), channel_id=1, source_target_pairs={{0,4},{2,6},{4,0},{6,2},{8,12},{10,14},{12,8},{14,10},{16,20},{18,... | collective-permute-start | bytes 172040 | tf_op jit(solution)/shard_map/ppermute | solution.py:179
  15.0 4.2 %collective-permute-start.3 = (bf16[32,896]{1,0:T(8,128)(2,1)S(1)}, bf16[32,896]{1,0:T(8,128)(2,1)S(1)}, u32[]{:S(2)}, u32[]{:S(2)}) collective-permute-start(bf16[32,896]{1,0:T(8,128)(2,1)S(1)} %pad_maximum_fusion.block), channel_id=1, source_target_pairs={{0,2},{2,0},{4,6},{6,4},{8,10},{10,8},{12,14},{14,12},{16,18},{18,... | collective-permute-start | bytes 172040 | tf_op jit(solution)/shard_map/ppermute | solution.py:179
  15.6 1.2 %collective-permute-start.6 = (bf16[32,128]{1,0:T(8,128)(2,1)S(1)}, bf16[32,128]{1,0:T(8,128)(2,1)S(1)}, u32[]{:S(2)}, u32[]{:S(2)}) collective-permute-start(bf16[32,128]{1,0:T(8,128)(2,1)S(1)} %slice.4), channel_id=1, source_target_pairs={{0,1},{1,0},{2,3},{3,2},{4,5},{5,4},{6,7},{7,6},{8,9},{9,8},{10,11... | collective-permute-start | bytes 24584 | tf_op jit(solution)/shard_map/ppermute | solution.py:179
  19.2 2.8 %copy-start = (bf16[512,512]{1,0:T(8,128)(2,1)S(1)}, bf16[512,512]{1,0:T(8,128)(2,1)}, u32[]{:S(2)}) copy-start(bf16[512,512]{1,0:T(8,128)(2,1)} %w_second.3) | copy-start | bytes 1572868
  19.2 2.8 %copy-start.1 = (bf16[768,512]{1,0:T(8,128)(2,1)S(1)}, bf16[768,512]{1,0:T(8,128)(2,1)}, u32[]{:S(2)}) copy-start(bf16[768,512]{1,0:T(8,128)(2,1)} %w_first.1) | copy-start | bytes 2359300
  19.2 2.8 %copy-start.2 = (s32[2,512]{1,0:T(2,128)S(1)}, s32[2,512]{1,0:T(2,128)}, u32[]{:S(2)}) copy-start(s32[2,512]{1,0:T(2,128)} %negatives.1) | copy-start | bytes 12292
  19.3 2.8 %copy-start.3 = (s32[2,16]{1,0:T(2,128)S(1)}, s32[2,16]{1,0:T(2,128)}, u32[]{:S(2)}) copy-start(s32[2,16]{1,0:T(2,128)} %partner.1) | copy-start | bytes 388
  19.3 2.7 %collective-permute-start.7 = (bf16[128,896]{1,0:T(8,128)(2,1)S(1)}, bf16[128,896]{1,0:T(8,128)(2,1)S(1)}, u32[]{:S(2)}, u32[]{:S(2)}) collective-permute-start(bf16[128,896]{1,0:T(8,128)(2,1)S(1)} %constant_dynamic-update-slice_fusion.block.mine), channel_id=1, source_target_pairs={{0,1},{1,0},{2,3},{3,2},{4,5},{5,4},{6,7},{7,6},{8,9},{9,8},{10,11... | collective-permute-start | bytes 688136 | tf_op jit(solution)/shard_map/ppermute | solution.py:179
  29.3 1.7 %collective-permute-start.8 = (bf16[256,512]{1,0:T(8,128)(2,1)S(1)}, bf16[256,512]{1,0:T(8,128)(2,1)S(1)}, u32[]{:S(2)}, u32[]{:S(2)}) collective-permute-start(bf16[256,512]{1,0:T(8,128)(2,1)S(1)} %get-tuple-element.27.grad_mine), channel_id=1, source_target_pairs={{0,1},{1,0},{2,3},{3,2},{4,5},{5,4},{6,7},{7,6},{8,9},{9,8},{10,11... | collective-permute-start | bytes 786440 | tf_op jit(solution)/shard_map/ppermute | solution.py:179
  29.8 1.2 %collective-permute-start.9 = (f32[1,256]{1,0:T(1,128)S(1)}, f32[1,256]{1,0:T(1,128)S(1)}, u32[]{:S(2)}, u32[]{:S(2)}) collective-permute-start(f32[1,256]{1,0:T(1,128)S(1)} %get-tuple-element.30.loss_mine), channel_id=1, source_target_pairs={{0,1},{1,0},{2,3},{3,2},{4,5},{5,4},{6,7},{7,6},{8,9},{9,8},{10,11... | collective-permute-start | bytes 3080 | tf_op jit(solution)/shard_map/ppermute | solution.py:179

commit v4 on v3

--- a/solution.py
+++ b/solution.py
@@ -188,10 +188,14 @@
     return steps
 
 
-def join(value, axis, step, beside):
-    arrived = [swap(value, axis, distance) for distance in step]
-    *arrived, beside = lax.optimization_barrier((*arrived[::-1], beside))
-    return jnp.concatenate([value] + arrived[::-1], axis=0), beside
+def arrivals(value, axis, step):
+    return [swap(value, axis, distance) for distance in step]
+
+
+def join(value, arrived, *beside):
+    count = len(arrived)
+    done = lax.optimization_barrier((*arrived, *beside))
+    return jnp.concatenate([value, *done[:count]], axis=0), *done[count:]
 
 
 def keys_of(size):
@@ -250,23 +254,12 @@
     packed[:, width:] = jnp.concatenate(columns, axis=0).astype(F32).astype(BF16)
 
 
-def early_kernel(rows, width, block, other_ids, table, picked, picked_other, ids, ids_other):
-    ids[...] = block[:, width:].astype(F32)
-    ids_other[...] = other_ids[...].astype(F32)
+def pick_kernel(rows, offset, skipped, block, table, *rest):
+    picked, ids = rest[-2:]
+    ids[...] = block[:, block.shape[1] - LANES :].astype(F32)
     me = lax.axis_index("grp").astype(jnp.int32)
-    for place in range(block.shape[0] // rows):
-        low, high = [
-            jnp.concatenate([id_row(member, kind, place, me, rows) for member in (ids, ids_other)], axis=1)
-            for kind in (LOW, HIGH)
-        ]
-        picked[place], picked_other[place] = pick_relations(low, high, table)
-
-
-def late_kernel(rows, width, skipped, block, table, begun, picked, ids):
-    del begun
-    ids[...] = block[:, width:].astype(F32)
-    me = lax.axis_index("grp").astype(jnp.int32)
-    pick_blocks(ids, range(skipped, block.shape[0] // rows), me, rows, table, picked)
+    count = block.shape[0] // rows
+    pick_blocks(ids, range(skipped, count), me, rows, table, picked.at[pl.ds(offset, count)])
 
 
 def sigmoid_parts(value):
@@ -453,12 +446,9 @@
     loss_out,
     first_out,
     second_out,
-    first,
-    second,
 ):
     me = lax.axis_index("grp").astype(jnp.int32)
     all_rows = mine.shape[0]
-    width = first.shape[0]
     grad = jnp.concatenate(
         [
             grad_mine[:all_rows].astype(F32) + grad_other[all_rows:].astype(F32),
@@ -467,22 +457,23 @@
         axis=0,
     ).astype(BF16)
     across = (((0,), (0,)), ((), ()))
-    total_second = lax.dot_general(hidden[...], grad, across, preferred_element_type=F32)
     grad_hidden = lax.dot_general(
         grad, w_second[...], (((1,), (1,)), ((), ())), preferred_element_type=F32
     )
     grad_pre = (grad_hidden * slope[...]).astype(BF16)
-    features = jnp.concatenate([mine[:, :width], other[:, :width]], axis=0)
-    total_first = lax.dot_general(features, grad_pre, across, preferred_element_type=F32)
-    squares = jnp.sum(total_first * total_first, axis=(0, 1), keepdims=True) + jnp.sum(
-        total_second * total_second, axis=(0, 1), keepdims=True
-    )
+    squares = jnp.zeros((1, 1), F32)
+    for target, parts, factor in ((second_out, (hidden,), grad), (first_out, (mine, other), grad_pre)):
+        share = target.shape[0]
+        for member in (me, 1 - me):
+            columns = pl.ds(pl.multiple_of(member * share, share), share)
+            rows = jnp.concatenate([part[:, columns] for part in parts], axis=0)
+            total = lax.dot_general(rows, factor, across, preferred_element_type=F32)
+            squares = squares + jnp.sum(total * total, axis=(0, 1), keepdims=True)
+            if member is me:
+                target[...] = total
     factor = jnp.minimum(1.0, limit / jnp.sqrt(squares + 1e-06))
-    first[...] = total_first
-    second[...] = total_second
-    for source, target in ((first, first_out), (second, second_out)):
-        share = target.shape[0]
-        target[...] = source[pl.ds(pl.multiple_of(me * share, share), share), :] * factor
+    first_out[...] = first_out[...] * factor
+    second_out[...] = second_out[...] * factor
     edges = loss_out.shape[1]
     for member in range(2):
         loss_out[pl.ds(member, 1), :] = jnp.where(
@@ -534,27 +525,28 @@
         mebibytes=60,
     )(features, heads, relations, tails)
     for step in steps[:-1]:
-        block, table = join(block, "dom", step, table)
+        block, table = join(block, arrivals(block, "dom", step), table)
     early = block.shape[0] // rows
+
+    def pick(block, count, *begun, offset=0, skipped=0):
+        places = block.shape[0] // rows
+        return kernel_call(
+            functools.partial(pick_kernel, rows, offset, skipped),
+            "pick",
+            shape((count, encoded_width, edges), BF16),
+            [pltpu.VMEM((places * rows, edges), F32)],
+            flops * (places - skipped),
+            [pltpu.VMEM] * (2 + len(begun)),
+            input_output_aliases={2: 0} if begun else {},
+        )(block, table, *begun)
+
     early_ids = swap(block[:, width:], "grp", 1)
-    picked, picked_early = kernel_call(
-        functools.partial(early_kernel, rows, width),
-        "early",
-        (picked_shape, shape((early, encoded_width, edges), BF16)),
-        [pltpu.VMEM((early * rows, edges), F32)] * 2,
-        flops * early * 2,
-        [pltpu.VMEM] * 3,
-    )(block, early_ids, table)
-    mine, picked = join(block, "dom", steps[-1], picked)
-    picked = kernel_call(
-        functools.partial(late_kernel, rows, width, early),
-        "late",
-        picked_shape,
-        [pltpu.VMEM((size * rows, edges), F32)],
-        flops * (size - early),
-        [pltpu.VMEM, pltpu.VMEM, pltpu.VMEM],
-        input_output_aliases={2: 0},
-    )(mine, table, picked)
+    arrived = arrivals(block, "dom", steps[-1])
+    picked = pick(block, size)
+    picked_early = pick(early_ids, early)
+    picked = pick(arrived[0], size, picked, offset=early)
+    mine, picked, picked_early = join(block, arrived, picked, picked_early)
+    picked = pick(mine, size, picked, skipped=2 * early)
     other = swap(mine, "grp", 1)
 
     grad, loss, slope, hidden = kernel_call(
@@ -589,9 +581,7 @@
             shape((w_first.shape[0] // 2, w_first.shape[1]), F32),
             shape((w_second.shape[0] // 2, w_second.shape[1]), F32),
         ),
-        [pltpu.VMEM(w_first.shape, F32), pltpu.VMEM(w_second.shape, F32)],
-        0,
-        [pltpu.VMEM] * 9,
+        spaces=[pltpu.VMEM] * 9,
     )(mine, other, grad, grad_other, slope, hidden, w_second, loss, loss_other)
 
 

time: 33.6 us -> 32.5 us (0.967)
  waiting for transfers between devices: 4.36 us -> 3.15 us
    ppermute x10, waiting for transfers between devices: 4.36 us -> 3.15 us  [swap(): lax.ppermute(value, axis, [(i, i ^ distance) for i in range(lax.axis_size...]
    pallas_call x2 -> x4, Pallas kernels: 4.43 us -> 4.81 us  [pick(): kernel_call(functools.partial(pick_kernel, rows, offset, skipped), 'pick'...]
  transfers between devices with their start and end apart: 10 -> 10, of which waited for: 5 -> 4; matrix products, arithmetic and copies ran while one was open for 8% -> 8% of each run, Pallas kernels for 13% -> 15%
where the time goes in v4:
time: 32.5 us; the launch traced here: 32.2 us
  Pallas kernels  15.4 us (47%)
  starting transfers between devices  10 us (31%)
  waiting for transfers between devices  3.15 us (10%)
  local copies, waits for them, and re-layouts  2.76 us (8%)
  between operations  0.83 us (3%)
    ppermute x10, starting transfers between devices, swap(): lax.ppermute(value, axis, [(i, i ^ distance) for i in range(lax.axis_size...  10 us
    pallas_call x1, Pallas kernels, together(): kernel_call(functools.partial(score_kernel, rows, keys), 'scores', (shape...  7.2 us
    pallas_call x4, Pallas kernels, pick(): kernel_call(functools.partial(pick_kernel, rows, offset, skipped), 'pick'...  4.81 us
    ppermute x10, waiting for transfers between devices, swap(): lax.ppermute(value, axis, [(i, i ^ distance) for i in range(lax.axis_size...  3.15 us
    unnamed x17, local copies, waits for them, and re-layouts  2.63 us
    pallas_call x1, Pallas kernels, together(): kernel_call(functools.partial(total_kernel, math.sqrt(w_first.size + w_se...  2.03 us
    pallas_call x1, Pallas kernels, together(): kernel_call(pack_kernel, 'pack', shape((rows, width + edges), BF16), [plt...  1.37 us
  transfers between devices with their start and end apart: 10, of which 4 were waited for; matrix products, arithmetic and copies ran while one was open for 8% of the time, Pallas kernels for 15%

profile of v4, /device:TPU:0, one launch (start us, length us, event | category | flops | bytes accessed | tf_op | source)
XLA Modules:
  0.0 32.2 jit_solution(8739121274168693974)
XLA Ops:
  0.6 1.4 %pack.1 = bf16[8,896]{1,0:T(8,128)(2,1)} custom-call(bf16[8,768]{1,0:T(8,128)(2,1)} %features.1, s32[2,128]{1,0:T(2,128)} %heads.1, s32[2,128]{1,0:T(2,128)} %relations.1, s32[2,128]{1,0:T(2,128)} %tails.1), custom_call_target="tpu_custom_call" | custom-call | tf_op jit(solution)/shard_map/pack/pallas_call | solution.py:515
  2.0 5.1 %collective-permute-start = (bf16[8,896]{1,0:T(8,128)(2,1)}, bf16[8,896]{1,0:T(8,128)(2,1)S(1)}, u32[]{:S(2)}, u32[]{:S(2)}) collective-permute-start(bf16[8,896]{1,0:T(8,128)(2,1)} %pack.1), channel_id=1, source_target_pairs={{0,24},{2,26},{4,28},{6,30},{8,16},{10,18},{12,20},{14,22},{16,8},... | collective-permute-start | bytes 43016 | tf_op jit(solution)/shard_map/ppermute | solution.py:179
  7.1 0.0 collective-permute-start.1
  7.1 0.6 %collective-permute-start.2 = (bf16[8,896]{1,0:T(8,128)(2,1)}, bf16[8,896]{1,0:T(8,128)(2,1)S(1)}, u32[]{:S(2)}, u32[]{:S(2)}) collective-permute-start(bf16[8,896]{1,0:T(8,128)(2,1)} %pack.1), channel_id=1, source_target_pairs={{0,8},{2,10},{4,12},{6,14},{8,0},{10,2},{12,4},{14,6},{16,24},{18,... | collective-permute-start | bytes 43016 | tf_op jit(solution)/shard_map/ppermute | solution.py:179
  7.8 0.7 %constant_dynamic-update-slice_fusion.6 = bf16[128,896]{1,0:T(8,128)(2,1)S(1)} fusion(bf16[8,896]{1,0:T(8,128)(2,1)} %pack.1), kind=kLoop, calls=%fused_computation.7 | loop fusion | bytes 28672
  8.5 1.8 %copy.14 = bf16[1387,512]{0,1:T(8,128)(2,1)S(1)} copy(bf16[1387,512]{1,0:T(8,128)(2,1)} %param.12) | data formatting | bytes 2840576 | tf_op args[3]
  10.3 0.0 copy-start.4
  10.3 0.1 pad.4.table
  10.5 0.0 collective-permute-done
  10.5 1.5 %collective-permute-done.1 = bf16[8,896]{1,0:T(8,128)(2,1)S(1)} collective-permute-done((bf16[8,896]{1,0:T(8,128)(2,1)}, bf16[8,896]{1,0:T(8,128)(2,1)S(1)}, u32[]{:S(2)}, u32[]{:S(2)}) %collective-permute-start.1) | collective-permute-done | bytes 14368 | tf_op jit(solution)/shard_map/ppermute | solution.py:179
  12.0 0.0 collective-permute-done.2
  12.0 0.0 copy-done.4
  12.0 2.5 %collective-permute-start.3 = (bf16[32,896]{1,0:T(8,128)(2,1)S(1)}, bf16[32,896]{1,0:T(8,128)(2,1)S(1)}, u32[]{:S(2)}, u32[]{:S(2)}) collective-permute-start(bf16[32,896]{1,0:T(8,128)(2,1)S(1)} %pad_maximum_fusion.block), channel_id=1, source_target_pairs={{0,6},{2,4},{4,2},{6,0},{8,14},{10,12},{12,10},{14,8},{16,22},{18,... | collective-permute-start | bytes 172040 | tf_op jit(solution)/shard_map/ppermute | solution.py:179
  14.5 0.5 %collective-permute-start.4 = (bf16[32,896]{1,0:T(8,128)(2,1)S(1)}, bf16[32,896]{1,0:T(8,128)(2,1)S(1)}, u32[]{:S(2)}, u32[]{:S(2)}) collective-permute-start(bf16[32,896]{1,0:T(8,128)(2,1)S(1)} %pad_maximum_fusion.block), channel_id=1, source_target_pairs={{0,4},{2,6},{4,0},{6,2},{8,12},{10,14},{12,8},{14,10},{16,20},{18,... | collective-permute-start | bytes 172040 | tf_op jit(solution)/shard_map/ppermute | solution.py:179
  15.0 0.5 %collective-permute-start.5 = (bf16[32,896]{1,0:T(8,128)(2,1)S(1)}, bf16[32,896]{1,0:T(8,128)(2,1)S(1)}, u32[]{:S(2)}, u32[]{:S(2)}) collective-permute-start(bf16[32,896]{1,0:T(8,128)(2,1)S(1)} %pad_maximum_fusion.block), channel_id=1, source_target_pairs={{0,2},{2,0},{4,6},{6,4},{8,10},{10,8},{12,14},{14,12},{16,18},{18,... | collective-permute-start | bytes 172040 | tf_op jit(solution)/shard_map/ppermute | solution.py:179
  15.5 0.0 collective-permute-start.6
  15.6 1.0 %pick.4.rest_0_ = bf16[16,512,128]{2,1,0:T(8,128)(2,1)S(1)} custom-call(bf16[32,896]{1,0:T(8,128)(2,1)S(1)} %pad_maximum_fusion.block, bf16[512,1408]{1,0:T(8,128)(2,1)S(1)} %pad.4.table), custom_call_target="tpu_custom_call" | custom-call | flops 738197504 | tf_op jit(solution)/shard_map/pick/pallas_call | solution.py:533
  16.6 0.1 collective-permute-done.6.block
  16.7 1.0 %pick.6.picked_early = bf16[4,512,128]{2,1,0:T(8,128)(2,1)S(1)} custom-call(bf16[32,128]{1,0:T(8,128)(2,1)S(1)} %collective-permute-done.6.block, bf16[512,1408]{1,0:T(8,128)(2,1)S(1)} %pad.4.table), custom_call_target="tpu_custom_call" | custom-call | flops 738197504 | tf_op jit(solution)/shard_map/pick/pallas_call | solution.py:533
  17.7 0.0 collective-permute-done.3.block
  17.7 1.0 %pick.5.rest_0_ = bf16[16,512,128]{2,1,0:T(8,128)(2,1)S(1)} custom-call(bf16[32,896]{1,0:T(8,128)(2,1)S(1)} %collective-permute-done.3.block, bf16[512,1408]{1,0:T(8,128)(2,1)S(1)} %pad.4.table, bf16[16,512,128]{2,1,0:T(8,128)(2,1)S(1)} %pick.4.rest_0_), custom_call_target="tpu_custom_call", output_to_operand_aliasing={{}: (2, {})} | custom-call | flops 738197504 | tf_op jit(solution)/shard_map/pick/pallas_call | solution.py:533
  18.7 0.0 collective-permute-done.4
  18.7 0.4 %collective-permute-done.5 = bf16[32,896]{1,0:T(8,128)(2,1)S(1)} collective-permute-done((bf16[32,896]{1,0:T(8,128)(2,1)S(1)}, bf16[32,896]{1,0:T(8,128)(2,1)S(1)}, u32[]{:S(2)}, u32[]{:S(2)}) %collective-permute-start.5) | collective-permute-done | bytes 57376 | tf_op jit(solution)/shard_map/ppermute | solution.py:179
  19.2 0.0 copy-start
  19.2 0.0 copy-start.1
  19.2 0.0 copy-start.2
  19.2 0.0 copy-start.3
  19.3 0.1 collective-permute-start.7
  19.3 1.8 %pick.7.picked_mine = bf16[16,512,128]{2,1,0:T(8,128)(2,1)S(1)} custom-call(bf16[128,896]{1,0:T(8,128)(2,1)S(1)} %constant_dynamic-update-slice_fusion.block.mine, bf16[512,1408]{1,0:T(8,128)(2,1)S(1)} %pad.4.table, bf16[16,512,128]{2,1,0:T(8,128)(2,1)S(1)} %pick.5.rest_0_), custom_call_target="tpu_custom_call", output_to_operand_aliasing={{}: (2, {})} | custom-call | flops 1476395008 | tf_op jit(solution)/shard_map/pick/pallas_call | solution.py:533
  21.2 0.0 collective-permute-done.7.other
  21.2 0.0 copy-done
  21.2 0.0 copy-done.1
  21.2 0.0 copy-done.2
  21.2 0.0 copy-done.3
  21.2 7.2 %scores.1 = (bf16[256,512]{1,0:T(8,128)(2,1)S(1)}, f32[1,256]{1,0:T(1,128)S(1)}, f32[256,512]{1,0:T(8,128)S(1)}, bf16[256,512]{1,0:T(8,128)(2,1)S(1)}) custom-call(s32[2,16]{1,0:T(2,128)S(1)} %copy-done.3, bf16[128,896]{1,0:T(8,128)(2,1)S(1)} %constant_dynamic-update-slice_fusion.block.mine, bf16[128,896]{1,0:T(8,128)(2,1)S(1)} %collective-permute-done.7.other, ...), custom_call_target="tpu_custom_call" | custom-call | flops 5905580032 | tf_op jit(solution)/shard_map/scores/pallas_call | solution.py:552
  28.4 0.6 %collective-permute-start.8 = (bf16[256,512]{1,0:T(8,128)(2,1)S(1)}, bf16[256,512]{1,0:T(8,128)(2,1)S(1)}, u32[]{:S(2)}, u32[]{:S(2)}) collective-permute-start(bf16[256,512]{1,0:T(8,128)(2,1)S(1)} %get-tuple-element.25.grad_mine), channel_id=1, source_target_pairs={{0,1},{1,0},{2,3},{3,2},{4,5},{5,4},{6,7},{7,6},{8,9},{9,8},{10,11... | collective-permute-start | bytes 786440 | tf_op jit(solution)/shard_map/ppermute | solution.py:179
  29.0 0.1 collective-permute-start.9
  29.1 1.1 %collective-permute-done.9.loss_other = f32[1,256]{1,0:T(1,128)S(1)} collective-permute-done((f32[1,256]{1,0:T(1,128)S(1)}, f32[1,256]{1,0:T(1,128)S(1)}, u32[]{:S(2)}, u32[]{:S(2)}) %collective-permute-start.9) | collective-permute-done | bytes 1056 | tf_op jit(solution)/shard_map/ppermute | solution.py:179
  30.1 0.0 collective-permute-done.8.grad_other
  30.1 2.0 %totals.1 = (f32[2,128]{1,0:T(2,128)}, f32[384,512]{1,0:T(8,128)}, f32[256,512]{1,0:T(8,128)}) custom-call(bf16[128,896]{1,0:T(8,128)(2,1)S(1)} %constant_dynamic-update-slice_fusion.block.mine, bf16[128,896]{1,0:T(8,128)(2,1)S(1)} %collective-permute-done.7.other, bf16[256,512]{1,0:T(8,128)(2,1)S(1)} %get-tuple-element.25.grad_mine, ...), custom_call_target="tpu_custom_call" | custom-call | tf_op jit(solution)/shard_map/totals/pallas_call | solution.py:576
  (8 shorter events, 0.1 us)
Async XLA Ops:
  2.0 8.5 %collective-permute-start = (bf16[8,896]{1,0:T(8,128)(2,1)}, bf16[8,896]{1,0:T(8,128)(2,1)S(1)}, u32[]{:S(2)}, u32[]{:S(2)}) collective-permute-start(bf16[8,896]{1,0:T(8,128)(2,1)} %pack.1), channel_id=1, source_target_pairs={{0,24},{2,26},{4,28},{6,30},{8,16},{10,18},{12,20},{14,22},{16,8},... | collective-permute-start | bytes 43016 | tf_op jit(solution)/shard_map/ppermute | solution.py:179
  7.1 4.8 %collective-permute-start.1 = (bf16[8,896]{1,0:T(8,128)(2,1)}, bf16[8,896]{1,0:T(8,128)(2,1)S(1)}, u32[]{:S(2)}, u32[]{:S(2)}) collective-permute-start(bf16[8,896]{1,0:T(8,128)(2,1)} %pack.1), channel_id=1, source_target_pairs={{0,16},{2,18},{4,20},{6,22},{8,24},{10,26},{12,28},{14,30},{16,0},... | collective-permute-start | bytes 43016 | tf_op jit(solution)/shard_map/ppermute | solution.py:179
  7.1 4.8 %collective-permute-start.2 = (bf16[8,896]{1,0:T(8,128)(2,1)}, bf16[8,896]{1,0:T(8,128)(2,1)S(1)}, u32[]{:S(2)}, u32[]{:S(2)}) collective-permute-start(bf16[8,896]{1,0:T(8,128)(2,1)} %pack.1), channel_id=1, source_target_pairs={{0,8},{2,10},{4,12},{6,14},{8,0},{10,2},{12,4},{14,6},{16,24},{18,... | collective-permute-start | bytes 43016 | tf_op jit(solution)/shard_map/ppermute | solution.py:179
  10.3 1.6 %copy-start.4 = (bf16[8,896]{1,0:T(8,128)(2,1)S(1)}, bf16[8,896]{1,0:T(8,128)(2,1)}, u32[]{:S(2)}) copy-start(bf16[8,896]{1,0:T(8,128)(2,1)} %pack.1) | copy-start | bytes 43012
  12.0 5.7 %collective-permute-start.3 = (bf16[32,896]{1,0:T(8,128)(2,1)S(1)}, bf16[32,896]{1,0:T(8,128)(2,1)S(1)}, u32[]{:S(2)}, u32[]{:S(2)}) collective-permute-start(bf16[32,896]{1,0:T(8,128)(2,1)S(1)} %pad_maximum_fusion.block), channel_id=1, source_target_pairs={{0,6},{2,4},{4,2},{6,0},{8,14},{10,12},{12,10},{14,8},{16,22},{18,... | collective-permute-start | bytes 172040 | tf_op jit(solution)/shard_map/ppermute | solution.py:179
  14.5 4.2 %collective-permute-start.4 = (bf16[32,896]{1,0:T(8,128)(2,1)S(1)}, bf16[32,896]{1,0:T(8,128)(2,1)S(1)}, u32[]{:S(2)}, u32[]{:S(2)}) collective-permute-start(bf16[32,896]{1,0:T(8,128)(2,1)S(1)} %pad_maximum_fusion.block), channel_id=1, source_target_pairs={{0,4},{2,6},{4,0},{6,2},{8,12},{10,14},{12,8},{14,10},{16,20},{18,... | collective-permute-start | bytes 172040 | tf_op jit(solution)/shard_map/ppermute | solution.py:179
  15.0 4.2 %collective-permute-start.5 = (bf16[32,896]{1,0:T(8,128)(2,1)S(1)}, bf16[32,896]{1,0:T(8,128)(2,1)S(1)}, u32[]{:S(2)}, u32[]{:S(2)}) collective-permute-start(bf16[32,896]{1,0:T(8,128)(2,1)S(1)} %pad_maximum_fusion.block), channel_id=1, source_target_pairs={{0,2},{2,0},{4,6},{6,4},{8,10},{10,8},{12,14},{14,12},{16,18},{18,... | collective-permute-start | bytes 172040 | tf_op jit(solution)/shard_map/ppermute | solution.py:179
  15.5 1.2 %collective-permute-start.6 = (bf16[32,128]{1,0:T(8,128)(2,1)S(1)}, bf16[32,128]{1,0:T(8,128)(2,1)S(1)}, u32[]{:S(2)}, u32[]{:S(2)}) collective-permute-start(bf16[32,128]{1,0:T(8,128)(2,1)S(1)} %slice.4), channel_id=1, source_target_pairs={{0,1},{1,0},{2,3},{3,2},{4,5},{5,4},{6,7},{7,6},{8,9},{9,8},{10,11... | collective-permute-start | bytes 24584 | tf_op jit(solution)/shard_map/ppermute | solution.py:179
  19.2 2.0 %copy-start = (bf16[512,512]{1,0:T(8,128)(2,1)S(1)}, bf16[512,512]{1,0:T(8,128)(2,1)}, u32[]{:S(2)}) copy-start(bf16[512,512]{1,0:T(8,128)(2,1)} %w_second.3) | copy-start | bytes 1572868
  19.2 2.0 %copy-start.1 = (bf16[768,512]{1,0:T(8,128)(2,1)S(1)}, bf16[768,512]{1,0:T(8,128)(2,1)}, u32[]{:S(2)}) copy-start(bf16[768,512]{1,0:T(8,128)(2,1)} %w_first.1) | copy-start | bytes 2359300
  19.2 2.0 %copy-start.2 = (s32[2,512]{1,0:T(2,128)S(1)}, s32[2,512]{1,0:T(2,128)}, u32[]{:S(2)}) copy-start(s32[2,512]{1,0:T(2,128)} %negatives.1) | copy-start | bytes 12292
  19.2 2.0 %copy-start.3 = (s32[2,16]{1,0:T(2,128)S(1)}, s32[2,16]{1,0:T(2,128)}, u32[]{:S(2)}) copy-start(s32[2,16]{1,0:T(2,128)} %partner.1) | copy-start | bytes 388
  19.3 1.9 %collective-permute-start.7 = (bf16[128,896]{1,0:T(8,128)(2,1)S(1)}, bf16[128,896]{1,0:T(8,128)(2,1)S(1)}, u32[]{:S(2)}, u32[]{:S(2)}) collective-permute-start(bf16[128,896]{1,0:T(8,128)(2,1)S(1)} %constant_dynamic-update-slice_fusion.block.mine), channel_id=1, source_target_pairs={{0,1},{1,0},{2,3},{3,2},{4,5},{5,4},{6,7},{7,6},{8,9},{9,8},{10,11... | collective-permute-start | bytes 688136 | tf_op jit(solution)/shard_map/ppermute | solution.py:179
  28.4 1.7 %collective-permute-start.8 = (bf16[256,512]{1,0:T(8,128)(2,1)S(1)}, bf16[256,512]{1,0:T(8,128)(2,1)S(1)}, u32[]{:S(2)}, u32[]{:S(2)}) collective-permute-start(bf16[256,512]{1,0:T(8,128)(2,1)S(1)} %get-tuple-element.25.grad_mine), channel_id=1, source_target_pairs={{0,1},{1,0},{2,3},{3,2},{4,5},{5,4},{6,7},{7,6},{8,9},{9,8},{10,11... | collective-permute-start | bytes 786440 | tf_op jit(solution)/shard_map/ppermute | solution.py:179
  29.0 1.2 %collective-permute-start.9 = (f32[1,256]{1,0:T(1,128)S(1)}, f32[1,256]{1,0:T(1,128)S(1)}, u32[]{:S(2)}, u32[]{:S(2)}) collective-permute-start(f32[1,256]{1,0:T(1,128)S(1)} %get-tuple-element.28.loss_mine), channel_id=1, source_target_pairs={{0,1},{1,0},{2,3},{3,2},{4,5},{5,4},{6,7},{7,6},{8,9},{9,8},{10,11... | collective-permute-start | bytes 3080 | tf_op jit(solution)/shard_map/ppermute | solution.py:179

commit v5 on v4

--- a/solution.py
+++ b/solution.py
@@ -173,6 +173,7 @@
 
 ROUNDS = 2
 HEAD, TAIL, HIGH, LOW = 0, 1, 2, 3
+LANE_BITS = LANES.bit_length() - 1
 
 
 def swap(value, axis, distance):
@@ -237,21 +238,22 @@
         picked[first], picked[first + 1] = pick_relations(low, high, table)
 
 
-def pack_kernel(features, heads, relations, tails, packed, rows, ids, sems):
-    sources = (features, heads, relations, tails)
-    targets = (rows, ids.at[0], ids.at[1], ids.at[2])
-    copies = [
-        pltpu.make_async_copy(source, target, sems.at[i])
-        for i, (source, target) in enumerate(zip(sources, targets, strict=True))
-    ]
-    for copy in copies:
-        copy.start()
-    for copy in copies:
-        copy.wait()
-    width = features.shape[1]
-    packed[:, :width] = rows[...]
-    columns = [ids[0], ids[2], ids[1] // LANES, ids[1] % LANES]
-    packed[:, width:] = jnp.concatenate(columns, axis=0).astype(F32).astype(BF16)
+def pack(features, heads, tails, relations):
+    rows, width = features.shape
+
+    def placed(value, top, left):
+        beyond = rows - top - value.shape[0], width + LANES - left - value.shape[1]
+        return lax.pad(value, jnp.zeros((), value.dtype), ((top, beyond[0], 0), (left, beyond[1], 0)))
+
+    kinds = ((HEAD, heads), (TAIL, tails), (HIGH, relations))
+    ids = sum(placed(value, kind * ROUNDS, width) for kind, value in kinds)
+    both = placed(features, 0, 0).astype(F32) + ids.astype(F32)
+    both = lax.optimization_barrier(both)
+    ids = both[:, width:]
+    high = jnp.floor(ids[HIGH * ROUNDS : LOW * ROUNDS] * (1.0 / LANES))
+    low = ids[HIGH * ROUNDS : LOW * ROUNDS] - high * LANES
+    ids = jnp.concatenate([ids[: HIGH * ROUNDS], high, low], axis=0)
+    return jnp.concatenate([both[:, :width], ids], axis=1).astype(BF16)
 
 
 def pick_kernel(rows, offset, skipped, block, table, *rest):
@@ -378,6 +380,22 @@
         weight = (chance / negative_count).astype(BF16).astype(F32) * counts
         weights_kept[place] = (weight - jnp.where(is_tail, chance_positive, 0.0)).astype(BF16)
 
+    sublane = lax.broadcasted_iota(jnp.int32, (rows, half), 0)
+
+    def halved(value):
+        return value[:rows] + value[rows:]
+
+    def row_sums(blocks):
+        step = 1
+        while len(blocks) > 1:
+            upper = (sublane & step) != 0
+            blocks = [
+                jnp.where(upper, second, first) + pltpu.roll(jnp.where(upper, first, second), step, 0)
+                for first, second in zip(blocks[::2], blocks[1::2], strict=True)
+            ]
+            step *= 2
+        return blocks[0]
+
     for pair in range(places // 2):
         place = pair + (pair & -low_bit)
         far = place ^ far_place
@@ -415,15 +433,18 @@
             far_grad_re = far_grad_re + (row_re * part_re + row_im * part_im)
             far_grad_im = far_grad_im + (row_im * part_re - row_re * part_im)
             near_grad.append(
-                jnp.concatenate(
-                    [
-                        jnp.sum(far_re * part_re - far_im * part_im, axis=0, keepdims=True),
-                        jnp.sum(far_im * part_re + far_re * part_im, axis=0, keepdims=True),
-                    ],
-                    axis=1,
+                (
+                    halved(far_re * part_re - far_im * part_im),
+                    halved(far_im * part_re + far_re * part_im),
                 )
             )
-        near_grad = jnp.concatenate(near_grad, axis=0)
+        near_grad = jnp.concatenate(
+            [
+                jnp.concatenate([row_sums([part[k] for part in near_grad[i : i + rows]]) for k in (0, 1)], axis=1)
+                for i in range(0, group_rows, rows)
+            ],
+            axis=0,
+        )
         far_grad = jnp.concatenate([far_grad_re, far_grad_im], axis=1)
         for member, base in enumerate(members):
             span = slice(member * rows, (member + 1) * rows)
@@ -512,18 +533,7 @@
     picked_shape = shape((size, encoded_width, edges), BF16)
     flops = 2 * table.size * edges
 
-    block = kernel_call(
-        pack_kernel,
-        "pack",
-        shape((rows, width + edges), BF16),
-        [
-            pltpu.VMEM(features.shape, BF16),
-            pltpu.VMEM((3, rounds, edges), jnp.int32),
-            pltpu.SemaphoreType.DMA((4,)),
-        ],
-        spaces=[pltpu.HBM] * 4,
-        mebibytes=60,
-    )(features, heads, relations, tails)
+    block = pack(features, heads, tails, relations)
     for step in steps[:-1]:
         block, table = join(block, arrivals(block, "dom", step), table)
     early = block.shape[0] // rows
@@ -594,6 +604,7 @@
             and edges == LANES
             and 4 * rounds == rows
             and mesh.shape["dom"] >= 8
+            and relation_table.shape[0] <= LANES * 256
         )
         plan = together if fits else spread
         return plan(features, w_first, w_second, relation_table, heads, relations, tails, *rest)

time: 32.5 us -> 31.5 us (0.969)
  Pallas kernels: 15.4 us -> 13.8 us
  other arithmetic: 0.01 us -> 0.81 us
  local copies, waits for them, and re-layouts: 2.76 us -> 2.01 us
  waiting for transfers between devices: 3.15 us -> 3.71 us
    pallas_call x1 -> x0, Pallas kernels: 1.37 us -> none  [together(): kernel_call(pack_kernel, 'pack', shape((rows, width + edges), BF16), [plt...]
    add x0 -> x1, other arithmetic: none -> 0.77 us  [pack(): both = placed(features, 0, 0).astype(F32) + ids.astype(F32)]
    unnamed x17 -> x14, local copies, waits for them, and re-layouts: 2.63 us -> 1.88 us
    ppermute x10, waiting for transfers between devices: 3.15 us -> 3.71 us  [swap(): lax.ppermute(value, axis, [(i, i ^ distance) for i in range(lax.axis_size...]
  transfers between devices with their start and end apart: 10 -> 10, of which waited for: 4 -> 4; matrix products, arithmetic and copies ran while one was open for 8% -> 6% of each run, Pallas kernels for 15% -> 15%
where the time goes in v5:
time: 31.5 us; the launch traced here: 31.2 us
  Pallas kernels  13.8 us (44%)
  starting transfers between devices  10.1 us (32%)
  waiting for transfers between devices  3.71 us (12%)
  local copies, waits for them, and re-layouts  2.01 us (6%)
  between operations  0.84 us (3%)
  other arithmetic  0.81 us (3%)
    ppermute x10, starting transfers between devices, swap(): lax.ppermute(value, axis, [(i, i ^ distance) for i in range(lax.axis_size...  10.1 us
    pallas_call x1, Pallas kernels, together(): kernel_call(functools.partial(score_kernel, rows, keys), 'scores', (shape...  6.99 us
    pallas_call x4, Pallas kernels, pick(): kernel_call(functools.partial(pick_kernel, rows, offset, skipped), 'pick'...  4.8 us
    ppermute x10, waiting for transfers between devices, swap(): lax.ppermute(value, axis, [(i, i ^ distance) for i in range(lax.axis_size...  3.71 us
    pallas_call x1, Pallas kernels, together(): kernel_call(functools.partial(total_kernel, math.sqrt(w_first.size + w_se...  2.04 us
    unnamed x14, local copies, waits for them, and re-layouts  1.88 us
    add x1, other arithmetic, pack(): both = placed(features, 0, 0).astype(F32) + ids.astype(F32)  0.77 us
  transfers between devices with their start and end apart: 10, of which 4 were waited for; matrix products, arithmetic and copies ran while one was open for 6% of the time, Pallas kernels for 15%

profile of v5, /device:TPU:0, one launch (start us, length us, event | category | flops | bytes accessed | tf_op | source)
XLA Modules:
  0.0 31.2 jit_solution(5538222702271602811)
XLA Ops:
  0.6 0.8 %convert_add_fusion = f32[8,896]{1,0:T(8,128)S(1)} fusion(s32[2,128]{1,0:T(2,128)} %param.14, s32[2,128]{1,0:T(2,128)} %param.15, s32[2,128]{1,0:T(2,128)} %param.13, bf16[8,768]{1,0:T(8,128)(2,1)} %param.9), kind=kLoop, calls=%fused_computation.1 | loop fusion | flops 35840 | bytes 44032 | tf_op jit(solution)/shard_map/add | solution.py:250
  1.5 5.1 %collective-permute-start = (bf16[8,896]{1,0:T(8,128)(2,1)S(1)}, bf16[8,896]{1,0:T(8,128)(2,1)S(1)}, u32[]{:S(2)}, u32[]{:S(2)}) collective-permute-start(bf16[8,896]{1,0:T(8,128)(2,1)S(1)} %get-tuple-element.31), channel_id=1, source_target_pairs={{0,24},{2,26},{4,28},{6,30},{8,16},{10,18},{12,20},{14,22},{16,8},... | collective-permute-start | bytes 43016 | tf_op jit(solution)/shard_map/ppermute | solution.py:180
  6.6 0.0 collective-permute-start.1
  6.6 0.6 %collective-permute-start.2 = (bf16[8,896]{1,0:T(8,128)(2,1)S(1)}, bf16[8,896]{1,0:T(8,128)(2,1)S(1)}, u32[]{:S(2)}, u32[]{:S(2)}) collective-permute-start(bf16[8,896]{1,0:T(8,128)(2,1)S(1)} %get-tuple-element.31), channel_id=1, source_target_pairs={{0,8},{2,10},{4,12},{6,14},{8,0},{10,2},{12,4},{14,6},{16,24},{18,... | collective-permute-start | bytes 43016 | tf_op jit(solution)/shard_map/ppermute | solution.py:180
  7.2 1.8 %copy.14 = bf16[1387,512]{0,1:T(8,128)(2,1)S(1)} copy(bf16[1387,512]{1,0:T(8,128)(2,1)} %param.12) | data formatting | bytes 2840576 | tf_op args[3]
  9.0 0.1 pad.20.table
  9.1 0.0 collective-permute-done
  9.2 2.0 %collective-permute-done.1 = bf16[8,896]{1,0:T(8,128)(2,1)S(1)} collective-permute-done((bf16[8,896]{1,0:T(8,128)(2,1)S(1)}, bf16[8,896]{1,0:T(8,128)(2,1)S(1)}, u32[]{:S(2)}, u32[]{:S(2)}) %collective-permute-start.1) | collective-permute-done | bytes 14368 | tf_op jit(solution)/shard_map/ppermute | solution.py:180
  11.2 0.0 collective-permute-done.2
  11.2 2.5 %collective-permute-start.3 = (bf16[32,896]{1,0:T(8,128)(2,1)S(1)}, bf16[32,896]{1,0:T(8,128)(2,1)S(1)}, u32[]{:S(2)}, u32[]{:S(2)}) collective-permute-start(bf16[32,896]{1,0:T(8,128)(2,1)S(1)} %pad_maximum_fusion.block), channel_id=1, source_target_pairs={{0,6},{2,4},{4,2},{6,0},{8,14},{10,12},{12,10},{14,8},{16,22},{18,... | collective-permute-start | bytes 172040 | tf_op jit(solution)/shard_map/ppermute | solution.py:180
  13.7 0.5 %collective-permute-start.4 = (bf16[32,896]{1,0:T(8,128)(2,1)S(1)}, bf16[32,896]{1,0:T(8,128)(2,1)S(1)}, u32[]{:S(2)}, u32[]{:S(2)}) collective-permute-start(bf16[32,896]{1,0:T(8,128)(2,1)S(1)} %pad_maximum_fusion.block), channel_id=1, source_target_pairs={{0,4},{2,6},{4,0},{6,2},{8,12},{10,14},{12,8},{14,10},{16,20},{18,... | collective-permute-start | bytes 172040 | tf_op jit(solution)/shard_map/ppermute | solution.py:180
  14.2 0.5 %collective-permute-start.5 = (bf16[32,896]{1,0:T(8,128)(2,1)S(1)}, bf16[32,896]{1,0:T(8,128)(2,1)S(1)}, u32[]{:S(2)}, u32[]{:S(2)}) collective-permute-start(bf16[32,896]{1,0:T(8,128)(2,1)S(1)} %pad_maximum_fusion.block), channel_id=1, source_target_pairs={{0,2},{2,0},{4,6},{6,4},{8,10},{10,8},{12,14},{14,12},{16,18},{18,... | collective-permute-start | bytes 172040 | tf_op jit(solution)/shard_map/ppermute | solution.py:180
  14.8 0.0 collective-permute-start.6
  14.8 1.0 %pick.4.rest_0_ = bf16[16,512,128]{2,1,0:T(8,128)(2,1)S(1)} custom-call(bf16[32,896]{1,0:T(8,128)(2,1)S(1)} %pad_maximum_fusion.block, bf16[512,1408]{1,0:T(8,128)(2,1)S(1)} %pad.20.table), custom_call_target="tpu_custom_call" | custom-call | flops 738197504 | tf_op jit(solution)/shard_map/pick/pallas_call | solution.py:543
  15.8 0.1 collective-permute-done.6.block
  15.9 1.0 %pick.6.picked_early = bf16[4,512,128]{2,1,0:T(8,128)(2,1)S(1)} custom-call(bf16[32,128]{1,0:T(8,128)(2,1)S(1)} %collective-permute-done.6.block, bf16[512,1408]{1,0:T(8,128)(2,1)S(1)} %pad.20.table), custom_call_target="tpu_custom_call" | custom-call | flops 738197504 | tf_op jit(solution)/shard_map/pick/pallas_call | solution.py:543
  16.9 0.0 collective-permute-done.3.block
  17.0 1.0 %pick.5.rest_0_ = bf16[16,512,128]{2,1,0:T(8,128)(2,1)S(1)} custom-call(bf16[32,896]{1,0:T(8,128)(2,1)S(1)} %collective-permute-done.3.block, bf16[512,1408]{1,0:T(8,128)(2,1)S(1)} %pad.20.table, bf16[16,512,128]{2,1,0:T(8,128)(2,1)S(1)} %pick.4.rest_0_), custom_call_target="tpu_custom_call", output_to_operand_aliasing={{}: (2, {})} | custom-call | flops 738197504 | tf_op jit(solution)/shard_map/pick/pallas_call | solution.py:543
  18.0 0.0 collective-permute-done.4
  18.0 0.4 %collective-permute-done.5 = bf16[32,896]{1,0:T(8,128)(2,1)S(1)} collective-permute-done((bf16[32,896]{1,0:T(8,128)(2,1)S(1)}, bf16[32,896]{1,0:T(8,128)(2,1)S(1)}, u32[]{:S(2)}, u32[]{:S(2)}) %collective-permute-start.5) | collective-permute-done | bytes 57376 | tf_op jit(solution)/shard_map/ppermute | solution.py:180
  18.5 0.0 copy-start
  18.5 0.0 copy-start.1
  18.5 0.0 copy-start.2
  18.5 0.0 copy-start.3
  18.5 0.1 collective-permute-start.7
  18.6 1.8 %pick.7.picked_mine = bf16[16,512,128]{2,1,0:T(8,128)(2,1)S(1)} custom-call(bf16[128,896]{1,0:T(8,128)(2,1)S(1)} %constant_dynamic-update-slice_fusion.block.mine, bf16[512,1408]{1,0:T(8,128)(2,1)S(1)} %pad.20.table, bf16[16,512,128]{2,1,0:T(8,128)(2,1)S(1)} %pick.5.rest_0_), custom_call_target="tpu_custom_call", output_to_operand_aliasing={{}: (2, {})} | custom-call | flops 1476395008 | tf_op jit(solution)/shard_map/pick/pallas_call | solution.py:543
  20.4 0.0 collective-permute-done.7.other
  20.4 0.0 copy-done
  20.4 0.0 copy-done.1
  20.4 0.0 copy-done.2
  20.4 0.0 copy-done.3
  20.4 7.0 %scores.1 = (bf16[256,512]{1,0:T(8,128)(2,1)S(1)}, f32[1,256]{1,0:T(1,128)S(1)}, f32[256,512]{1,0:T(8,128)S(1)}, bf16[256,512]{1,0:T(8,128)(2,1)S(1)}) custom-call(s32[2,16]{1,0:T(2,128)S(1)} %copy-done.3, bf16[128,896]{1,0:T(8,128)(2,1)S(1)} %constant_dynamic-update-slice_fusion.block.mine, bf16[128,896]{1,0:T(8,128)(2,1)S(1)} %collective-permute-done.7.other, ...), custom_call_target="tpu_custom_call" | custom-call | flops 5905580032 | tf_op jit(solution)/shard_map/scores/pallas_call | solution.py:562
  27.4 0.6 %collective-permute-start.8 = (bf16[256,512]{1,0:T(8,128)(2,1)S(1)}, bf16[256,512]{1,0:T(8,128)(2,1)S(1)}, u32[]{:S(2)}, u32[]{:S(2)}) collective-permute-start(bf16[256,512]{1,0:T(8,128)(2,1)S(1)} %get-tuple-element.25.grad_mine), channel_id=1, source_target_pairs={{0,1},{1,0},{2,3},{3,2},{4,5},{5,4},{6,7},{7,6},{8,9},{9,8},{10,11... | collective-permute-start | bytes 786440 | tf_op jit(solution)/shard_map/ppermute | solution.py:180
  28.0 0.1 collective-permute-start.9
  28.1 1.1 %collective-permute-done.9.loss_other = f32[1,256]{1,0:T(1,128)S(1)} collective-permute-done((f32[1,256]{1,0:T(1,128)S(1)}, f32[1,256]{1,0:T(1,128)S(1)}, u32[]{:S(2)}, u32[]{:S(2)}) %collective-permute-start.9) | collective-permute-done | bytes 1056 | tf_op jit(solution)/shard_map/ppermute | solution.py:180
  29.2 0.0 collective-permute-done.8.grad_other
  29.2 2.0 %totals.1 = (f32[2,128]{1,0:T(2,128)}, f32[384,512]{1,0:T(8,128)}, f32[256,512]{1,0:T(8,128)}) custom-call(bf16[128,896]{1,0:T(8,128)(2,1)S(1)} %constant_dynamic-update-slice_fusion.block.mine, bf16[128,896]{1,0:T(8,128)(2,1)S(1)} %collective-permute-done.7.other, bf16[256,512]{1,0:T(8,128)(2,1)S(1)} %get-tuple-element.25.grad_mine, ...), custom_call_target="tpu_custom_call" | custom-call | tf_op jit(solution)/shard_map/totals/pallas_call | solution.py:586
  (13 shorter events, 0.1 us)
Async XLA Ops:
  1.5 7.7 %collective-permute-start = (bf16[8,896]{1,0:T(8,128)(2,1)S(1)}, bf16[8,896]{1,0:T(8,128)(2,1)S(1)}, u32[]{:S(2)}, u32[]{:S(2)}) collective-permute-start(bf16[8,896]{1,0:T(8,128)(2,1)S(1)} %get-tuple-element.31), channel_id=1, source_target_pairs={{0,24},{2,26},{4,28},{6,30},{8,16},{10,18},{12,20},{14,22},{16,8},... | collective-permute-start | bytes 43016 | tf_op jit(solution)/shard_map/ppermute | solution.py:180
  6.6 4.6 %collective-permute-start.1 = (bf16[8,896]{1,0:T(8,128)(2,1)S(1)}, bf16[8,896]{1,0:T(8,128)(2,1)S(1)}, u32[]{:S(2)}, u32[]{:S(2)}) collective-permute-start(bf16[8,896]{1,0:T(8,128)(2,1)S(1)} %get-tuple-element.31), channel_id=1, source_target_pairs={{0,16},{2,18},{4,20},{6,22},{8,24},{10,26},{12,28},{14,30},{16,0},... | collective-permute-start | bytes 43016 | tf_op jit(solution)/shard_map/ppermute | solution.py:180
  6.6 4.6 %collective-permute-start.2 = (bf16[8,896]{1,0:T(8,128)(2,1)S(1)}, bf16[8,896]{1,0:T(8,128)(2,1)S(1)}, u32[]{:S(2)}, u32[]{:S(2)}) collective-permute-start(bf16[8,896]{1,0:T(8,128)(2,1)S(1)} %get-tuple-element.31), channel_id=1, source_target_pairs={{0,8},{2,10},{4,12},{6,14},{8,0},{10,2},{12,4},{14,6},{16,24},{18,... | collective-permute-start | bytes 43016 | tf_op jit(solution)/shard_map/ppermute | solution.py:180
  11.2 5.7 %collective-permute-start.3 = (bf16[32,896]{1,0:T(8,128)(2,1)S(1)}, bf16[32,896]{1,0:T(8,128)(2,1)S(1)}, u32[]{:S(2)}, u32[]{:S(2)}) collective-permute-start(bf16[32,896]{1,0:T(8,128)(2,1)S(1)} %pad_maximum_fusion.block), channel_id=1, source_target_pairs={{0,6},{2,4},{4,2},{6,0},{8,14},{10,12},{12,10},{14,8},{16,22},{18,... | collective-permute-start | bytes 172040 | tf_op jit(solution)/shard_map/ppermute | solution.py:180
  13.7 4.2 %collective-permute-start.4 = (bf16[32,896]{1,0:T(8,128)(2,1)S(1)}, bf16[32,896]{1,0:T(8,128)(2,1)S(1)}, u32[]{:S(2)}, u32[]{:S(2)}) collective-permute-start(bf16[32,896]{1,0:T(8,128)(2,1)S(1)} %pad_maximum_fusion.block), channel_id=1, source_target_pairs={{0,4},{2,6},{4,0},{6,2},{8,12},{10,14},{12,8},{14,10},{16,20},{18,... | collective-permute-start | bytes 172040 | tf_op jit(solution)/shard_map/ppermute | solution.py:180
  14.2 4.2 %collective-permute-start.5 = (bf16[32,896]{1,0:T(8,128)(2,1)S(1)}, bf16[32,896]{1,0:T(8,128)(2,1)S(1)}, u32[]{:S(2)}, u32[]{:S(2)}) collective-permute-start(bf16[32,896]{1,0:T(8,128)(2,1)S(1)} %pad_maximum_fusion.block), channel_id=1, source_target_pairs={{0,2},{2,0},{4,6},{6,4},{8,10},{10,8},{12,14},{14,12},{16,18},{18,... | collective-permute-start | bytes 172040 | tf_op jit(solution)/shard_map/ppermute | solution.py:180
  14.8 1.2 %collective-permute-start.6 = (bf16[32,128]{1,0:T(8,128)(2,1)S(1)}, bf16[32,128]{1,0:T(8,128)(2,1)S(1)}, u32[]{:S(2)}, u32[]{:S(2)}) collective-permute-start(bf16[32,128]{1,0:T(8,128)(2,1)S(1)} %slice.25), channel_id=1, source_target_pairs={{0,1},{1,0},{2,3},{3,2},{4,5},{5,4},{6,7},{7,6},{8,9},{9,8},{10,11... | collective-permute-start | bytes 24584 | tf_op jit(solution)/shard_map/ppermute | solution.py:180
  18.5 2.0 %copy-start = (bf16[512,512]{1,0:T(8,128)(2,1)S(1)}, bf16[512,512]{1,0:T(8,128)(2,1)}, u32[]{:S(2)}) copy-start(bf16[512,512]{1,0:T(8,128)(2,1)} %w_second.3) | copy-start | bytes 1572868
  18.5 2.0 %copy-start.1 = (bf16[768,512]{1,0:T(8,128)(2,1)S(1)}, bf16[768,512]{1,0:T(8,128)(2,1)}, u32[]{:S(2)}) copy-start(bf16[768,512]{1,0:T(8,128)(2,1)} %w_first.1) | copy-start | bytes 2359300
  18.5 2.0 %copy-start.2 = (s32[2,512]{1,0:T(2,128)S(1)}, s32[2,512]{1,0:T(2,128)}, u32[]{:S(2)}) copy-start(s32[2,512]{1,0:T(2,128)} %negatives.1) | copy-start | bytes 12292
  18.5 2.0 %copy-start.3 = (s32[2,16]{1,0:T(2,128)S(1)}, s32[2,16]{1,0:T(2,128)}, u32[]{:S(2)}) copy-start(s32[2,16]{1,0:T(2,128)} %partner.1) | copy-start | bytes 388
  18.5 1.9 %collective-permute-start.7 = (bf16[128,896]{1,0:T(8,128)(2,1)S(1)}, bf16[128,896]{1,0:T(8,128)(2,1)S(1)}, u32[]{:S(2)}, u32[]{:S(2)}) collective-permute-start(bf16[128,896]{1,0:T(8,128)(2,1)S(1)} %constant_dynamic-update-slice_fusion.block.mine), channel_id=1, source_target_pairs={{0,1},{1,0},{2,3},{3,2},{4,5},{5,4},{6,7},{7,6},{8,9},{9,8},{10,11... | collective-permute-start | bytes 688136 | tf_op jit(solution)/shard_map/ppermute | solution.py:180
  27.4 1.8 %collective-permute-start.8 = (bf16[256,512]{1,0:T(8,128)(2,1)S(1)}, bf16[256,512]{1,0:T(8,128)(2,1)S(1)}, u32[]{:S(2)}, u32[]{:S(2)}) collective-permute-start(bf16[256,512]{1,0:T(8,128)(2,1)S(1)} %get-tuple-element.25.grad_mine), channel_id=1, source_target_pairs={{0,1},{1,0},{2,3},{3,2},{4,5},{5,4},{6,7},{7,6},{8,9},{9,8},{10,11... | collective-permute-start | bytes 786440 | tf_op jit(solution)/shard_map/ppermute | solution.py:180
  28.0 1.2 %collective-permute-start.9 = (f32[1,256]{1,0:T(1,128)S(1)}, f32[1,256]{1,0:T(1,128)S(1)}, u32[]{:S(2)}, u32[]{:S(2)}) collective-permute-start(f32[1,256]{1,0:T(1,128)S(1)} %get-tuple-element.28.loss_mine), channel_id=1, source_target_pairs={{0,1},{1,0},{2,3},{3,2},{4,5},{5,4},{6,7},{7,6},{8,9},{9,8},{10,11... | collective-permute-start | bytes 3080 | tf_op jit(solution)/shard_map/ppermute | solution.py:180

commit v6 on v5

--- a/solution.py
+++ b/solution.py
@@ -256,12 +256,12 @@
     return jnp.concatenate([both[:, :width], ids], axis=1).astype(BF16)
 
 
-def pick_kernel(rows, offset, skipped, block, table, *rest):
+def pick_kernel(rows, offset, skipped, stop, block, table, *rest):
     picked, ids = rest[-2:]
     ids[...] = block[:, block.shape[1] - LANES :].astype(F32)
     me = lax.axis_index("grp").astype(jnp.int32)
     count = block.shape[0] // rows
-    pick_blocks(ids, range(skipped, count), me, rows, table, picked.at[pl.ds(offset, count)])
+    pick_blocks(ids, range(skipped, stop), me, rows, table, picked.at[pl.ds(offset, count)])
 
 
 def sigmoid_parts(value):
@@ -538,14 +538,15 @@
         block, table = join(block, arrivals(block, "dom", step), table)
     early = block.shape[0] // rows
 
-    def pick(block, count, *begun, offset=0, skipped=0):
+    def pick(block, count, *begun, offset=0, skipped=0, stop=None):
         places = block.shape[0] // rows
+        stop = places if stop is None else stop
         return kernel_call(
-            functools.partial(pick_kernel, rows, offset, skipped),
+            functools.partial(pick_kernel, rows, offset, skipped, stop),
             "pick",
             shape((count, encoded_width, edges), BF16),
             [pltpu.VMEM((places * rows, edges), F32)],
-            flops * (places - skipped),
+            flops * (stop - skipped),
             [pltpu.VMEM] * (2 + len(begun)),
             input_output_aliases={2: 0} if begun else {},
         )(block, table, *begun)
@@ -555,8 +556,12 @@
     picked = pick(block, size)
     picked_early = pick(early_ids, early)
     picked = pick(arrived[0], size, picked, offset=early)
+    done = 2 * early
+    if len(arrived) > 1:
+        picked = pick(arrived[1], size, picked, offset=done, stop=early // 2)
+        done += early // 2
     mine, picked, picked_early = join(block, arrived, picked, picked_early)
-    picked = pick(mine, size, picked, skipped=2 * early)
+    picked = pick(mine, size, picked, skipped=done)
     other = swap(mine, "grp", 1)
 
     grad, loss, slope, hidden = kernel_call(

time: 31.5 us -> 31.5 us (level)
  waiting for transfers between devices: 3.71 us -> 3.21 us
    ppermute x10, waiting for transfers between devices: 3.71 us -> 3.21 us  [swap(): lax.ppermute(value, axis, [(i, i ^ distance) for i in range(lax.axis_size...]
    pallas_call x4 -> x5, Pallas kernels: 4.8 us -> 4.97 us  [pick(): kernel_call(functools.partial(pick_kernel, rows, offset, skipped, stop),...]
  transfers between devices with their start and end apart: 10 -> 10, of which waited for: 4 -> 3; matrix products, arithmetic and copies ran while one was open for 6% -> 6% of each run, Pallas kernels for 15% -> 16%
where the time goes in v6:
time: 31.5 us; the launch traced here: 31.2 us
  Pallas kernels  14 us (44%)
  starting transfers between devices  10.3 us (33%)
  waiting for transfers between devices  3.21 us (10%)
  local copies, waits for them, and re-layouts  2.01 us (6%)
  between operations  0.85 us (3%)
  other arithmetic  0.81 us (3%)
    ppermute x10, starting transfers between devices, swap(): lax.ppermute(value, axis, [(i, i ^ distance) for i in range(lax.axis_size...  10.3 us
    pallas_call x1, Pallas kernels, together(): kernel_call(functools.partial(score_kernel, rows, keys), 'scores', (shape...  7 us
    pallas_call x5, Pallas kernels, pick(): kernel_call(functools.partial(pick_kernel, rows, offset, skipped, stop),...  4.97 us
    ppermute x10, waiting for transfers between devices, swap(): lax.ppermute(value, axis, [(i, i ^ distance) for i in range(lax.axis_size...  3.21 us
    pallas_call x1, Pallas kernels, together(): kernel_call(functools.partial(total_kernel, math.sqrt(w_first.size + w_se...  2.05 us
    unnamed x14, local copies, waits for them, and re-layouts  1.88 us
    add x1, other arithmetic, pack(): both = placed(features, 0, 0).astype(F32) + ids.astype(F32)  0.77 us
  transfers between devices with their start and end apart: 10, of which 3 were waited for; matrix products, arithmetic and copies ran while one was open for 6% of the time, Pallas kernels for 16%

profile of v6, /device:TPU:0, one launch (start us, length us, event | category | flops | bytes accessed | tf_op | source)
XLA Modules:
  0.0 31.2 jit_solution(14370785221594764925)
XLA Ops:
  0.6 0.8 %convert_add_fusion = f32[8,896]{1,0:T(8,128)S(1)} fusion(s32[2,128]{1,0:T(2,128)} %param.14, s32[2,128]{1,0:T(2,128)} %param.15, s32[2,128]{1,0:T(2,128)} %param.13, bf16[8,768]{1,0:T(8,128)(2,1)} %param.9), kind=kLoop, calls=%fused_computation.1 | loop fusion | flops 35840 | bytes 44032 | tf_op jit(solution)/shard_map/add | solution.py:250
  1.5 5.1 %collective-permute-start = (bf16[8,896]{1,0:T(8,128)(2,1)S(1)}, bf16[8,896]{1,0:T(8,128)(2,1)S(1)}, u32[]{:S(2)}, u32[]{:S(2)}) collective-permute-start(bf16[8,896]{1,0:T(8,128)(2,1)S(1)} %get-tuple-element.31), channel_id=1, source_target_pairs={{0,24},{2,26},{4,28},{6,30},{8,16},{10,18},{12,20},{14,22},{16,8},... | collective-permute-start | bytes 43016 | tf_op jit(solution)/shard_map/ppermute | solution.py:180
  6.6 0.0 collective-permute-start.1
  6.6 0.6 %collective-permute-start.2 = (bf16[8,896]{1,0:T(8,128)(2,1)S(1)}, bf16[8,896]{1,0:T(8,128)(2,1)S(1)}, u32[]{:S(2)}, u32[]{:S(2)}) collective-permute-start(bf16[8,896]{1,0:T(8,128)(2,1)S(1)} %get-tuple-element.31), channel_id=1, source_target_pairs={{0,8},{2,10},{4,12},{6,14},{8,0},{10,2},{12,4},{14,6},{16,24},{18,... | collective-permute-start | bytes 43016 | tf_op jit(solution)/shard_map/ppermute | solution.py:180
  7.2 1.8 %copy.15 = bf16[1387,512]{0,1:T(8,128)(2,1)S(1)} copy(bf16[1387,512]{1,0:T(8,128)(2,1)} %param.12) | data formatting | bytes 2840576 | tf_op args[3]
  9.0 0.1 pad.20.table
  9.1 0.0 collective-permute-done
  9.2 2.0 %collective-permute-done.1 = bf16[8,896]{1,0:T(8,128)(2,1)S(1)} collective-permute-done((bf16[8,896]{1,0:T(8,128)(2,1)S(1)}, bf16[8,896]{1,0:T(8,128)(2,1)S(1)}, u32[]{:S(2)}, u32[]{:S(2)}) %collective-permute-start.1) | collective-permute-done | bytes 14368 | tf_op jit(solution)/shard_map/ppermute | solution.py:180
  11.2 0.0 collective-permute-done.2
  11.2 2.5 %collective-permute-start.3 = (bf16[32,896]{1,0:T(8,128)(2,1)S(1)}, bf16[32,896]{1,0:T(8,128)(2,1)S(1)}, u32[]{:S(2)}, u32[]{:S(2)}) collective-permute-start(bf16[32,896]{1,0:T(8,128)(2,1)S(1)} %pad_maximum_fusion.block), channel_id=1, source_target_pairs={{0,6},{2,4},{4,2},{6,0},{8,14},{10,12},{12,10},{14,8},{16,22},{18,... | collective-permute-start | bytes 172040 | tf_op jit(solution)/shard_map/ppermute | solution.py:180
  13.7 0.5 %collective-permute-start.4 = (bf16[32,896]{1,0:T(8,128)(2,1)S(1)}, bf16[32,896]{1,0:T(8,128)(2,1)S(1)}, u32[]{:S(2)}, u32[]{:S(2)}) collective-permute-start(bf16[32,896]{1,0:T(8,128)(2,1)S(1)} %pad_maximum_fusion.block), channel_id=1, source_target_pairs={{0,4},{2,6},{4,0},{6,2},{8,12},{10,14},{12,8},{14,10},{16,20},{18,... | collective-permute-start | bytes 172040 | tf_op jit(solution)/shard_map/ppermute | solution.py:180
  14.2 0.5 %collective-permute-start.5 = (bf16[32,896]{1,0:T(8,128)(2,1)S(1)}, bf16[32,896]{1,0:T(8,128)(2,1)S(1)}, u32[]{:S(2)}, u32[]{:S(2)}) collective-permute-start(bf16[32,896]{1,0:T(8,128)(2,1)S(1)} %pad_maximum_fusion.block), channel_id=1, source_target_pairs={{0,2},{2,0},{4,6},{6,4},{8,10},{10,8},{12,14},{14,12},{16,18},{18,... | collective-permute-start | bytes 172040 | tf_op jit(solution)/shard_map/ppermute | solution.py:180
  14.8 0.0 collective-permute-start.6
  14.8 1.0 %pick.5.rest_0_ = bf16[16,512,128]{2,1,0:T(8,128)(2,1)S(1)} custom-call(bf16[32,896]{1,0:T(8,128)(2,1)S(1)} %pad_maximum_fusion.block, bf16[512,1408]{1,0:T(8,128)(2,1)S(1)} %pad.20.table), custom_call_target="tpu_custom_call" | custom-call | flops 738197504 | tf_op jit(solution)/shard_map/pick/pallas_call | solution.py:544
  15.8 0.1 collective-permute-done.6.block
  15.9 1.0 %pick.8.picked_early = bf16[4,512,128]{2,1,0:T(8,128)(2,1)S(1)} custom-call(bf16[32,128]{1,0:T(8,128)(2,1)S(1)} %collective-permute-done.6.block, bf16[512,1408]{1,0:T(8,128)(2,1)S(1)} %pad.20.table), custom_call_target="tpu_custom_call" | custom-call | flops 738197504 | tf_op jit(solution)/shard_map/pick/pallas_call | solution.py:544
  16.9 0.0 collective-permute-done.3.block
  17.0 1.0 %pick.6.rest_0_ = bf16[16,512,128]{2,1,0:T(8,128)(2,1)S(1)} custom-call(bf16[32,896]{1,0:T(8,128)(2,1)S(1)} %collective-permute-done.3.block, bf16[512,1408]{1,0:T(8,128)(2,1)S(1)} %pad.20.table, bf16[16,512,128]{2,1,0:T(8,128)(2,1)S(1)} %pick.5.rest_0_), custom_call_target="tpu_custom_call", output_to_operand_aliasing={{}: (2, {})} | custom-call | flops 738197504 | tf_op jit(solution)/shard_map/pick/pallas_call | solution.py:544
  18.0 0.0 collective-permute-done.4.block
  18.0 0.6 %pick.7.rest_0_ = bf16[16,512,128]{2,1,0:T(8,128)(2,1)S(1)} custom-call(bf16[32,896]{1,0:T(8,128)(2,1)S(1)} %collective-permute-done.4.block, bf16[512,1408]{1,0:T(8,128)(2,1)S(1)} %pad.20.table, bf16[16,512,128]{2,1,0:T(8,128)(2,1)S(1)} %pick.6.rest_0_), custom_call_target="tpu_custom_call", output_to_operand_aliasing={{}: (2, {})} | custom-call | flops 369098752 | tf_op jit(solution)/shard_map/pick/pallas_call | solution.py:544
  18.6 0.0 collective-permute-done.5
  18.6 0.0 copy-start
  18.6 0.0 copy-start.1
  18.6 0.0 copy-start.2
  18.7 0.0 copy-start.3
  18.7 0.4 %collective-permute-start.7 = (bf16[128,896]{1,0:T(8,128)(2,1)S(1)}, bf16[128,896]{1,0:T(8,128)(2,1)S(1)}, u32[]{:S(2)}, u32[]{:S(2)}) collective-permute-start(bf16[128,896]{1,0:T(8,128)(2,1)S(1)} %constant_dynamic-update-slice_fusion.block.mine), channel_id=1, source_target_pairs={{0,1},{1,0},{2,3},{3,2},{4,5},{5,4},{6,7},{7,6},{8,9},{9,8},{10,11... | collective-permute-start | bytes 688136 | tf_op jit(solution)/shard_map/ppermute | solution.py:180
  19.1 1.4 %pick.9.picked_mine = bf16[16,512,128]{2,1,0:T(8,128)(2,1)S(1)} custom-call(bf16[128,896]{1,0:T(8,128)(2,1)S(1)} %constant_dynamic-update-slice_fusion.block.mine, bf16[512,1408]{1,0:T(8,128)(2,1)S(1)} %pad.20.table, bf16[16,512,128]{2,1,0:T(8,128)(2,1)S(1)} %pick.7.rest_0_), custom_call_target="tpu_custom_call", output_to_operand_aliasing={{}: (2, {})} | custom-call | flops 1107296256 | tf_op jit(solution)/shard_map/pick/pallas_call | solution.py:544
  20.5 0.0 collective-permute-done.7.other
  20.5 0.0 copy-done
  20.5 0.0 copy-done.1
  20.6 0.0 copy-done.2
  20.6 0.0 copy-done.3
  20.6 7.0 %scores.1 = (bf16[256,512]{1,0:T(8,128)(2,1)S(1)}, f32[1,256]{1,0:T(1,128)S(1)}, f32[256,512]{1,0:T(8,128)S(1)}, bf16[256,512]{1,0:T(8,128)(2,1)S(1)}) custom-call(s32[2,16]{1,0:T(2,128)S(1)} %copy-done.3, bf16[128,896]{1,0:T(8,128)(2,1)S(1)} %constant_dynamic-update-slice_fusion.block.mine, bf16[128,896]{1,0:T(8,128)(2,1)S(1)} %collective-permute-done.7.other, ...), custom_call_target="tpu_custom_call" | custom-call | flops 5905580032 | tf_op jit(solution)/shard_map/scores/pallas_call | solution.py:567
  27.6 0.2 collective-permute-start.8
  27.8 0.4 %collective-permute-start.9 = (f32[1,256]{1,0:T(1,128)S(1)}, f32[1,256]{1,0:T(1,128)S(1)}, u32[]{:S(2)}, u32[]{:S(2)}) collective-permute-start(f32[1,256]{1,0:T(1,128)S(1)} %get-tuple-element.28.loss_mine), channel_id=1, source_target_pairs={{0,1},{1,0},{2,3},{3,2},{4,5},{5,4},{6,7},{7,6},{8,9},{9,8},{10,11... | collective-permute-start | bytes 3080 | tf_op jit(solution)/shard_map/ppermute | solution.py:180
  28.2 1.0 %collective-permute-done.9.loss_other = f32[1,256]{1,0:T(1,128)S(1)} collective-permute-done((f32[1,256]{1,0:T(1,128)S(1)}, f32[1,256]{1,0:T(1,128)S(1)}, u32[]{:S(2)}, u32[]{:S(2)}) %collective-permute-start.9) | collective-permute-done | bytes 1056 | tf_op jit(solution)/shard_map/ppermute | solution.py:180
  29.2 0.0 collective-permute-done.8.grad_other
  29.2 2.0 %totals.1 = (f32[2,128]{1,0:T(2,128)}, f32[384,512]{1,0:T(8,128)}, f32[256,512]{1,0:T(8,128)}) custom-call(bf16[128,896]{1,0:T(8,128)(2,1)S(1)} %constant_dynamic-update-slice_fusion.block.mine, bf16[128,896]{1,0:T(8,128)(2,1)S(1)} %collective-permute-done.7.other, bf16[256,512]{1,0:T(8,128)(2,1)S(1)} %get-tuple-element.25.grad_mine, ...), custom_call_target="tpu_custom_call" | custom-call | tf_op jit(solution)/shard_map/totals/pallas_call | solution.py:591
  (13 shorter events, 0.1 us)
Async XLA Ops:
  1.5 7.7 %collective-permute-start = (bf16[8,896]{1,0:T(8,128)(2,1)S(1)}, bf16[8,896]{1,0:T(8,128)(2,1)S(1)}, u32[]{:S(2)}, u32[]{:S(2)}) collective-permute-start(bf16[8,896]{1,0:T(8,128)(2,1)S(1)} %get-tuple-element.31), channel_id=1, source_target_pairs={{0,24},{2,26},{4,28},{6,30},{8,16},{10,18},{12,20},{14,22},{16,8},... | collective-permute-start | bytes 43016 | tf_op jit(solution)/shard_map/ppermute | solution.py:180
  6.6 4.6 %collective-permute-start.1 = (bf16[8,896]{1,0:T(8,128)(2,1)S(1)}, bf16[8,896]{1,0:T(8,128)(2,1)S(1)}, u32[]{:S(2)}, u32[]{:S(2)}) collective-permute-start(bf16[8,896]{1,0:T(8,128)(2,1)S(1)} %get-tuple-element.31), channel_id=1, source_target_pairs={{0,16},{2,18},{4,20},{6,22},{8,24},{10,26},{12,28},{14,30},{16,0},... | collective-permute-start | bytes 43016 | tf_op jit(solution)/shard_map/ppermute | solution.py:180
  6.6 4.6 %collective-permute-start.2 = (bf16[8,896]{1,0:T(8,128)(2,1)S(1)}, bf16[8,896]{1,0:T(8,128)(2,1)S(1)}, u32[]{:S(2)}, u32[]{:S(2)}) collective-permute-start(bf16[8,896]{1,0:T(8,128)(2,1)S(1)} %get-tuple-element.31), channel_id=1, source_target_pairs={{0,8},{2,10},{4,12},{6,14},{8,0},{10,2},{12,4},{14,6},{16,24},{18,... | collective-permute-start | bytes 43016 | tf_op jit(solution)/shard_map/ppermute | solution.py:180
  11.2 5.7 %collective-permute-start.3 = (bf16[32,896]{1,0:T(8,128)(2,1)S(1)}, bf16[32,896]{1,0:T(8,128)(2,1)S(1)}, u32[]{:S(2)}, u32[]{:S(2)}) collective-permute-start(bf16[32,896]{1,0:T(8,128)(2,1)S(1)} %pad_maximum_fusion.block), channel_id=1, source_target_pairs={{0,6},{2,4},{4,2},{6,0},{8,14},{10,12},{12,10},{14,8},{16,22},{18,... | collective-permute-start | bytes 172040 | tf_op jit(solution)/shard_map/ppermute | solution.py:180
  13.7 4.2 %collective-permute-start.4 = (bf16[32,896]{1,0:T(8,128)(2,1)S(1)}, bf16[32,896]{1,0:T(8,128)(2,1)S(1)}, u32[]{:S(2)}, u32[]{:S(2)}) collective-permute-start(bf16[32,896]{1,0:T(8,128)(2,1)S(1)} %pad_maximum_fusion.block), channel_id=1, source_target_pairs={{0,4},{2,6},{4,0},{6,2},{8,12},{10,14},{12,8},{14,10},{16,20},{18,... | collective-permute-start | bytes 172040 | tf_op jit(solution)/shard_map/ppermute | solution.py:180
  14.2 4.3 %collective-permute-start.5 = (bf16[32,896]{1,0:T(8,128)(2,1)S(1)}, bf16[32,896]{1,0:T(8,128)(2,1)S(1)}, u32[]{:S(2)}, u32[]{:S(2)}) collective-permute-start(bf16[32,896]{1,0:T(8,128)(2,1)S(1)} %pad_maximum_fusion.block), channel_id=1, source_target_pairs={{0,2},{2,0},{4,6},{6,4},{8,10},{10,8},{12,14},{14,12},{16,18},{18,... | collective-permute-start | bytes 172040 | tf_op jit(solution)/shard_map/ppermute | solution.py:180
  14.8 1.2 %collective-permute-start.6 = (bf16[32,128]{1,0:T(8,128)(2,1)S(1)}, bf16[32,128]{1,0:T(8,128)(2,1)S(1)}, u32[]{:S(2)}, u32[]{:S(2)}) collective-permute-start(bf16[32,128]{1,0:T(8,128)(2,1)S(1)} %slice.25), channel_id=1, source_target_pairs={{0,1},{1,0},{2,3},{3,2},{4,5},{5,4},{6,7},{7,6},{8,9},{9,8},{10,11... | collective-permute-start | bytes 24584 | tf_op jit(solution)/shard_map/ppermute | solution.py:180
  18.6 1.9 %copy-start = (bf16[512,512]{1,0:T(8,128)(2,1)S(1)}, bf16[512,512]{1,0:T(8,128)(2,1)}, u32[]{:S(2)}) copy-start(bf16[512,512]{1,0:T(8,128)(2,1)} %w_second.3) | copy-start | bytes 1572868
  18.6 1.9 %copy-start.1 = (bf16[768,512]{1,0:T(8,128)(2,1)S(1)}, bf16[768,512]{1,0:T(8,128)(2,1)}, u32[]{:S(2)}) copy-start(bf16[768,512]{1,0:T(8,128)(2,1)} %w_first.1) | copy-start | bytes 2359300
  18.6 1.9 %copy-start.2 = (s32[2,512]{1,0:T(2,128)S(1)}, s32[2,512]{1,0:T(2,128)}, u32[]{:S(2)}) copy-start(s32[2,512]{1,0:T(2,128)} %negatives.1) | copy-start | bytes 12292
  18.7 1.9 %copy-start.3 = (s32[2,16]{1,0:T(2,128)S(1)}, s32[2,16]{1,0:T(2,128)}, u32[]{:S(2)}) copy-start(s32[2,16]{1,0:T(2,128)} %partner.1) | copy-start | bytes 388
  18.7 1.9 %collective-permute-start.7 = (bf16[128,896]{1,0:T(8,128)(2,1)S(1)}, bf16[128,896]{1,0:T(8,128)(2,1)S(1)}, u32[]{:S(2)}, u32[]{:S(2)}) collective-permute-start(bf16[128,896]{1,0:T(8,128)(2,1)S(1)} %constant_dynamic-update-slice_fusion.block.mine), channel_id=1, source_target_pairs={{0,1},{1,0},{2,3},{3,2},{4,5},{5,4},{6,7},{7,6},{8,9},{9,8},{10,11... | collective-permute-start | bytes 688136 | tf_op jit(solution)/shard_map/ppermute | solution.py:180
  27.6 1.6 %collective-permute-start.8 = (bf16[256,512]{1,0:T(8,128)(2,1)S(1)}, bf16[256,512]{1,0:T(8,128)(2,1)S(1)}, u32[]{:S(2)}, u32[]{:S(2)}) collective-permute-start(bf16[256,512]{1,0:T(8,128)(2,1)S(1)} %get-tuple-element.25.grad_mine), channel_id=1, source_target_pairs={{0,1},{1,0},{2,3},{3,2},{4,5},{5,4},{6,7},{7,6},{8,9},{9,8},{10,11... | collective-permute-start | bytes 786440 | tf_op jit(solution)/shard_map/ppermute | solution.py:180
  27.8 1.4 %collective-permute-start.9 = (f32[1,256]{1,0:T(1,128)S(1)}, f32[1,256]{1,0:T(1,128)S(1)}, u32[]{:S(2)}, u32[]{:S(2)}) collective-permute-start(f32[1,256]{1,0:T(1,128)S(1)} %get-tuple-element.28.loss_mine), channel_id=1, source_target_pairs={{0,1},{1,0},{2,3},{3,2},{4,5},{5,4},{6,7},{7,6},{8,9},{9,8},{10,11... | collective-permute-start | bytes 3080 | tf_op jit(solution)/shard_map/ppermute | solution.py:180

commit v7 on v6

--- a/solution.py
+++ b/solution.py
@@ -181,11 +181,14 @@
 
 
 def distances_of(size):
+    bits = [1 << i for i in reversed(range(size.bit_length() - 1))]
     steps = []
-    while size > 1:
-        radix = min(size, 4)
-        size //= radix
-        steps.append([i * size for i in range(radix - 1, 0, -1)])
+    while bits:
+        step = [bits.pop(0)]
+        if bits:
+            step.append(bits.pop(len(bits) // 2))
+            step.insert(0, sum(step))
+        steps.append(step)
     return steps
 
 

time: 31.5 us -> 31.4 us (level)
  no operation moved by 1% of the time
where the time goes in v7:
time: 31.4 us; the launch traced here: 31.2 us
  Pallas kernels  14 us (45%)
  starting transfers between devices  10.3 us (33%)
  waiting for transfers between devices  3.21 us (10%)
  local copies, waits for them, and re-layouts  2.01 us (6%)
  between operations  0.85 us (3%)
  other arithmetic  0.81 us (3%)
    ppermute x10, starting transfers between devices, swap(): lax.ppermute(value, axis, [(i, i ^ distance) for i in range(lax.axis_size...  10.3 us
    pallas_call x1, Pallas kernels, together(): kernel_call(functools.partial(score_kernel, rows, keys), 'scores', (shape...  7.03 us
    pallas_call x5, Pallas kernels, pick(): kernel_call(functools.partial(pick_kernel, rows, offset, skipped, stop),...  4.97 us
    ppermute x10, waiting for transfers between devices, swap(): lax.ppermute(value, axis, [(i, i ^ distance) for i in range(lax.axis_size...  3.21 us
    pallas_call x1, Pallas kernels, together(): kernel_call(functools.partial(total_kernel, math.sqrt(w_first.size + w_se...  2.04 us
    unnamed x14, local copies, waits for them, and re-layouts  1.88 us
    add x1, other arithmetic, pack(): both = placed(features, 0, 0).astype(F32) + ids.astype(F32)  0.77 us
  transfers between devices with their start and end apart: 10, of which 3 were waited for; matrix products, arithmetic and copies ran while one was open for 6% of the time, Pallas kernels for 16%

profile of v7, /device:TPU:0, one launch (start us, length us, event | category | flops | bytes accessed | tf_op | source)
XLA Modules:
  0.0 31.2 jit_solution(14577914241833879395)
XLA Ops:
  0.6 0.8 %convert_add_fusion = f32[8,896]{1,0:T(8,128)S(1)} fusion(s32[2,128]{1,0:T(2,128)} %param.14, s32[2,128]{1,0:T(2,128)} %param.15, s32[2,128]{1,0:T(2,128)} %param.13, bf16[8,768]{1,0:T(8,128)(2,1)} %param.9), kind=kLoop, calls=%fused_computation.1 | loop fusion | flops 35840 | bytes 44032 | tf_op jit(solution)/shard_map/add | solution.py:253
  1.5 5.1 %collective-permute-start = (bf16[8,896]{1,0:T(8,128)(2,1)S(1)}, bf16[8,896]{1,0:T(8,128)(2,1)S(1)}, u32[]{:S(2)}, u32[]{:S(2)}) collective-permute-start(bf16[8,896]{1,0:T(8,128)(2,1)S(1)} %get-tuple-element.31), channel_id=1, source_target_pairs={{0,20},{2,22},{4,16},{6,18},{8,28},{10,30},{12,24},{14,26},{16,4},... | collective-permute-start | bytes 43016 | tf_op jit(solution)/shard_map/ppermute | solution.py:180
  6.5 0.3 %collective-permute-start.1 = (bf16[8,896]{1,0:T(8,128)(2,1)S(1)}, bf16[8,896]{1,0:T(8,128)(2,1)S(1)}, u32[]{:S(2)}, u32[]{:S(2)}) collective-permute-start(bf16[8,896]{1,0:T(8,128)(2,1)S(1)} %get-tuple-element.31), channel_id=1, source_target_pairs={{0,16},{2,18},{4,20},{6,22},{8,24},{10,26},{12,28},{14,30},{16,0},... | collective-permute-start | bytes 43016 | tf_op jit(solution)/shard_map/ppermute | solution.py:180
  6.9 0.3 collective-permute-start.2
  7.2 1.8 %copy.15 = bf16[1387,512]{0,1:T(8,128)(2,1)S(1)} copy(bf16[1387,512]{1,0:T(8,128)(2,1)} %param.12) | data formatting | bytes 2840576 | tf_op args[3]
  9.0 0.1 pad.20.table
  9.1 0.0 collective-permute-done
  9.1 2.0 %collective-permute-done.1 = bf16[8,896]{1,0:T(8,128)(2,1)S(1)} collective-permute-done((bf16[8,896]{1,0:T(8,128)(2,1)S(1)}, bf16[8,896]{1,0:T(8,128)(2,1)S(1)}, u32[]{:S(2)}, u32[]{:S(2)}) %collective-permute-start.1) | collective-permute-done | bytes 14368 | tf_op jit(solution)/shard_map/ppermute | solution.py:180
  11.1 0.0 collective-permute-done.2
  11.2 2.6 %collective-permute-start.3 = (bf16[32,896]{1,0:T(8,128)(2,1)S(1)}, bf16[32,896]{1,0:T(8,128)(2,1)S(1)}, u32[]{:S(2)}, u32[]{:S(2)}) collective-permute-start(bf16[32,896]{1,0:T(8,128)(2,1)S(1)} %pad_maximum_fusion.block), channel_id=1, source_target_pairs={{0,10},{2,8},{4,14},{6,12},{8,2},{10,0},{12,6},{14,4},{16,26},{18,... | collective-permute-start | bytes 172040 | tf_op jit(solution)/shard_map/ppermute | solution.py:180
  13.7 0.4 %collective-permute-start.4 = (bf16[32,896]{1,0:T(8,128)(2,1)S(1)}, bf16[32,896]{1,0:T(8,128)(2,1)S(1)}, u32[]{:S(2)}, u32[]{:S(2)}) collective-permute-start(bf16[32,896]{1,0:T(8,128)(2,1)S(1)} %pad_maximum_fusion.block), channel_id=1, source_target_pairs={{0,8},{2,10},{4,12},{6,14},{8,0},{10,2},{12,4},{14,6},{16,24},{18,... | collective-permute-start | bytes 172040 | tf_op jit(solution)/shard_map/ppermute | solution.py:180
  14.2 0.5 %collective-permute-start.5 = (bf16[32,896]{1,0:T(8,128)(2,1)S(1)}, bf16[32,896]{1,0:T(8,128)(2,1)S(1)}, u32[]{:S(2)}, u32[]{:S(2)}) collective-permute-start(bf16[32,896]{1,0:T(8,128)(2,1)S(1)} %pad_maximum_fusion.block), channel_id=1, source_target_pairs={{0,2},{2,0},{4,6},{6,4},{8,10},{10,8},{12,14},{14,12},{16,18},{18,... | collective-permute-start | bytes 172040 | tf_op jit(solution)/shard_map/ppermute | solution.py:180
  14.7 0.0 collective-permute-start.6
  14.7 1.0 %pick.5.rest_0_ = bf16[16,512,128]{2,1,0:T(8,128)(2,1)S(1)} custom-call(bf16[32,896]{1,0:T(8,128)(2,1)S(1)} %pad_maximum_fusion.block, bf16[512,1408]{1,0:T(8,128)(2,1)S(1)} %pad.20.table), custom_call_target="tpu_custom_call" | custom-call | flops 738197504 | tf_op jit(solution)/shard_map/pick/pallas_call | solution.py:547
  15.7 0.1 collective-permute-done.6.block
  15.9 1.0 %pick.8.picked_early = bf16[4,512,128]{2,1,0:T(8,128)(2,1)S(1)} custom-call(bf16[32,128]{1,0:T(8,128)(2,1)S(1)} %collective-permute-done.6.block, bf16[512,1408]{1,0:T(8,128)(2,1)S(1)} %pad.20.table), custom_call_target="tpu_custom_call" | custom-call | flops 738197504 | tf_op jit(solution)/shard_map/pick/pallas_call | solution.py:547
  16.9 0.0 collective-permute-done.3.block
  16.9 1.0 %pick.6.rest_0_ = bf16[16,512,128]{2,1,0:T(8,128)(2,1)S(1)} custom-call(bf16[32,896]{1,0:T(8,128)(2,1)S(1)} %collective-permute-done.3.block, bf16[512,1408]{1,0:T(8,128)(2,1)S(1)} %pad.20.table, bf16[16,512,128]{2,1,0:T(8,128)(2,1)S(1)} %pick.5.rest_0_), custom_call_target="tpu_custom_call", output_to_operand_aliasing={{}: (2, {})} | custom-call | flops 738197504 | tf_op jit(solution)/shard_map/pick/pallas_call | solution.py:547
  17.9 0.0 collective-permute-done.4.block
  17.9 0.6 %pick.7.rest_0_ = bf16[16,512,128]{2,1,0:T(8,128)(2,1)S(1)} custom-call(bf16[32,896]{1,0:T(8,128)(2,1)S(1)} %collective-permute-done.4.block, bf16[512,1408]{1,0:T(8,128)(2,1)S(1)} %pad.20.table, bf16[16,512,128]{2,1,0:T(8,128)(2,1)S(1)} %pick.6.rest_0_), custom_call_target="tpu_custom_call", output_to_operand_aliasing={{}: (2, {})} | custom-call | flops 369098752 | tf_op jit(solution)/shard_map/pick/pallas_call | solution.py:547
  18.5 0.0 collective-permute-done.5
  18.6 0.0 copy-start
  18.6 0.0 copy-start.1
  18.6 0.0 copy-start.2
  18.6 0.0 copy-start.3
  18.6 0.4 %collective-permute-start.7 = (bf16[128,896]{1,0:T(8,128)(2,1)S(1)}, bf16[128,896]{1,0:T(8,128)(2,1)S(1)}, u32[]{:S(2)}, u32[]{:S(2)}) collective-permute-start(bf16[128,896]{1,0:T(8,128)(2,1)S(1)} %constant_dynamic-update-slice_fusion.block.mine), channel_id=1, source_target_pairs={{0,1},{1,0},{2,3},{3,2},{4,5},{5,4},{6,7},{7,6},{8,9},{9,8},{10,11... | collective-permute-start | bytes 688136 | tf_op jit(solution)/shard_map/ppermute | solution.py:180
  19.1 1.4 %pick.9.picked_mine = bf16[16,512,128]{2,1,0:T(8,128)(2,1)S(1)} custom-call(bf16[128,896]{1,0:T(8,128)(2,1)S(1)} %constant_dynamic-update-slice_fusion.block.mine, bf16[512,1408]{1,0:T(8,128)(2,1)S(1)} %pad.20.table, bf16[16,512,128]{2,1,0:T(8,128)(2,1)S(1)} %pick.7.rest_0_), custom_call_target="tpu_custom_call", output_to_operand_aliasing={{}: (2, {})} | custom-call | flops 1107296256 | tf_op jit(solution)/shard_map/pick/pallas_call | solution.py:547
  20.5 0.0 collective-permute-done.7.other
  20.5 0.0 copy-done
  20.5 0.0 copy-done.1
  20.5 0.0 copy-done.2
  20.5 0.0 copy-done.3
  20.5 7.0 %scores.1 = (bf16[256,512]{1,0:T(8,128)(2,1)S(1)}, f32[1,256]{1,0:T(1,128)S(1)}, f32[256,512]{1,0:T(8,128)S(1)}, bf16[256,512]{1,0:T(8,128)(2,1)S(1)}) custom-call(s32[2,16]{1,0:T(2,128)S(1)} %copy-done.3, bf16[128,896]{1,0:T(8,128)(2,1)S(1)} %constant_dynamic-update-slice_fusion.block.mine, bf16[128,896]{1,0:T(8,128)(2,1)S(1)} %collective-permute-done.7.other, ...), custom_call_target="tpu_custom_call" | custom-call | flops 5905580032 | tf_op jit(solution)/shard_map/scores/pallas_call | solution.py:570
  27.6 0.2 collective-permute-start.8
  27.7 0.4 %collective-permute-start.9 = (f32[1,256]{1,0:T(1,128)S(1)}, f32[1,256]{1,0:T(1,128)S(1)}, u32[]{:S(2)}, u32[]{:S(2)}) collective-permute-start(f32[1,256]{1,0:T(1,128)S(1)} %get-tuple-element.28.loss_mine), channel_id=1, source_target_pairs={{0,1},{1,0},{2,3},{3,2},{4,5},{5,4},{6,7},{7,6},{8,9},{9,8},{10,11... | collective-permute-start | bytes 3080 | tf_op jit(solution)/shard_map/ppermute | solution.py:180
  28.1 1.0 %collective-permute-done.9.loss_other = f32[1,256]{1,0:T(1,128)S(1)} collective-permute-done((f32[1,256]{1,0:T(1,128)S(1)}, f32[1,256]{1,0:T(1,128)S(1)}, u32[]{:S(2)}, u32[]{:S(2)}) %collective-permute-start.9) | collective-permute-done | bytes 1056 | tf_op jit(solution)/shard_map/ppermute | solution.py:180
  29.2 0.0 collective-permute-done.8.grad_other
  29.2 2.0 %totals.1 = (f32[2,128]{1,0:T(2,128)}, f32[384,512]{1,0:T(8,128)}, f32[256,512]{1,0:T(8,128)}) custom-call(bf16[128,896]{1,0:T(8,128)(2,1)S(1)} %constant_dynamic-update-slice_fusion.block.mine, bf16[128,896]{1,0:T(8,128)(2,1)S(1)} %collective-permute-done.7.other, bf16[256,512]{1,0:T(8,128)(2,1)S(1)} %get-tuple-element.25.grad_mine, ...), custom_call_target="tpu_custom_call" | custom-call | tf_op jit(solution)/shard_map/totals/pallas_call | solution.py:594
  (13 shorter events, 0.1 us)
Async XLA Ops:
  1.5 7.6 %collective-permute-start = (bf16[8,896]{1,0:T(8,128)(2,1)S(1)}, bf16[8,896]{1,0:T(8,128)(2,1)S(1)}, u32[]{:S(2)}, u32[]{:S(2)}) collective-permute-start(bf16[8,896]{1,0:T(8,128)(2,1)S(1)} %get-tuple-element.31), channel_id=1, source_target_pairs={{0,20},{2,22},{4,16},{6,18},{8,28},{10,30},{12,24},{14,26},{16,4},... | collective-permute-start | bytes 43016 | tf_op jit(solution)/shard_map/ppermute | solution.py:180
  6.5 4.6 %collective-permute-start.1 = (bf16[8,896]{1,0:T(8,128)(2,1)S(1)}, bf16[8,896]{1,0:T(8,128)(2,1)S(1)}, u32[]{:S(2)}, u32[]{:S(2)}) collective-permute-start(bf16[8,896]{1,0:T(8,128)(2,1)S(1)} %get-tuple-element.31), channel_id=1, source_target_pairs={{0,16},{2,18},{4,20},{6,22},{8,24},{10,26},{12,28},{14,30},{16,0},... | collective-permute-start | bytes 43016 | tf_op jit(solution)/shard_map/ppermute | solution.py:180
  6.9 4.3 %collective-permute-start.2 = (bf16[8,896]{1,0:T(8,128)(2,1)S(1)}, bf16[8,896]{1,0:T(8,128)(2,1)S(1)}, u32[]{:S(2)}, u32[]{:S(2)}) collective-permute-start(bf16[8,896]{1,0:T(8,128)(2,1)S(1)} %get-tuple-element.31), channel_id=1, source_target_pairs={{0,4},{2,6},{4,0},{6,2},{8,12},{10,14},{12,8},{14,10},{16,20},{18,... | collective-permute-start | bytes 43016 | tf_op jit(solution)/shard_map/ppermute | solution.py:180
  11.2 5.7 %collective-permute-start.3 = (bf16[32,896]{1,0:T(8,128)(2,1)S(1)}, bf16[32,896]{1,0:T(8,128)(2,1)S(1)}, u32[]{:S(2)}, u32[]{:S(2)}) collective-permute-start(bf16[32,896]{1,0:T(8,128)(2,1)S(1)} %pad_maximum_fusion.block), channel_id=1, source_target_pairs={{0,10},{2,8},{4,14},{6,12},{8,2},{10,0},{12,6},{14,4},{16,26},{18,... | collective-permute-start | bytes 172040 | tf_op jit(solution)/shard_map/ppermute | solution.py:180
  13.7 4.2 %collective-permute-start.4 = (bf16[32,896]{1,0:T(8,128)(2,1)S(1)}, bf16[32,896]{1,0:T(8,128)(2,1)S(1)}, u32[]{:S(2)}, u32[]{:S(2)}) collective-permute-start(bf16[32,896]{1,0:T(8,128)(2,1)S(1)} %pad_maximum_fusion.block), channel_id=1, source_target_pairs={{0,8},{2,10},{4,12},{6,14},{8,0},{10,2},{12,4},{14,6},{16,24},{18,... | collective-permute-start | bytes 172040 | tf_op jit(solution)/shard_map/ppermute | solution.py:180
  14.2 4.3 %collective-permute-start.5 = (bf16[32,896]{1,0:T(8,128)(2,1)S(1)}, bf16[32,896]{1,0:T(8,128)(2,1)S(1)}, u32[]{:S(2)}, u32[]{:S(2)}) collective-permute-start(bf16[32,896]{1,0:T(8,128)(2,1)S(1)} %pad_maximum_fusion.block), channel_id=1, source_target_pairs={{0,2},{2,0},{4,6},{6,4},{8,10},{10,8},{12,14},{14,12},{16,18},{18,... | collective-permute-start | bytes 172040 | tf_op jit(solution)/shard_map/ppermute | solution.py:180
  14.7 1.2 %collective-permute-start.6 = (bf16[32,128]{1,0:T(8,128)(2,1)S(1)}, bf16[32,128]{1,0:T(8,128)(2,1)S(1)}, u32[]{:S(2)}, u32[]{:S(2)}) collective-permute-start(bf16[32,128]{1,0:T(8,128)(2,1)S(1)} %slice.25), channel_id=1, source_target_pairs={{0,1},{1,0},{2,3},{3,2},{4,5},{5,4},{6,7},{7,6},{8,9},{9,8},{10,11... | collective-permute-start | bytes 24584 | tf_op jit(solution)/shard_map/ppermute | solution.py:180
  18.6 1.9 %copy-start = (bf16[512,512]{1,0:T(8,128)(2,1)S(1)}, bf16[512,512]{1,0:T(8,128)(2,1)}, u32[]{:S(2)}) copy-start(bf16[512,512]{1,0:T(8,128)(2,1)} %w_second.3) | copy-start | bytes 1572868
  18.6 1.9 %copy-start.1 = (bf16[768,512]{1,0:T(8,128)(2,1)S(1)}, bf16[768,512]{1,0:T(8,128)(2,1)}, u32[]{:S(2)}) copy-start(bf16[768,512]{1,0:T(8,128)(2,1)} %w_first.1) | copy-start | bytes 2359300
  18.6 1.9 %copy-start.2 = (s32[2,512]{1,0:T(2,128)S(1)}, s32[2,512]{1,0:T(2,128)}, u32[]{:S(2)}) copy-start(s32[2,512]{1,0:T(2,128)} %negatives.1) | copy-start | bytes 12292
  18.6 1.9 %copy-start.3 = (s32[2,16]{1,0:T(2,128)S(1)}, s32[2,16]{1,0:T(2,128)}, u32[]{:S(2)}) copy-start(s32[2,16]{1,0:T(2,128)} %partner.1) | copy-start | bytes 388
  18.6 1.9 %collective-permute-start.7 = (bf16[128,896]{1,0:T(8,128)(2,1)S(1)}, bf16[128,896]{1,0:T(8,128)(2,1)S(1)}, u32[]{:S(2)}, u32[]{:S(2)}) collective-permute-start(bf16[128,896]{1,0:T(8,128)(2,1)S(1)} %constant_dynamic-update-slice_fusion.block.mine), channel_id=1, source_target_pairs={{0,1},{1,0},{2,3},{3,2},{4,5},{5,4},{6,7},{7,6},{8,9},{9,8},{10,11... | collective-permute-start | bytes 688136 | tf_op jit(solution)/shard_map/ppermute | solution.py:180
  27.6 1.6 %collective-permute-start.8 = (bf16[256,512]{1,0:T(8,128)(2,1)S(1)}, bf16[256,512]{1,0:T(8,128)(2,1)S(1)}, u32[]{:S(2)}, u32[]{:S(2)}) collective-permute-start(bf16[256,512]{1,0:T(8,128)(2,1)S(1)} %get-tuple-element.25.grad_mine), channel_id=1, source_target_pairs={{0,1},{1,0},{2,3},{3,2},{4,5},{5,4},{6,7},{7,6},{8,9},{9,8},{10,11... | collective-permute-start | bytes 786440 | tf_op jit(solution)/shard_map/ppermute | solution.py:180
  27.7 1.4 %collective-permute-start.9 = (f32[1,256]{1,0:T(1,128)S(1)}, f32[1,256]{1,0:T(1,128)S(1)}, u32[]{:S(2)}, u32[]{:S(2)}) collective-permute-start(f32[1,256]{1,0:T(1,128)S(1)} %get-tuple-element.28.loss_mine), channel_id=1, source_target_pairs={{0,1},{1,0},{2,3},{3,2},{4,5},{5,4},{6,7},{7,6},{8,9},{9,8},{10,11... | collective-permute-start | bytes 3080 | tf_op jit(solution)/shard_map/ppermute | solution.py:180
